TPU v7x, 32 devices: a whole 2x2x4 slice. The times are simulated.
32 devices in a mesh: wide: 8 (over z, core), narrow: 4 (over y, x).
Axes of the slice: x: 2, y: 2, z: 4, core: 2. Of those that a mesh axis runs over, the one named last changes fastest.
Arguments:
- normals: bfloat16 [3, 256, 1024, 512], P(None, 'wide', 'narrow'), may hold values from -6 to 6
- counts: int32 [256, 1024, 512], P('wide', 'narrow'), may hold values from 0 to 63
Outputs:
- spectrum: bfloat16 [512, 256, 1024], P(('wide', 'narrow'))
Inputs may be any that keep to these rules, and one draw needn't show every extreme that they name: counts are splat sample counts of a cell.
All inputs are finite; a program needn't handle non-finite values.
Results may differ from a plain program's by a relative error of at most 0.0068.
Values may be sent and summed in bfloat16 or wider, within the bound.
No kernel may reach another device: no remote copies, remote signals or barrier semaphores. Data moves between devices by JAX's collectives and lax.ppermute only.
A program may use at most 192 MiB of HBM per device.

v0:
```python
import jax
import jax.numpy as jnp
from jax import lax
from jax.sharding import PartitionSpec as P


def with_halo(cells, sides, width):
    for axis, dim in sides:
        count = lax.axis_size(axis)
        ends = count - 1
        head = lax.slice_in_dim(cells, 0, width, axis=dim)
        tail = lax.slice_in_dim(cells, cells.shape[dim] - width, cells.shape[dim], axis=dim)
        cells = jnp.concatenate(
            [
                lax.ppermute(tail, axis, [(i, (i + 1) % count) for i in range(ends)]),
                cells,
                lax.ppermute(head, axis, [((i + 1) % count, i) for i in range(ends)]),
            ],
            axis=dim,
        )
    return cells


def cosine_table(size):
    freq = jnp.arange(size, dtype=jnp.float32)[:, None]
    place = jnp.arange(size, dtype=jnp.float32)[None, :]
    waves = jnp.cos(jnp.pi * (2.0 * place + 1.0) * freq / (2.0 * size))
    scales = jnp.where(freq == 0.0, jnp.sqrt(1.0 / size), jnp.sqrt(2.0 / size))
    return (scales * waves).astype(jnp.bfloat16)


def per_device(normals, counts):
    values = counts.astype(jnp.float32)
    weight = values / (values + 4.0)
    flux_x = weight * normals[0].astype(jnp.float32)
    flux_y = weight * normals[1].astype(jnp.float32)
    flux_z = weight * normals[2].astype(jnp.float32)
    padded_x = with_halo(flux_x, (("wide", 0),), 1)
    padded_y = with_halo(flux_y, (("narrow", 1),), 1)
    padded_z = jnp.pad(flux_z, ((0, 0), (0, 0), (1, 1)))
    diff_x = padded_x[2:] - padded_x[:-2]
    diff_y = padded_y[:, 2:] - padded_y[:, :-2]
    diff_z = padded_z[:, :, 2:] - padded_z[:, :, :-2]
    divergence = (0.5 * (diff_x + diff_y + diff_z)).astype(jnp.bfloat16)
    depth = divergence.shape[2]
    table_z = cosine_table(depth)
    along_z = jnp.einsum(
        "kn,xyn->kxy", table_z, divergence, preferred_element_type=jnp.float32
    ).astype(jnp.bfloat16)
    tile_x = along_z.shape[1]
    tile_y = along_z.shape[2]
    wide_count = lax.axis_size("wide")
    narrow_count = lax.axis_size("narrow")
    slab = depth // (wide_count * narrow_count)
    arrived = lax.all_to_all(along_z, ("wide", "narrow"), split_axis=0, concat_axis=0, tiled=True)
    arrived = arrived.reshape(wide_count, narrow_count, slab, tile_x, tile_y)
    pencil = jnp.transpose(arrived, (2, 0, 3, 1, 4)).reshape(
        slab, wide_count * tile_x, narrow_count * tile_y
    )
    full_y = pencil.shape[2]
    table_y = cosine_table(full_y)
    flat = pencil.reshape(-1, full_y)
    spectrum = lax.dot_general(
        flat, table_y, (((1,), (1,)), ((), ())), preferred_element_type=jnp.float32
    )
    return spectrum.reshape(pencil.shape).astype(jnp.bfloat16)


def solution(mesh):
    placed = (P(None, "wide", "narrow", None), P("wide", "narrow", None))
    return jax.shard_map(
        per_device,
        mesh=mesh,
        in_specs=placed,
        out_specs=P(("wide", "narrow"), None, None),
        check_vma=False,
    )
```

profile of v0, /device:TPU:0, one launch (start us, length us, event | category | flops | bytes accessed | tf_op | source)
XLA Modules:
  0.0 349.5 jit_solution(7338264178347005740)
XLA Ops:
  0.0 29.2 %convert_multiply_fusion.2 = (f32[32,256,512]{2,1,0:T(8,128)}, f32[32,256,512]{2,1,0:T(8,128)}, f32[32,256,512]{2,1,0:T(8,128)}) fusion(bf16[3,32,256,512]{3,2,1,0:T(8,128)(2,1)} %param.2, s32[32,256,512]{2,1,0:T(8,128)} %param.3), kind=kLoop, calls=%fused_computation.16 | loop fusion | flops 37748736 | bytes 92274688 | tf_op jit(solution)/shard_map/mul | solution.py:35
  29.2 1.3 fusion.29
  30.5 1.3 collective-permute-start
  31.8 3.1 collective-permute-start.1
  34.9 1.3 fusion.30
  36.2 1.3 collective-permute-start.2
  37.5 5.5 %collective-permute-start.3 = (f32[32,1,512]{2,1,0:T(1,128)S(1)}, f32[32,1,512]{2,1,0:T(1,128)S(1)}, u32[]{:S(2)}, u32[]{:S(2)}) collective-permute-start(f32[32,1,512]{2,1,0:T(1,128)S(1)} %get-tuple-element.11), channel_id=1, source_target_pairs={{0,1},{1,2},{2,3},{4,5},{5,6},{6,7},{8,9},{9,10},{10,11},{12,13},{... | collective-permute-start | bytes 196616 | tf_op jit(solution)/shard_map/ppermute | solution.py:15
  43.0 0.3 collective-permute-done.2
  43.3 1.8 collective-permute-done.3
  45.1 0.0 collective-permute-done
  45.1 0.0 collective-permute-done.1
  45.1 33.7 %fusion.38 = bf16[32,256,512]{2,1,0:T(8,128)(2,1)S(1)} fusion(f32[32,256,512]{2,1,0:T(8,128)} %get-tuple-element.6, f32[32,256,512]{2,1,0:T(8,128)} %get-tuple-element.7, f32[32,1,512]{2,1,0:T(1,128)S(1)} %collective-permute-done.3, f32[32,1,512]{2,1,0:T(1,128)S(1)} %collective-permute-done.2, f32[32,256,512]{2,1,0:T(8,128)} %get-tuple-element.5, ...), kind=kLoop, calls=%fused_computation.6.clone.clone.clone.clone.2 | loop fusion | flops 46137344 | bytes 59899904 | tf_op jit(solution)/shard_map/kn,xyn->kxy/dot_general | solution.py:47
  78.8 10.3 %fusion.9 = bf16[512,32,256]{2,0,1:T(8,128)(2,1)} fusion(f32[512]{0:T(512)S(1)} %get-tuple-element.12, f32[512]{0:T(512)S(1)} %get-tuple-element.13, bf16[32,256,512]{2,1,0:T(8,128)(2,1)S(1)} %fusion.38), kind=kOutput, calls=%fused_computation.20 | convolution fusion | flops 4300210176 | bytes 16781312 | tf_op jit(solution)/shard_map/kn,xyn->kxy/dot_general | solution.py:47
  89.1 11.4 %copy.4 = bf16[512,32,256]{2,1,0:T(8,128)(2,1)} copy(bf16[512,32,256]{2,0,1:T(8,128)(2,1)} %fusion.9) | data formatting | bytes 16777216 | tf_op jit(solution)/shard_map/convert_element_type | solution.py:49
  100.5 8.2 %all-to-all-start = ((bf16[512,32,256]{2,1,0:T(8,128)(2,1)}), bf16[512,32,256]{2,1,0:T(8,128)(2,1)}, u32[]{:S(2)}, u32[]{:S(2)}) async-start(bf16[512,32,256]{2,1,0:T(8,128)(2,1)} %copy.4), calls=%async_computation | async-start | bytes 16777216 | tf_op jit(solution)/shard_map/all_to_all | solution.py:55
  108.7 187.8 %all-to-all-done = bf16[512,32,256]{2,1,0:T(8,128)(2,1)} async-done(((bf16[512,32,256]{2,1,0:T(8,128)(2,1)}), bf16[512,32,256]{2,1,0:T(8,128)(2,1)}, u32[]{:S(2)}, u32[]{:S(2)}) %all-to-all-start) | async-done | bytes 8388640 | tf_op jit(solution)/shard_map/all_to_all | solution.py:55
  296.5 11.1 %copy.7 = bf16[8,4,16,32,256]{4,1,3,0,2:T(4,128)(2,1)} copy(bf16[8,4,16,32,256]{4,3,2,1,0:T(8,128)(2,1)} %bitcast.4) | data formatting | bytes 16777216 | tf_op jit(solution)/shard_map/reshape | solution.py:56
  307.6 14.3 %dot_general.9 = bf16[16,256,1024]{2,1,0:T(8,128)(2,1)} reshape(bf16[16,8,32,4,256]{4,3,2,1,0:T(4,128)(2,1)} %bitcast.24) | data formatting | bytes 16777216 | tf_op jit(solution)/shard_map/dot_general | solution.py:63
  321.9 27.6 %convolution_convert_fusion = bf16[16,256,1024]{2,1,0:T(8,128)(2,1)} fusion(bf16[16,256,1024]{2,1,0:T(8,128)(2,1)} %dot_general.9, f32[1024]{0:T(1024)S(1)} %get-tuple-element.14, f32[1024]{0:T(1024)S(1)} %get-tuple-element.15), kind=kOutput, calls=%fused_computation.19 | convolution fusion | flops 8598323200 | bytes 16785408 | tf_op jit(solution)/shard_map/dot_general | solution.py:63
  (2 shorter events, 0.0 us)
Async XLA Ops:
  30.5 14.6 %collective-permute-start = (f32[1,256,512]{2,1,0:T(8,128)S(1)}, f32[1,256,512]{2,1,0:T(8,128)S(1)}, u32[]{:S(2)}, u32[]{:S(2)}) collective-permute-start(f32[1,256,512]{2,1,0:T(8,128)S(1)} %get-tuple-element.8), channel_id=1, source_target_pairs={{4,0},{8,4},{12,8},{16,12},{20,16},{24,20},{28,24},{5,1},{9,5},{13... | collective-permute-start | bytes 1572872 | tf_op jit(solution)/shard_map/ppermute | solution.py:17
  31.8 13.3 %collective-permute-start.1 = (f32[1,256,512]{2,1,0:T(8,128)S(1)}, f32[1,256,512]{2,1,0:T(8,128)S(1)}, u32[]{:S(2)}, u32[]{:S(2)}) collective-permute-start(f32[1,256,512]{2,1,0:T(8,128)S(1)} %get-tuple-element.9), channel_id=1, source_target_pairs={{0,4},{4,8},{8,12},{12,16},{16,20},{20,24},{24,28},{1,5},{5,9},{9,... | collective-permute-start | bytes 1572872 | tf_op jit(solution)/shard_map/ppermute | solution.py:15
  36.2 7.1 %collective-permute-start.2 = (f32[32,1,512]{2,1,0:T(1,128)S(1)}, f32[32,1,512]{2,1,0:T(1,128)S(1)}, u32[]{:S(2)}, u32[]{:S(2)}) collective-permute-start(f32[32,1,512]{2,1,0:T(1,128)S(1)} %get-tuple-element.10), channel_id=1, source_target_pairs={{1,0},{2,1},{3,2},{5,4},{6,5},{7,6},{9,8},{10,9},{11,10},{13,12},{... | collective-permute-start | bytes 196616 | tf_op jit(solution)/shard_map/ppermute | solution.py:17
  37.5 7.6 %collective-permute-start.3 = (f32[32,1,512]{2,1,0:T(1,128)S(1)}, f32[32,1,512]{2,1,0:T(1,128)S(1)}, u32[]{:S(2)}, u32[]{:S(2)}) collective-permute-start(f32[32,1,512]{2,1,0:T(1,128)S(1)} %get-tuple-element.11), channel_id=1, source_target_pairs={{0,1},{1,2},{2,3},{4,5},{5,6},{6,7},{8,9},{9,10},{10,11},{12,13},{... | collective-permute-start | bytes 196616 | tf_op jit(solution)/shard_map/ppermute | solution.py:15
  100.5 196.1 %all-to-all-start = ((bf16[512,32,256]{2,1,0:T(8,128)(2,1)}), bf16[512,32,256]{2,1,0:T(8,128)(2,1)}, u32[]{:S(2)}, u32[]{:S(2)}) async-start(bf16[512,32,256]{2,1,0:T(8,128)(2,1)} %copy.4), calls=%async_computation | async-start | bytes 16777216 | tf_op jit(solution)/shard_map/all_to_all | solution.py:55
where the time goes:
time: 350 us; the launch traced here: 349 us
  waiting for transfers between devices  190 us (54%)
  other arithmetic  62.9 us (18%)
  local copies, waits for them, and re-layouts  39.3 us (11%)
  matrix products  37.9 us (11%)
  starting transfers between devices  19.3 us (6%)
    all_to_all x1, waiting for transfers between devices, per_device(): lax.all_to_all(along_z, ('wide', 'narrow'), split_axis=0, concat_axis=0,...  188 us
    dot_general x1, other arithmetic, per_device(): jnp.einsum('kn,xyn->kxy', table_z, divergence, preferred_element_type=jnp...  33.7 us
    mul x1, other arithmetic, per_device(): flux_x = weight * normals[0].astype(jnp.float32)  29.2 us
    dot_general x1, matrix products, per_device(): lax.dot_general(flat, table_y, (((1,), (1,)), ((), ())), preferred_elemen...  27.6 us
    dot_general x1, local copies, waits for them, and re-layouts, per_device(): lax.dot_general(flat, table_y, (((1,), (1,)), ((), ())), preferred_elemen...  14.3 us
    convert_element_type x1, local copies, waits for them, and re-layouts, per_device(): along_z = jnp.einsum('kn,xyn->kxy', table_z, divergence, preferred_elemen...  11.4 us
    reshape x1, local copies, waits for them, and re-layouts, per_device(): arrived = arrived.reshape(wide_count, narrow_count, slab, tile_x, tile_y)  11.1 us
    dot_general x1, matrix products, per_device(): jnp.einsum('kn,xyn->kxy', table_z, divergence, preferred_element_type=jnp...  10.3 us
  transfers between devices with their start and end apart: 5, of which 3 were waited for; matrix products, arithmetic and copies ran while one was open for 0% of the time, Pallas kernels for 0%

commit v1 on v0

v1 whole, which is shorter than its diff:
```python
import functools

import jax
import jax.numpy as jnp
import ml_dtypes
import numpy as np
from jax import lax
from jax.experimental import pallas as pl
from jax.experimental.pallas import tpu as pltpu
from jax.sharding import PartitionSpec as P

VMEM_BYTES = 56 * 1024 * 1024
PAD = 8


def cosine_table(size):
    freq = np.arange(size, dtype=np.float64)[:, None]
    place = np.arange(size, dtype=np.float64)[None, :]
    waves = np.cos(np.pi * (2.0 * place + 1.0) * freq / (2.0 * size))
    scales = np.where(freq == 0.0, np.sqrt(1.0 / size), np.sqrt(2.0 / size))
    return (scales * waves).astype(ml_dtypes.bfloat16)


def weight_of(counts):
    values = counts.astype(jnp.float32)
    return values / (values + 4.0)


def strip_rows(rows):
    return 32 if rows % 32 == 0 else 8


def planes_kernel(start, planes, total, normals, counts, low_y, high_y, low_x, high_x, table, out,
                  flux_y, weights, last_x, partial, divergence):
    step = pl.program_id(0)
    plane = jnp.clip(start - 1 + step, 0, total - 1)
    rows, depth = weights.shape
    strip = strip_rows(rows)
    strips = [slice(r, r + strip) for r in range(0, rows, strip)]

    for at in strips:
        weight = weight_of(counts[0, at, :])
        weights[at, :] = weight
        flux_y[PAD + at.start:PAD + at.stop, :] = weight * normals[1, 0, at, :].astype(jnp.float32)
    flux_y[PAD - 1:PAD, :] = low_y[pl.ds(plane, 1), :]
    flux_y[PAD + rows:PAD + rows + 1, :] = high_y[pl.ds(plane, 1), :]

    lane = lax.broadcasted_iota(jnp.int32, (strip, depth), 1)
    for at in strips:
        weight = weights[at, :]
        flux_x = weight * normals[0, 0, at, :].astype(jnp.float32)
        if start == 0:
            flux_x = jnp.where(step == 0, low_x[at, :].astype(jnp.float32), flux_x)
        if start + planes == total:
            flux_x = jnp.where(step == planes + 1, high_x[at, :].astype(jnp.float32), flux_x)
        flux_z = weight * normals[2, 0, at, :].astype(jnp.float32)
        after_z = jnp.where(lane == depth - 1, 0.0, pltpu.roll(flux_z, depth - 1, 1))
        before_z = jnp.where(lane == 0, 0.0, pltpu.roll(flux_z, 1, 1))
        diff_y = flux_y[PAD + at.start + 1:PAD + at.stop + 1, :] - flux_y[PAD + at.start - 1:PAD + at.stop - 1, :]
        divergence[at, :] = (0.5 * (flux_x + partial[at, :])).astype(jnp.bfloat16)
        partial[at, :] = diff_y + (after_z - before_z) - last_x[at, :]
        last_x[at, :] = flux_x

    @pl.when(step >= 2)
    def _():
        along = lax.dot_general(
            table[...], divergence[...], (((1,), (1,)), ((), ())), preferred_element_type=jnp.float32
        ).astype(jnp.bfloat16)
        out[:, 0] = along.reshape(out.shape[0], out.shape[2], rows)


def along_z_of(normals, counts, halos, table, start, planes, groups):
    _, total, rows, depth = normals.shape

    def plane_at(step):
        return jnp.clip(start - 1 + step, 0, total - 1)

    whole = pl.BlockSpec((rows, depth), lambda step: (0, 0))
    lines = pl.BlockSpec((total, depth), lambda step: (0, 0))
    size = planes * rows * depth
    return pl.pallas_call(
        functools.partial(planes_kernel, start, planes, total),
        grid=(planes + 2,),
        in_specs=[
            pl.BlockSpec((3, 1, rows, depth), lambda step: (0, plane_at(step), 0, 0)),
            pl.BlockSpec((1, rows, depth), lambda step: (plane_at(step), 0, 0)),
            lines,
            lines,
            whole,
            whole,
            pl.BlockSpec((depth, depth), lambda step: (0, 0)),
        ],
        out_specs=pl.BlockSpec((groups, 1, depth // groups, rows), lambda step: (0, jnp.maximum(step - 2, 0), 0, 0)),
        out_shape=jax.ShapeDtypeStruct((groups, planes, depth // groups, rows), jnp.bfloat16),
        scratch_shapes=[
            pltpu.VMEM((rows + 2 * PAD, depth), jnp.float32),
            pltpu.VMEM((rows, depth), jnp.float32),
            pltpu.VMEM((rows, depth), jnp.float32),
            pltpu.VMEM((rows, depth), jnp.float32),
            pltpu.VMEM((rows, depth), jnp.bfloat16),
        ],
        compiler_params=pltpu.CompilerParams(vmem_limit_bytes=VMEM_BYTES),
        cost_estimate=pl.CostEstimate(flops=2 * size * depth, bytes_accessed=12 * size, transcendentals=size),
    )(normals, counts, *halos, table)


def y_kernel(arrived, table, order, *rest):
    out = rest[-1]
    tiles, planes, slab, rows = arrived.shape
    total = jnp.zeros((planes * slab, table.shape[1]), jnp.float32)
    for tile in range(tiles):
        total += jnp.dot(
            arrived[tile].reshape(planes * slab, rows),
            table[tile * rows:(tile + 1) * rows, :],
            preferred_element_type=jnp.float32,
        )
    moved = jnp.dot(order[...], total.astype(jnp.bfloat16), preferred_element_type=jnp.float32)
    out[...] = moved.astype(jnp.bfloat16).reshape(slab, planes, table.shape[1])


def along_y_of(arrived, table, so_far, start, total, wide, narrow):
    _, planes, slab, rows = arrived.shape
    full_y = table.shape[1]
    count = planes * slab
    order = np.zeros((slab, planes, planes, slab), np.float32)
    for k in range(slab):
        for i in range(planes):
            order[k, i, i, k] = 1.0
    order = jnp.asarray(order.reshape(count, count).astype(ml_dtypes.bfloat16))
    operands = [arrived, table, order]
    in_specs = [
        pl.BlockSpec((narrow, planes, slab, rows), lambda at: (at, 0, 0, 0)),
        pl.BlockSpec(table.shape, lambda at: (0, 0)),
        pl.BlockSpec(order.shape, lambda at: (0, 0)),
    ]
    aliases = {}
    if so_far is not None:
        operands.append(so_far)
        in_specs.append(pl.BlockSpec(memory_space=pl.ANY))
        aliases = {3: 0}
    size = wide * count * full_y
    return pl.pallas_call(
        y_kernel,
        grid=(wide,),
        in_specs=in_specs,
        out_specs=pl.BlockSpec((slab, planes, full_y), lambda at: (0, at * (total // planes) + start // planes, 0)),
        out_shape=jax.ShapeDtypeStruct((slab, wide * total, full_y), jnp.bfloat16),
        input_output_aliases=aliases,
        compiler_params=pltpu.CompilerParams(vmem_limit_bytes=VMEM_BYTES),
        cost_estimate=pl.CostEstimate(flops=2 * size * (full_y + count), bytes_accessed=4 * size, transcendentals=0),
    )(*operands)


def halos_of(normals, counts):
    wide = lax.axis_size("wide")
    narrow = lax.axis_size("narrow")
    up = lambda count: [(i, i + 1) for i in range(count - 1)]
    down = lambda count: [(i + 1, i) for i in range(count - 1)]
    edge_y = lambda at: weight_of(counts[:, at, :]) * normals[1, :, at, :].astype(jnp.float32)
    edge_x = lambda at: (weight_of(counts[at]) * normals[0, at].astype(jnp.float32)).astype(jnp.bfloat16)
    return (
        lax.ppermute(edge_y(counts.shape[1] - 1), "narrow", up(narrow)),
        lax.ppermute(edge_y(0), "narrow", down(narrow)),
        lax.ppermute(edge_x(counts.shape[0] - 1), "wide", up(wide)),
        lax.ppermute(edge_x(0), "wide", down(wide)),
    )


def per_device(normals, counts):
    wide = lax.axis_size("wide")
    narrow = lax.axis_size("narrow")
    _, total, rows, depth = normals.shape
    full_y = narrow * rows
    slab = depth // (wide * narrow)
    halos = halos_of(normals, counts)
    table_z = jnp.asarray(cosine_table(depth))
    table_y = jnp.asarray(np.ascontiguousarray(cosine_table(full_y).T))
    if slab % 16 == 0:
        planes = 8
        quarter = total // planes
        starts = [((at + 1) % quarter) * planes for at in range(quarter)]
        spectrum = None
        for start in starts:
            along = along_z_of(normals, counts, halos, table_z, start, planes, wide * narrow)
            arrived = lax.all_to_all(along, ("wide", "narrow"), split_axis=0, concat_axis=0, tiled=True)
            spectrum = along_y_of(arrived, table_y, spectrum, start, total, wide, narrow)
        return spectrum
    along = along_z_of(normals, counts, halos, table_z, 0, total, 1)
    along = along.reshape(total, wide * narrow, slab, rows)
    arrived = lax.all_to_all(along, ("wide", "narrow"), split_axis=1, concat_axis=1, tiled=True)
    arrived = arrived.reshape(total, wide, narrow, slab, rows)
    pencil = jnp.transpose(arrived, (3, 1, 0, 2, 4)).reshape(slab * wide * total, full_y)
    spectrum = jnp.dot(pencil, table_y, preferred_element_type=jnp.float32).astype(jnp.bfloat16)
    return spectrum.reshape(slab, wide * total, full_y)


def solution(mesh):
    placed = (P(None, "wide", "narrow", None), P("wide", "narrow", None))
    return jax.shard_map(
        per_device,
        mesh=mesh,
        in_specs=placed,
        out_specs=P(("wide", "narrow"), None, None),
        check_vma=False,
    )
```

time: 350 us -> 263 us (0.75)
  the two profiles are of different devices: /device:TPU:0 before, /device:TPU:8 now
where the time goes in v1:
time: 263 us; the launch traced here: 259 us
  waiting for transfers between devices  133 us (51%)
  Pallas kernels  87.3 us (33%)
  starting transfers between devices  30.2 us (11%)
  local copies, waits for them, and re-layouts  6.57 us (2%)
    all_to_all x4, waiting for transfers between devices, per_device(): lax.all_to_all(along, ('wide', 'narrow'), split_axis=0, concat_axis=0, ti...  128 us
    pallas_call x4, Pallas kernels, along_z_of(): pl.pallas_call(functools.partial(planes_kernel, start, planes, total), gr...  52.2 us
    pallas_call x4, Pallas kernels, along_y_of(): pl.pallas_call(y_kernel, grid=(wide,), in_specs=in_specs, out_specs=pl.Bl...  35.1 us
    all_to_all x4, starting transfers between devices, per_device(): lax.all_to_all(along, ('wide', 'narrow'), split_axis=0, concat_axis=0, ti...  19.9 us
  transfers between devices with their start and end apart: 8, of which 5 were waited for; matrix products, arithmetic and copies ran while one was open for 1% of the time, Pallas kernels for 25%

profile of v1, /device:TPU:8, one launch (start us, length us, event | category | flops | bytes accessed | tf_op | source)
XLA Modules:
  0.0 258.9 jit_solution(8015035618121647111)
XLA Ops:
  0.0 1.3 fusion.9
  2.5 3.4 %collective-permute-start = (f32[32,512]{1,0:T(8,128)S(1)}, f32[32,512]{1,0:T(8,128)S(1)}, u32[]{:S(2)}, u32[]{:S(2)}) collective-permute-start(f32[32,512]{1,0:T(8,128)S(1)} %fusion.4), channel_id=1, source_target_pairs={{0,1},{1,2},{2,3},{4,5},{5,6},{6,7},{8,9},{9,10},{10,11},{12,13},{... | collective-permute-start | bytes 196616 | tf_op jit(solution)/shard_map/ppermute | solution.py:162
  5.9 1.6 fusion.3
  7.5 1.9 collective-permute-start.2
  9.4 3.6 %collective-permute-start.3 = (bf16[256,512]{1,0:T(8,128)(2,1)S(1)}, bf16[256,512]{1,0:T(8,128)(2,1)S(1)}, u32[]{:S(2)}, u32[]{:S(2)}) collective-permute-start(bf16[256,512]{1,0:T(8,128)(2,1)S(1)} %get-tuple-element.5), channel_id=1, source_target_pairs={{4,0},{8,4},{12,8},{16,12},{20,16},{24,20},{28,24},{5,1},{9,5},{13... | collective-permute-start | bytes 786440 | tf_op jit(solution)/shard_map/ppermute | solution.py:165
  14.4 4.8 %collective-permute-done.1.high_y = f32[32,512]{1,0:T(8,128)S(1)} collective-permute-done((f32[32,512]{1,0:T(8,128)S(1)}, f32[32,512]{1,0:T(8,128)S(1)}, u32[]{:S(2)}, u32[]{:S(2)}) %collective-permute-start.1) | collective-permute-done | bytes 65568 | tf_op jit(solution)/shard_map/ppermute | solution.py:163
  20.7 13.0 %shard_map.85 = bf16[32,8,16,256]{3,2,1,0:T(8,128)(2,1)} custom-call(bf16[3,32,256,512]{3,2,1,0:T(8,128)(2,1)} %normals.7, s32[32,256,512]{2,1,0:T(8,128)} %counts.7, f32[32,512]{1,0:T(8,128)} %copy-done.5, f32[32,512]{1,0:T(8,128)} %copy-done.6, bf16[256,512]{1,0:T(8,128)(2,1)} %copy-done.3, bf16[256,512]{1,0:T(8,128)(2,1)} %copy-done.4, ...), custom_call_target="tpu_custom_call" | custom-call | flops 1073741824 | bytes 12582912 | tf_op jit(solution)/shard_map/pallas_call | solution.py:81
  33.7 6.0 %all-to-all-start.3 = ((bf16[32,8,16,256]{3,2,1,0:T(8,128)(2,1)}), bf16[32,8,16,256]{3,2,1,0:T(8,128)(2,1)S(1)}, u32[]{:S(2)}, u32[]{:S(2)}) async-start(bf16[32,8,16,256]{3,2,1,0:T(8,128)(2,1)} %shard_map.85), calls=%async_computation.3 | async-start | bytes 4194304 | tf_op jit(solution)/shard_map/all_to_all | solution.py:185
  39.7 13.0 %shard_map.84 = bf16[32,8,16,256]{3,2,1,0:T(8,128)(2,1)} custom-call(bf16[3,32,256,512]{3,2,1,0:T(8,128)(2,1)} %normals.7, s32[32,256,512]{2,1,0:T(8,128)} %counts.7, f32[32,512]{1,0:T(8,128)} %copy-done.5, f32[32,512]{1,0:T(8,128)} %copy-done.6, bf16[256,512]{1,0:T(8,128)(2,1)} %copy-done.3, bf16[256,512]{1,0:T(8,128)(2,1)} %copy-done.4, ...), custom_call_target="tpu_custom_call" | custom-call | flops 1073741824 | bytes 12582912 | tf_op jit(solution)/shard_map/pallas_call | solution.py:81
  52.7 35.4 %all-to-all-done.3.arrived = bf16[32,8,16,256]{3,2,1,0:T(8,128)(2,1)S(1)} async-done(((bf16[32,8,16,256]{3,2,1,0:T(8,128)(2,1)}), bf16[32,8,16,256]{3,2,1,0:T(8,128)(2,1)S(1)}, u32[]{:S(2)}, u32[]{:S(2)}) %all-to-all-start.3) | async-done | bytes 2097184 | tf_op jit(solution)/shard_map/all_to_all | solution.py:185
  88.1 1.3 copy-done.2
  89.5 4.6 %all-to-all-start.2 = ((bf16[32,8,16,256]{3,2,1,0:T(8,128)(2,1)}), bf16[32,8,16,256]{3,2,1,0:T(8,128)(2,1)S(1)}, u32[]{:S(2)}, u32[]{:S(2)}) async-start(bf16[32,8,16,256]{3,2,1,0:T(8,128)(2,1)} %shard_map.84), calls=%async_computation.2 | async-start | bytes 4194304 | tf_op jit(solution)/shard_map/all_to_all | solution.py:185
  94.1 13.0 %shard_map.83 = bf16[32,8,16,256]{3,2,1,0:T(8,128)(2,1)} custom-call(bf16[3,32,256,512]{3,2,1,0:T(8,128)(2,1)} %normals.7, s32[32,256,512]{2,1,0:T(8,128)} %counts.7, f32[32,512]{1,0:T(8,128)} %copy-done.5, f32[32,512]{1,0:T(8,128)} %copy-done.6, bf16[256,512]{1,0:T(8,128)(2,1)} %copy-done.3, bf16[256,512]{1,0:T(8,128)(2,1)} %copy-done.4, ...), custom_call_target="tpu_custom_call" | custom-call | flops 1073741824 | bytes 12582912 | tf_op jit(solution)/shard_map/pallas_call | solution.py:81
  107.1 35.4 %all-to-all-done.2.arrived = bf16[32,8,16,256]{3,2,1,0:T(8,128)(2,1)S(1)} async-done(((bf16[32,8,16,256]{3,2,1,0:T(8,128)(2,1)}), bf16[32,8,16,256]{3,2,1,0:T(8,128)(2,1)S(1)}, u32[]{:S(2)}, u32[]{:S(2)}) %all-to-all-start.2) | async-done | bytes 2097184 | tf_op jit(solution)/shard_map/all_to_all | solution.py:185
  142.5 4.7 %all-to-all-start.1 = ((bf16[32,8,16,256]{3,2,1,0:T(8,128)(2,1)}), bf16[32,8,16,256]{3,2,1,0:T(8,128)(2,1)}, u32[]{:S(2)}, u32[]{:S(2)}) async-start(bf16[32,8,16,256]{3,2,1,0:T(8,128)(2,1)} %shard_map.83), calls=%async_computation.1 | async-start | bytes 4194304 | tf_op jit(solution)/shard_map/all_to_all | solution.py:185
  147.2 13.2 %shard_map.82 = bf16[32,8,16,256]{3,2,1,0:T(8,128)(2,1)} custom-call(bf16[3,32,256,512]{3,2,1,0:T(8,128)(2,1)} %normals.7, s32[32,256,512]{2,1,0:T(8,128)} %counts.7, f32[32,512]{1,0:T(8,128)} %copy-done.5, f32[32,512]{1,0:T(8,128)} %copy-done.6, bf16[256,512]{1,0:T(8,128)(2,1)} %copy-done.3, bf16[256,512]{1,0:T(8,128)(2,1)} %copy-done.4, ...), custom_call_target="tpu_custom_call" | custom-call | flops 1073741824 | bytes 12582912 | tf_op jit(solution)/shard_map/pallas_call | solution.py:81
  160.5 35.3 %all-to-all-done.1.arrived = bf16[32,8,16,256]{3,2,1,0:T(8,128)(2,1)} async-done(((bf16[32,8,16,256]{3,2,1,0:T(8,128)(2,1)}), bf16[32,8,16,256]{3,2,1,0:T(8,128)(2,1)}, u32[]{:S(2)}, u32[]{:S(2)}) %all-to-all-start.1) | async-done | bytes 2097184 | tf_op jit(solution)/shard_map/all_to_all | solution.py:185
  195.7 4.6 %all-to-all-start = ((bf16[32,8,16,256]{3,2,1,0:T(8,128)(2,1)}), bf16[32,8,16,256]{3,2,1,0:T(8,128)(2,1)S(1)}, u32[]{:S(2)}, u32[]{:S(2)}) async-start(bf16[32,8,16,256]{3,2,1,0:T(8,128)(2,1)} %shard_map.82), calls=%async_computation | async-start | bytes 4194304 | tf_op jit(solution)/shard_map/all_to_all | solution.py:185
  200.4 8.8 %shard_map.86.rest_0_ = bf16[16,256,1024]{2,1,0:T(8,128)(2,1)} custom-call(bf16[32,8,16,256]{3,2,1,0:T(8,128)(2,1)} %copy-done.2, bf16[1024,1024]{1,0:T(8,128)(2,1)} %constant.10.clone.table, bf16[128,128]{1,0:T(8,128)(2,1)} %constant.11.clone.order), custom_call_target="tpu_custom_call" | custom-call | flops 2415919104 | bytes 4194304 | tf_op jit(solution)/shard_map/pallas_call | solution.py:142
  209.2 8.8 %shard_map.87.rest_0_ = bf16[16,256,1024]{2,1,0:T(8,128)(2,1)} custom-call(bf16[32,8,16,256]{3,2,1,0:T(8,128)(2,1)} %copy-done, bf16[1024,1024]{1,0:T(8,128)(2,1)} %constant.10.clone.table, bf16[128,128]{1,0:T(8,128)(2,1)} %constant.11.clone.order, bf16[16,256,1024]{2,1,0:T(8,128)(2,1)} %shard_map.86.rest_0_), custom_call_target="tpu_custom_call", output_to_operand_aliasing={{}: (3, {})} | custom-call | flops 2415919104 | bytes 4194304 | tf_op jit(solution)/shard_map/pallas_call | solution.py:142
  217.9 8.8 %shard_map.88.rest_0_ = bf16[16,256,1024]{2,1,0:T(8,128)(2,1)} custom-call(bf16[32,8,16,256]{3,2,1,0:T(8,128)(2,1)} %all-to-all-done.1.arrived, bf16[1024,1024]{1,0:T(8,128)(2,1)} %constant.10.clone.table, bf16[128,128]{1,0:T(8,128)(2,1)} %constant.11.clone.order, bf16[16,256,1024]{2,1,0:T(8,128)(2,1)} %shard_map.87.rest_0_), custom_call_target="tpu_custom_call", output_to_operand_aliasing={{}: (3, {})} | custom-call | flops 2415919104 | bytes 4194304 | tf_op jit(solution)/shard_map/pallas_call | solution.py:142
  226.7 22.1 %all-to-all-done.arrived = bf16[32,8,16,256]{3,2,1,0:T(8,128)(2,1)S(1)} async-done(((bf16[32,8,16,256]{3,2,1,0:T(8,128)(2,1)}), bf16[32,8,16,256]{3,2,1,0:T(8,128)(2,1)S(1)}, u32[]{:S(2)}, u32[]{:S(2)}) %all-to-all-start) | async-done | bytes 2097184 | tf_op jit(solution)/shard_map/all_to_all | solution.py:185
  248.8 1.3 copy-done.1
  250.2 8.8 %shard_map.89 = bf16[16,256,1024]{2,1,0:T(8,128)(2,1)} custom-call(bf16[32,8,16,256]{3,2,1,0:T(8,128)(2,1)} %copy-done.1, bf16[1024,1024]{1,0:T(8,128)(2,1)} %constant.10.clone.table, bf16[128,128]{1,0:T(8,128)(2,1)} %constant.11.clone.order, bf16[16,256,1024]{2,1,0:T(8,128)(2,1)} %shard_map.88.rest_0_), custom_call_target="tpu_custom_call", output_to_operand_aliasing={{}: (3, {})} | custom-call | flops 2415919104 | bytes 4194304 | tf_op jit(solution)/shard_map/pallas_call | solution.py:142
  (19 shorter events, 3.9 us)
Async XLA Ops:
  2.5 11.9 %collective-permute-start = (f32[32,512]{1,0:T(8,128)S(1)}, f32[32,512]{1,0:T(8,128)S(1)}, u32[]{:S(2)}, u32[]{:S(2)}) collective-permute-start(f32[32,512]{1,0:T(8,128)S(1)} %fusion.4), channel_id=1, source_target_pairs={{0,1},{1,2},{2,3},{4,5},{5,6},{6,7},{8,9},{9,10},{10,11},{12,13},{... | collective-permute-start | bytes 196616 | tf_op jit(solution)/shard_map/ppermute | solution.py:162
  7.5 11.8 %collective-permute-start.2 = (bf16[256,512]{1,0:T(8,128)(2,1)S(1)}, bf16[256,512]{1,0:T(8,128)(2,1)S(1)}, u32[]{:S(2)}, u32[]{:S(2)}) collective-permute-start(bf16[256,512]{1,0:T(8,128)(2,1)S(1)} %get-tuple-element.6), channel_id=1, source_target_pairs={{0,4},{4,8},{8,12},{12,16},{16,20},{20,24},{24,28},{1,5},{5,9},{9,... | collective-permute-start | bytes 786440 | tf_op jit(solution)/shard_map/ppermute | solution.py:164
  9.4 9.8 %collective-permute-start.3 = (bf16[256,512]{1,0:T(8,128)(2,1)S(1)}, bf16[256,512]{1,0:T(8,128)(2,1)S(1)}, u32[]{:S(2)}, u32[]{:S(2)}) collective-permute-start(bf16[256,512]{1,0:T(8,128)(2,1)S(1)} %get-tuple-element.5), channel_id=1, source_target_pairs={{4,0},{8,4},{12,8},{16,12},{20,16},{24,20},{28,24},{5,1},{9,5},{13... | collective-permute-start | bytes 786440 | tf_op jit(solution)/shard_map/ppermute | solution.py:165
  13.1 6.2 %collective-permute-start.1 = (f32[32,512]{1,0:T(8,128)S(1)}, f32[32,512]{1,0:T(8,128)S(1)}, u32[]{:S(2)}, u32[]{:S(2)}) collective-permute-start(f32[32,512]{1,0:T(8,128)S(1)} %fusion.5), channel_id=1, source_target_pairs={{1,0},{2,1},{3,2},{5,4},{6,5},{7,6},{9,8},{10,9},{11,10},{13,12},{... | collective-permute-start | bytes 196616 | tf_op jit(solution)/shard_map/ppermute | solution.py:163
  14.4 4.9 %copy-start.5 = (f32[32,512]{1,0:T(8,128)}, f32[32,512]{1,0:T(8,128)S(1)}, u32[]{:S(2)}) copy-start(f32[32,512]{1,0:T(8,128)S(1)} %collective-permute-done.low_y) | copy-start | bytes 196612
  19.3 0.6 copy-start.6
  19.3 0.7 copy-start.3
  20.0 0.7 copy-start.4
  33.7 54.4 %all-to-all-start.3 = ((bf16[32,8,16,256]{3,2,1,0:T(8,128)(2,1)}), bf16[32,8,16,256]{3,2,1,0:T(8,128)(2,1)S(1)}, u32[]{:S(2)}, u32[]{:S(2)}) async-start(bf16[32,8,16,256]{3,2,1,0:T(8,128)(2,1)} %shard_map.85), calls=%async_computation.3 | async-start | bytes 4194304 | tf_op jit(solution)/shard_map/all_to_all | solution.py:185
  88.1 1.3 copy-start.2
  89.5 53.1 %all-to-all-start.2 = ((bf16[32,8,16,256]{3,2,1,0:T(8,128)(2,1)}), bf16[32,8,16,256]{3,2,1,0:T(8,128)(2,1)S(1)}, u32[]{:S(2)}, u32[]{:S(2)}) async-start(bf16[32,8,16,256]{3,2,1,0:T(8,128)(2,1)} %shard_map.84), calls=%async_computation.2 | async-start | bytes 4194304 | tf_op jit(solution)/shard_map/all_to_all | solution.py:185
  142.5 17.9 %copy-start = (bf16[32,8,16,256]{3,2,1,0:T(8,128)(2,1)}, bf16[32,8,16,256]{3,2,1,0:T(8,128)(2,1)S(1)}, u32[]{:S(2)}) copy-start(bf16[32,8,16,256]{3,2,1,0:T(8,128)(2,1)S(1)} %all-to-all-done.2.arrived) | copy-start | bytes 6291460
  142.5 53.2 %all-to-all-start.1 = ((bf16[32,8,16,256]{3,2,1,0:T(8,128)(2,1)}), bf16[32,8,16,256]{3,2,1,0:T(8,128)(2,1)}, u32[]{:S(2)}, u32[]{:S(2)}) async-start(bf16[32,8,16,256]{3,2,1,0:T(8,128)(2,1)} %shard_map.83), calls=%async_computation.1 | async-start | bytes 4194304 | tf_op jit(solution)/shard_map/all_to_all | solution.py:185
  195.7 53.1 %all-to-all-start = ((bf16[32,8,16,256]{3,2,1,0:T(8,128)(2,1)}), bf16[32,8,16,256]{3,2,1,0:T(8,128)(2,1)S(1)}, u32[]{:S(2)}, u32[]{:S(2)}) async-start(bf16[32,8,16,256]{3,2,1,0:T(8,128)(2,1)} %shard_map.82), calls=%async_computation | async-start | bytes 4194304 | tf_op jit(solution)/shard_map/all_to_all | solution.py:185
  248.8 1.3 copy-start.1

commit v2 on v1

v2 whole, which is shorter than its diff:
```python
import functools

import jax
import jax.numpy as jnp
import ml_dtypes
import numpy as np
from jax import lax
from jax.experimental import pallas as pl
from jax.experimental.pallas import tpu as pltpu
from jax.sharding import PartitionSpec as P

VMEM_BYTES = 56 * 1024 * 1024
PAD = 8
LANES = 128


def cosine_table(size):
    freq = np.arange(size, dtype=np.float64)[:, None]
    place = np.arange(size, dtype=np.float64)[None, :]
    waves = np.cos(np.pi * (2.0 * place + 1.0) * freq / (2.0 * size))
    scales = np.where(freq == 0.0, np.sqrt(1.0 / size), np.sqrt(2.0 / size))
    return (scales * waves).astype(ml_dtypes.bfloat16)


def weight_of(counts):
    values = counts.astype(jnp.float32)
    return values / (values + 4.0)


def strip_rows(rows):
    return 32 if rows % 32 == 0 else 8


def partner(index, step):
    return index ^ step


def device():
    return lax.axis_index("wide") * lax.axis_size("narrow") + lax.axis_index("narrow")


def planes_kernel(start, planes, total, block, sizes, normals, counts, low_y, high_y, low, high, low_counts,
                  high_counts, table, *rest):
    *outs, flux_y, last_x, partial, divergence, ordered = rest
    step = pl.program_id(0)
    steps = planes // block
    rows, depth = last_x.shape
    strip = strip_rows(rows)
    strips = [slice(r, r + strip) for r in range(0, rows, strip)]
    columns = [slice(c, c + LANES) for c in range(0, depth, LANES)]
    now = lax.rem(step, 2)
    before = 1 - now

    @pl.when(step == 0)
    def _():
        if sizes is None:
            ordered[...] = table[...]
        else:
            far, near = sizes
            slab = depth // (far * near)
            for place in range(near):
                for turn in range(far):
                    owner = partner(device() // near, turn) * near + partner(device() % near, place)
                    into = (place * far + turn) * slab
                    ordered[into:into + slab, :] = table[pl.ds(pl.multiple_of(owner * slab, slab), slab), :]
        for at in strips:
            if start == 0:
                last_x[at, :] = low[at, :].astype(jnp.float32)
            else:
                last_x[at, :] = weight_of(low_counts[0, at, :]) * low[0, 0, at, :].astype(jnp.float32)

    def transform(plane):
        along = lax.dot_general(
            ordered[...], divergence[plane], (((1,), (1,)), ((), ())), preferred_element_type=jnp.float32
        ).astype(jnp.bfloat16)
        share = depth // len(outs)
        for at, out in enumerate(outs):
            out[:, plane] = along[at * share:(at + 1) * share].reshape(out.shape[0], out.shape[2], rows)

    def diff_y(slot, plane, tile, at):
        after_y = flux_y[slot, plane, tile, PAD + at.start + 1:PAD + at.stop + 1, :]
        return after_y - flux_y[slot, plane, tile, PAD + at.start - 1:PAD + at.stop - 1, :]

    lane = lax.broadcasted_iota(jnp.int32, (strip, LANES), 1)
    first, last = lane == 0, lane == LANES - 1

    def take_in(at):
        ahead = []
        for plane in range(block):
            flux_x, before_z, after_z = [], [], []
            for tile, cut in enumerate(columns):
                weight = weight_of(counts[plane, at, cut])
                flux_x.append(weight * normals[0, plane, at, cut].astype(jnp.float32))
                flux_y[now, plane, tile, PAD + at.start:PAD + at.stop, :] = (
                    weight * normals[1, plane, at, cut].astype(jnp.float32)
                )
                flux_z = weight * normals[2, plane, at, cut].astype(jnp.float32)
                before_z.append(pltpu.roll(flux_z, 1, 1))
                after_z.append(pltpu.roll(flux_z, LANES - 1, 1))
            for tile, cut in enumerate(columns):
                left = before_z[tile - 1] if tile > 0 else 0.0
                right = after_z[tile + 1] if tile + 1 < len(columns) else 0.0
                diff_z = jnp.where(last, right, after_z[tile]) - jnp.where(first, left, before_z[tile])
                if plane == 0:
                    partial[block, at, cut] = partial[block - 1, at, cut] + flux_x[tile]
                    partial[0, at, cut] = diff_z - last_x[at, cut]
                else:
                    partial[plane - 1, at, cut] = partial[plane - 1, at, cut] + flux_x[tile]
                    partial[plane, at, cut] = diff_z - ahead[tile]
                if plane == block - 1:
                    last_x[at, cut] = flux_x[tile]
            ahead = flux_x

    def put_out(at):
        for tile, cut in enumerate(columns):
            done = partial[block, at, cut] + diff_y(before, block - 1, tile, at)
            divergence[block - 1, at, cut] = done.astype(jnp.bfloat16)
            for plane in range(block - 1):
                done = partial[plane, at, cut] + diff_y(now, plane, tile, at)
                divergence[plane, at, cut] = done.astype(jnp.bfloat16)

    @pl.when(step < steps)
    def _():
        for plane in range(block - 1):
            transform(plane)
        for plane in range(block):
            low_line = low_y[pl.ds(start + step * block + plane, 1), :]
            high_line = high_y[pl.ds(start + step * block + plane, 1), :]
            for tile, cut in enumerate(columns):
                flux_y[now, plane, tile, PAD - 1:PAD, :] = low_line[:, cut]
                flux_y[now, plane, tile, PAD + rows:PAD + rows + 1, :] = high_line[:, cut]
        for number, at in enumerate(strips):
            take_in(at)
            if number:
                put_out(strips[number - 1])
        put_out(strips[-1])
        transform(block - 1)

    @pl.when(step == steps)
    def _():
        for plane in range(block - 1):
            transform(plane)
        for at in strips:
            for tile, cut in enumerate(columns):
                if start + planes == total:
                    flux_x = high[at, cut].astype(jnp.float32)
                else:
                    flux_x = weight_of(high_counts[0, at, cut]) * high[0, 0, at, cut].astype(jnp.float32)
                done = flux_x + (partial[block - 1, at, cut] + diff_y(before, block - 1, tile, at))
                divergence[block - 1, at, cut] = done.astype(jnp.bfloat16)
        transform(block - 1)


def along_z_of(normals, counts, halos, table, start, planes, count=1, groups=1, sizes=None):
    _, total, rows, depth = normals.shape
    low_y, high_y, low_x, high_x = halos
    block = 4 if planes % 4 == 0 else 1
    steps = planes // block

    def block_at(step):
        return start // block + jnp.minimum(step, steps - 1)

    def edge(plane):
        return pl.BlockSpec((1, 1, rows, depth), lambda step: (0, plane, 0, 0))

    def edge_counts(plane):
        return pl.BlockSpec((1, rows, depth), lambda step: (plane, 0, 0))

    whole = pl.BlockSpec((rows, depth), lambda step: (0, 0))
    lines = pl.BlockSpec((total, depth), lambda step: (0, 0))
    at_low, at_high = start == 0, start + planes == total
    below, above = max(start - 1, 0), min(start + planes, total - 1)
    size = planes * rows * depth
    share = depth // (groups * count)
    return pl.pallas_call(
        functools.partial(planes_kernel, start, planes, total, block, sizes),
        grid=(steps + 1,),
        in_specs=[
            pl.BlockSpec((3, block, rows, depth), lambda step: (0, block_at(step), 0, 0)),
            pl.BlockSpec((block, rows, depth), lambda step: (block_at(step), 0, 0)),
            lines,
            lines,
            whole if at_low else edge(below),
            whole if at_high else edge(above),
            edge_counts(below),
            edge_counts(above),
            pl.BlockSpec((depth, depth), lambda step: (0, 0)),
        ],
        out_specs=[
            pl.BlockSpec((groups, block, share, rows), lambda step: (0, jnp.maximum(step - 1, 0), 0, 0))
        ] * count,
        out_shape=[jax.ShapeDtypeStruct((groups, planes, share, rows), jnp.bfloat16)] * count,
        scratch_shapes=[
            pltpu.VMEM((2, block, depth // LANES, rows + 2 * PAD, LANES), jnp.float32),
            pltpu.VMEM((rows, depth), jnp.float32),
            pltpu.VMEM((block + 1, rows, depth), jnp.float32),
            pltpu.VMEM((block, rows, depth), jnp.bfloat16),
            pltpu.VMEM((depth, depth), jnp.bfloat16),
        ],
        compiler_params=pltpu.CompilerParams(vmem_limit_bytes=VMEM_BYTES),
        cost_estimate=pl.CostEstimate(flops=2 * size * depth, bytes_accessed=12 * size, transcendentals=size),
    )(normals, counts, low_y, high_y, low_x if at_low else normals, high_x if at_high else normals, counts, counts, table)


def order_of(planes, slab):
    order = np.zeros((slab, planes, planes, slab), np.float32)
    for k in range(slab):
        for i in range(planes):
            order[k, i, i, k] = 1.0
    return jnp.asarray(order.reshape(planes * slab, planes * slab).astype(ml_dtypes.bfloat16))


def y_of(groups, table, order):
    planes, slab, rows = groups[0][0].shape
    count = planes * slab
    lines = [
        jnp.concatenate([tile[...].reshape(count, rows) for tile in tiles], axis=1) for tiles in groups
    ]
    along = jnp.dot(jnp.concatenate(lines, axis=0), table[...], preferred_element_type=jnp.float32)
    along = along.astype(jnp.bfloat16)
    moved = []
    for at in range(len(groups)):
        part = jnp.dot(order[...], along[at * count:(at + 1) * count], preferred_element_type=jnp.float32)
        moved.append(part.astype(jnp.bfloat16).reshape(slab, planes, table.shape[1]))
    return moved


def near_kernel(near, narrow, *refs):
    tiles, (table, order), (*outs, ordered) = refs[:near], refs[near:near + 2], refs[near + 2:]
    planes, _, rows = tiles[0].shape

    @pl.when(pl.program_id(0) == 0)
    def _():
        for place in range(narrow):
            owner = partner(device() % narrow, place)
            ordered[place * rows:(place + 1) * rows, :] = table[pl.ds(pl.multiple_of(owner * rows, rows), rows), :]

    moved = y_of([tiles[at:at + narrow] for at in range(0, near, narrow)], ordered, order)
    for step, out in enumerate(outs):

        @pl.when(pl.program_id(0) == step)
        def _():
            for core, part in enumerate(moved):
                out[:, core * planes:(core + 1) * planes, :] = part


def far_kernel(narrow, tiles, table, order, out):
    groups = [[tiles.at[at + place] for place in range(narrow)] for at in range(0, tiles.shape[0], narrow)]
    for at, moved in enumerate(y_of(groups, table, order)):
        out[:, at, :moved.shape[1]] = moved


def y_cost(planes, slab, wide, full_y):
    size = planes * slab * wide * full_y
    return pl.CostEstimate(flops=2 * size * (full_y + planes * slab), bytes_accessed=4 * size, transcendentals=0)


def along_y_near(tiles, table, far, narrow):
    planes, share, rows = tiles[0].shape
    near = len(tiles)
    slab = share // far
    full_y = table.shape[1]
    count = planes * slab
    cores = near // narrow
    return pl.pallas_call(
        functools.partial(near_kernel, near, narrow),
        grid=(far,),
        in_specs=[pl.BlockSpec((planes, slab, rows), lambda step: (0, step, 0))] * near + [
            pl.BlockSpec(table.shape, lambda step: (0, 0)),
            pl.BlockSpec((count, count), lambda step: (0, 0)),
        ],
        out_specs=[pl.BlockSpec((slab, cores * planes, full_y), lambda step: (0, 0, 0))] * far,
        out_shape=[jax.ShapeDtypeStruct((slab, cores * planes, full_y), jnp.bfloat16)] * far,
        scratch_shapes=[pltpu.VMEM(table.shape, jnp.bfloat16)],
        compiler_params=pltpu.CompilerParams(vmem_limit_bytes=VMEM_BYTES),
        cost_estimate=y_cost(planes, slab, far * cores, full_y),
    )(*tiles, table, order_of(planes, slab))


def along_y_far(tiles, table, total, narrow):
    count, planes, slab, rows = tiles.shape
    wide = count // narrow
    full_y = table.shape[1]
    return pl.pallas_call(
        functools.partial(far_kernel, narrow),
        grid=(wide // 2,),
        in_specs=[
            pl.BlockSpec((2 * narrow, planes, slab, rows), lambda at: (at, 0, 0, 0)),
            pl.BlockSpec(table.shape, lambda at: (0, 0)),
            pl.BlockSpec((planes * slab, planes * slab), lambda at: (0, 0)),
        ],
        out_specs=pl.BlockSpec((slab, 2, total, full_y), lambda at: (0, at, 0, 0)),
        out_shape=jax.ShapeDtypeStruct((slab, wide, total, full_y), jnp.bfloat16),
        compiler_params=pltpu.CompilerParams(vmem_limit_bytes=VMEM_BYTES),
        cost_estimate=y_cost(planes, slab, wide, full_y),
    )(tiles, table, order_of(planes, slab)).reshape(slab, wide * total, full_y)


def after(array, *others):
    return lax.optimization_barrier((array, *others))[0]


def swap_far(array, step, near):
    if step == 0:
        return array
    count = lax.axis_size("wide") * lax.axis_size("narrow")
    pairs = [(i, partner(i // near, step) * near + i % near) for i in range(count)]
    return lax.ppermute(array, ("wide", "narrow"), pairs)


def swap_near(array, step, near):
    if step == 0:
        return array
    count = lax.axis_size("wide") * lax.axis_size("narrow")
    pairs = [(i, i // near * near + partner(i % near, step)) for i in range(count)]
    return lax.ppermute(array, ("wide", "narrow"), pairs)


def halos_of(normals, counts):
    wide = lax.axis_size("wide")
    narrow = lax.axis_size("narrow")
    up = lambda count: [(i, i + 1) for i in range(count - 1)]
    down = lambda count: [(i + 1, i) for i in range(count - 1)]
    edge_y = lambda at: weight_of(counts[:, at, :]) * normals[1, :, at, :].astype(jnp.float32)
    edge_x = lambda at: (weight_of(counts[at]) * normals[0, at].astype(jnp.float32)).astype(jnp.bfloat16)
    low_y = lax.ppermute(edge_y(counts.shape[1] - 1), "narrow", up(narrow))
    high_y = lax.ppermute(edge_y(0), "narrow", down(narrow))
    low_x = lax.ppermute(edge_x(counts.shape[0] - 1), "wide", up(wide))
    high_x = lax.ppermute(edge_x(0), "wide", down(wide))
    return low_y, high_y, low_x, high_x


def per_device(normals, counts):
    wide = lax.axis_size("wide")
    narrow = lax.axis_size("narrow")
    _, total, rows, depth = normals.shape
    full_y = narrow * rows
    slab = depth // (wide * narrow)
    halos = halos_of(normals, counts)
    table_z = jnp.asarray(cosine_table(depth) * ml_dtypes.bfloat16(0.5))
    table_y = jnp.asarray(np.ascontiguousarray(cosine_table(full_y).T))
    cores = 2
    far = wide // cores
    near = cores * narrow
    if slab % 16 == 0 and total % 32 == 0 and wide == cores * far and far & (far - 1) == 0 and near & (near - 1) == 0:
        most = total * 3 // 4
        rest = total - most
        pieces = along_z_of(normals, counts, halos, after(table_z, halos[3]), 0, most, 1, wide * narrow)[0]
        later = after(table_z, pieces)
        pieces = lax.all_to_all(pieces, ("wide", "narrow"), split_axis=0, concat_axis=0, tiled=True)
        tiles = along_z_of(normals, counts, halos, later, most, rest, near, 1, (far, near))
        tiles = [swap_near(tile[0], step, near) for step, tile in enumerate(tiles)]
        far_pieces = along_y_near(tiles, table_y, far, narrow)
        pieces = after(pieces, far_pieces[0])
        far_pieces = [swap_far(piece, step, near) for step, piece in enumerate(far_pieces)]
        spectrum = along_y_far(pieces, table_y, total, narrow)
        mine = device() // near
        for step, piece in enumerate(far_pieces):
            for turn in range(cores):
                core = partner(device() % near // narrow, turn)
                at = (partner(mine, step) * cores + core) * total + most
                spectrum = lax.dynamic_update_slice(spectrum, piece[:, turn * rest:(turn + 1) * rest], (0, at, 0))
        return spectrum
    along = along_z_of(normals, counts, halos, table_z, 0, total)[0]
    along = along.reshape(total, wide * narrow, slab, rows)
    arrived = lax.all_to_all(along, ("wide", "narrow"), split_axis=1, concat_axis=1, tiled=True)
    arrived = arrived.reshape(total, wide, narrow, slab, rows)
    pencil = jnp.transpose(arrived, (3, 1, 0, 2, 4)).reshape(slab * wide * total, full_y)
    spectrum = jnp.dot(pencil, table_y, preferred_element_type=jnp.float32).astype(jnp.bfloat16)
    return spectrum.reshape(slab, wide * total, full_y)


def solution(mesh):
    placed = (P(None, "wide", "narrow", None), P("wide", "narrow", None))
    return jax.shard_map(
        per_device,
        mesh=mesh,
        in_specs=placed,
        out_specs=P(("wide", "narrow"), None, None),
        check_vma=False,
    )
```

time: 263 us -> 234 us (0.89)
  Pallas kernels: 87.3 us -> 50.2 us
  waiting for transfers between devices: 133 us -> 138 us
  local copies, waits for them, and re-layouts: 6.57 us -> 10.4 us
    ppermute x4 -> x14, waiting for transfers between devices: 4.85 us -> 77.3 us  [the longest x7 65.3 us: swap_near(): return lax.ppermute(array, ('wide', 'narrow'), pairs)]
    all_to_all x4 -> x1, waiting for transfers between devices: 128 us -> 60.9 us  [per_device(): lax.all_to_all(pieces, ('wide', 'narrow'), split_axis=0, concat_axis=0, t...]
    pallas_call x8 -> x4, Pallas kernels: 87.3 us -> 50.2 us  [the longest x2 28.6 us: along_z_of(): pl.pallas_call(functools.partial(planes_kernel, start, planes, total, blo...]
    ppermute x4 -> x14, starting transfers between devices: 10.3 us -> 26 us  [the longest x3 11.2 us: swap_far(): return lax.ppermute(array, ('wide', 'narrow'), pairs)]
    all_to_all x4 -> x1, starting transfers between devices: 19.9 us -> 5.57 us  [per_device(): lax.all_to_all(pieces, ('wide', 'narrow'), split_axis=0, concat_axis=0, t...]
    dynamic_update_slice x0 -> x8, local copies, waits for them, and re-layouts: none -> 5.78 us  [per_device(): lax.dynamic_update_slice(spectrum, piece[:, turn * rest:(turn + 1) * rest...]
  transfers between devices with their start and end apart: 8 -> 15, of which waited for: 5 -> 8; matrix products, arithmetic and copies ran while one was open for 1% -> 3% of each run, Pallas kernels for 25% -> 13%
where the time goes in v2:
time: 234 us; the launch traced here: 232 us
  waiting for transfers between devices  138 us (59%)
  Pallas kernels  50.2 us (21%)
  starting transfers between devices  31.5 us (13%)
  local copies, waits for them, and re-layouts  10.4 us (4%)
    ppermute x7, waiting for transfers between devices, swap_near(): return lax.ppermute(array, ('wide', 'narrow'), pairs)  65.3 us
    all_to_all x1, waiting for transfers between devices, per_device(): lax.all_to_all(pieces, ('wide', 'narrow'), split_axis=0, concat_axis=0, t...  60.9 us
    pallas_call x2, Pallas kernels, along_z_of(): pl.pallas_call(functools.partial(planes_kernel, start, planes, total, blo...  28.6 us
    pallas_call x1, Pallas kernels, along_y_far(): pl.pallas_call(functools.partial(far_kernel, narrow), grid=(wide // 2,),...  14 us
    ppermute x3, starting transfers between devices, swap_far(): return lax.ppermute(array, ('wide', 'narrow'), pairs)  11.2 us
    pallas_call x1, Pallas kernels, along_y_near(): pl.pallas_call(functools.partial(near_kernel, near, narrow), grid=(far,),...  7.5 us
    ppermute x3, waiting for transfers between devices, swap_far(): return lax.ppermute(array, ('wide', 'narrow'), pairs)  6.65 us
    dynamic_update_slice x8, local copies, waits for them, and re-layouts, per_device(): lax.dynamic_update_slice(spectrum, piece[:, turn * rest:(turn + 1) * rest...  5.78 us
  transfers between devices with their start and end apart: 15, of which 8 were waited for; matrix products, arithmetic and copies ran while one was open for 3% of the time, Pallas kernels for 13%

profile of v2, /device:TPU:8, one launch (start us, length us, event | category | flops | bytes accessed | tf_op | source)
XLA Modules:
  0.0 232.0 jit_solution(16051126844706929574)
XLA Ops:
  0.0 1.1 fusion.8
  1.1 1.3 fusion.9
  2.5 3.4 %collective-permute-start = (f32[32,512]{1,0:T(8,128)S(1)}, f32[32,512]{1,0:T(8,128)S(1)}, u32[]{:S(2)}, u32[]{:S(2)}) collective-permute-start(f32[32,512]{1,0:T(8,128)S(1)} %fusion.4), channel_id=1, source_target_pairs={{0,1},{1,2},{2,3},{4,5},{5,6},{6,7},{8,9},{9,10},{10,11},{12,13},{... | collective-permute-start | bytes 196616 | tf_op jit(solution)/shard_map/ppermute | solution.py:326
  5.9 1.6 fusion.3
  7.5 1.9 collective-permute-start.3
  9.4 2.4 %collective-permute-start.2 = (bf16[256,512]{1,0:T(8,128)(2,1)S(1)}, bf16[256,512]{1,0:T(8,128)(2,1)S(1)}, u32[]{:S(2)}, u32[]{:S(2)}) collective-permute-start(bf16[256,512]{1,0:T(8,128)(2,1)S(1)} %get-tuple-element.36), channel_id=1, source_target_pairs={{0,4},{4,8},{8,12},{12,16},{16,20},{20,24},{24,28},{1,5},{5,9},{9,... | collective-permute-start | bytes 786440 | tf_op jit(solution)/shard_map/ppermute | solution.py:328
  11.9 1.3 collective-permute-start.1
  13.3 5.2 %collective-permute-done.1.high_y = f32[32,512]{1,0:T(8,128)S(1)} collective-permute-done((f32[32,512]{1,0:T(8,128)S(1)}, f32[32,512]{1,0:T(8,128)S(1)}, u32[]{:S(2)}, u32[]{:S(2)}) %collective-permute-start.1) | collective-permute-done | bytes 65568 | tf_op jit(solution)/shard_map/ppermute | solution.py:327
  19.8 19.8 %shard_map.64 = bf16[32,24,16,256]{3,2,1,0:T(8,128)(2,1)} custom-call(bf16[3,32,256,512]{3,2,1,0:T(8,128)(2,1)} %low.1, s32[32,256,512]{2,1,0:T(8,128)} %high_counts.3, f32[32,512]{1,0:T(8,128)} %copy-done.3, f32[32,512]{1,0:T(8,128)} %copy-done.4, bf16[256,512]{1,0:T(8,128)(2,1)} %copy-done.2, bf16[3,32,256,512]{3,2,1,0:T(8,128)(2,1)} %low.1, ...), custom_call_target="tpu_custom_call" | custom-call | flops 3221225472 | bytes 37748736 | tf_op jit(solution)/shard_map/pallas_call | solution.py:175
  39.6 5.6 %all-to-all-start = ((bf16[32,24,16,256]{3,2,1,0:T(8,128)(2,1)}), bf16[32,24,16,256]{3,2,1,0:T(8,128)(2,1)}, u32[]{:S(2)}, u32[]{:S(2)}) async-start(bf16[32,24,16,256]{3,2,1,0:T(8,128)(2,1)} %shard_map.64), calls=%async_computation | async-start | bytes 12582912 | tf_op jit(solution)/shard_map/all_to_all | solution.py:350
  45.2 8.9 %shard_map.65 = (bf16[1,8,64,256]{3,2,1,0:T(8,128)(2,1)}, bf16[1,8,64,256]{3,2,1,0:T(8,128)(2,1)}, bf16[1,8,64,256]{3,2,1,0:T(8,128)(2,1)}, bf16[1,8,64,256]{3,2...) custom-call(bf16[3,32,256,512]{3,2,1,0:T(8,128)(2,1)} %low.1, ...), custom_call_target="tpu_custom_call" | custom-call | flops 1073741824 | bytes 12582912 | tf_op jit(solution)/shard_map/pallas_call | solution.py:175
  54.0 2.2 collective-permute-start.10
  57.4 2.4 %collective-permute-start.6 = (bf16[8,64,256]{2,1,0:T(8,128)(2,1)}, bf16[8,64,256]{2,1,0:T(8,128)(2,1)S(1)}, u32[]{:S(2)}, u32[]{:S(2)}) collective-permute-start(bf16[8,64,256]{2,1,0:T(8,128)(2,1)} %bitcast.42), channel_id=1, source_target_pairs={{0,3},{1,2},{2,1},{3,0},{4,7},{5,6},{6,5},{7,4},{8,11},{9,10},{10,... | collective-permute-start | bytes 786440 | tf_op jit(solution)/shard_map/ppermute | solution.py:316
  59.7 36.0 %collective-permute-done.10.refs_7_ = bf16[8,64,256]{2,1,0:T(8,128)(2,1)S(1)} collective-permute-done((bf16[8,64,256]{2,1,0:T(8,128)(2,1)}, bf16[8,64,256]{2,1,0:T(8,128)(2,1)S(1)}, u32[]{:S(2)}, u32[]{:S(2)}) %collective-permute-start.10) | collective-permute-done | bytes 262176 | tf_op jit(solution)/shard_map/ppermute | solution.py:316
  95.8 9.7 %collective-permute-done.4.refs_1_ = bf16[8,64,256]{2,1,0:T(8,128)(2,1)S(1)} collective-permute-done((bf16[8,64,256]{2,1,0:T(8,128)(2,1)}, bf16[8,64,256]{2,1,0:T(8,128)(2,1)S(1)}, u32[]{:S(2)}, u32[]{:S(2)}) %collective-permute-start.4) | collective-permute-done | bytes 262176 | tf_op jit(solution)/shard_map/ppermute | solution.py:316
  105.5 10.0 %collective-permute-done.6.refs_3_ = bf16[8,64,256]{2,1,0:T(8,128)(2,1)S(1)} collective-permute-done((bf16[8,64,256]{2,1,0:T(8,128)(2,1)}, bf16[8,64,256]{2,1,0:T(8,128)(2,1)S(1)}, u32[]{:S(2)}, u32[]{:S(2)}) %collective-permute-start.6) | collective-permute-done | bytes 262176 | tf_op jit(solution)/shard_map/ppermute | solution.py:316
  115.5 9.6 %collective-permute-done.8.refs_5_ = bf16[8,64,256]{2,1,0:T(8,128)(2,1)S(1)} collective-permute-done((bf16[8,64,256]{2,1,0:T(8,128)(2,1)}, bf16[8,64,256]{2,1,0:T(8,128)(2,1)S(1)}, u32[]{:S(2)}, u32[]{:S(2)}) %collective-permute-start.8) | collective-permute-done | bytes 262176 | tf_op jit(solution)/shard_map/ppermute | solution.py:316
  125.9 7.5 %shard_map.66 = (bf16[16,16,1024]{2,1,0:T(8,128)(2,1)}, bf16[16,16,1024]{2,1,0:T(8,128)(2,1)}, bf16[16,16,1024]{2,1,0:T(8,128)(2,1)}, bf16[16,16,1024]{2,1,0:T(8,128)(2,1)}) custom-call(bf16[8,64,256]{2,1,0:T(8,128)(2,1)} %bitcast.38, bf16[8,64,256]{2,1,0:T(8,128)(2,1)} %copy-done.6, bf16[8,64,256]{2,1,0:T(8,128)(2,1)} %copy-done.7, ...), custom_call_target="tpu_custom_call" | custom-call | flops 2415919104 | bytes 4194304 | tf_op jit(solution)/shard_map/pallas_call | solution.py:265
  133.4 9.7 %collective-permute-start.11 = (bf16[16,16,1024]{2,1,0:T(8,128)(2,1)}, bf16[16,16,1024]{2,1,0:T(8,128)(2,1)S(1)}, u32[]{:S(2)}, u32[]{:S(2)}) collective-permute-start(bf16[16,16,1024]{2,1,0:T(8,128)(2,1)} %get-tuple-element.32), channel_id=1, source_target_pairs={{0,8},{1,9},{2,10},{3,11},{4,12},{5,13},{6,14},{7,15},{8,0},{9,1},... | collective-permute-start | bytes 1572872 | tf_op jit(solution)/shard_map/ppermute | solution.py:308
  143.1 0.8 collective-permute-start.12
  144.7 60.9 %all-to-all-done.tiles = bf16[32,24,16,256]{3,2,1,0:T(8,128)(2,1)} async-done(((bf16[32,24,16,256]{3,2,1,0:T(8,128)(2,1)}), bf16[32,24,16,256]{3,2,1,0:T(8,128)(2,1)}, u32[]{:S(2)}, u32[]{:S(2)}) %all-to-all-start) | async-done | bytes 6291488 | tf_op jit(solution)/shard_map/all_to_all | solution.py:350
  205.5 14.0 %shard_map.67 = bf16[16,8,32,1024]{3,2,1,0:T(8,128)(2,1)} custom-call(bf16[32,24,16,256]{3,2,1,0:T(8,128)(2,1)} %all-to-all-done.tiles, bf16[1024,1024]{1,0:T(8,128)(2,1)} %constant.104.clone.refs_8_.table, bf16[384,384]{1,0:T(8,128)(2,1)} %constant.106.clone.order), custom_call_target="tpu_custom_call" | custom-call | flops 8858370048 | bytes 12582912 | tf_op jit(solution)/shard_map/pallas_call | solution.py:284
  219.5 0.7 slice_dynamic-update-slice_fusion.7
  223.9 6.6 %collective-permute-done.13 = bf16[16,16,1024]{2,1,0:T(8,128)(2,1)S(1)} collective-permute-done((bf16[16,16,1024]{2,1,0:T(8,128)(2,1)}, bf16[16,16,1024]{2,1,0:T(8,128)(2,1)S(1)}, u32[]{:S(2)}, u32[]{:S(2)}) %collective-permute-start.13) | collective-permute-done | bytes 524320 | tf_op jit(solution)/shard_map/ppermute | solution.py:308
  (47 shorter events, 9.2 us)
Async XLA Ops:
  2.5 10.8 %collective-permute-start = (f32[32,512]{1,0:T(8,128)S(1)}, f32[32,512]{1,0:T(8,128)S(1)}, u32[]{:S(2)}, u32[]{:S(2)}) collective-permute-start(f32[32,512]{1,0:T(8,128)S(1)} %fusion.4), channel_id=1, source_target_pairs={{0,1},{1,2},{2,3},{4,5},{5,6},{6,7},{8,9},{9,10},{10,11},{12,13},{... | collective-permute-start | bytes 196616 | tf_op jit(solution)/shard_map/ppermute | solution.py:326
  7.5 5.8 %collective-permute-start.3 = (bf16[256,512]{1,0:T(8,128)(2,1)S(1)}, bf16[256,512]{1,0:T(8,128)(2,1)S(1)}, u32[]{:S(2)}, u32[]{:S(2)}) collective-permute-start(bf16[256,512]{1,0:T(8,128)(2,1)S(1)} %get-tuple-element.35), channel_id=1, source_target_pairs={{4,0},{8,4},{12,8},{16,12},{20,16},{24,20},{28,24},{5,1},{9,5},{13... | collective-permute-start | bytes 786440 | tf_op jit(solution)/shard_map/ppermute | solution.py:329
  9.4 9.1 %collective-permute-start.2 = (bf16[256,512]{1,0:T(8,128)(2,1)S(1)}, bf16[256,512]{1,0:T(8,128)(2,1)S(1)}, u32[]{:S(2)}, u32[]{:S(2)}) collective-permute-start(bf16[256,512]{1,0:T(8,128)(2,1)S(1)} %get-tuple-element.36), channel_id=1, source_target_pairs={{0,4},{4,8},{8,12},{12,16},{16,20},{20,24},{24,28},{1,5},{5,9},{9,... | collective-permute-start | bytes 786440 | tf_op jit(solution)/shard_map/ppermute | solution.py:328
  11.9 6.6 %collective-permute-start.1 = (f32[32,512]{1,0:T(8,128)S(1)}, f32[32,512]{1,0:T(8,128)S(1)}, u32[]{:S(2)}, u32[]{:S(2)}) collective-permute-start(f32[32,512]{1,0:T(8,128)S(1)} %fusion.5), channel_id=1, source_target_pairs={{1,0},{2,1},{3,2},{5,4},{6,5},{7,6},{9,8},{10,9},{11,10},{13,12},{... | collective-permute-start | bytes 196616 | tf_op jit(solution)/shard_map/ppermute | solution.py:327
  13.3 26.3 %copy-start.1 = (bf16[256,512]{1,0:T(8,128)(2,1)}, bf16[256,512]{1,0:T(8,128)(2,1)S(1)}, u32[]{:S(2)}) copy-start(bf16[256,512]{1,0:T(8,128)(2,1)S(1)} %collective-permute-done.3.high) | copy-start | bytes 786436
  13.3 5.2 %copy-start.3 = (f32[32,512]{1,0:T(8,128)}, f32[32,512]{1,0:T(8,128)S(1)}, u32[]{:S(2)}) copy-start(f32[32,512]{1,0:T(8,128)S(1)} %collective-permute-done.low_y) | copy-start | bytes 196612
  39.6 165.9 %all-to-all-start = ((bf16[32,24,16,256]{3,2,1,0:T(8,128)(2,1)}), bf16[32,24,16,256]{3,2,1,0:T(8,128)(2,1)}, u32[]{:S(2)}, u32[]{:S(2)}) async-start(bf16[32,24,16,256]{3,2,1,0:T(8,128)(2,1)} %shard_map.64), calls=%async_computation | async-start | bytes 12582912 | tf_op jit(solution)/shard_map/all_to_all | solution.py:350
  54.0 41.7 %collective-permute-start.10 = (bf16[8,64,256]{2,1,0:T(8,128)(2,1)}, bf16[8,64,256]{2,1,0:T(8,128)(2,1)S(1)}, u32[]{:S(2)}, u32[]{:S(2)}) collective-permute-start(bf16[8,64,256]{2,1,0:T(8,128)(2,1)} %bitcast.45), channel_id=1, source_target_pairs={{0,7},{1,6},{2,5},{3,4},{4,3},{5,2},{6,1},{7,0},{8,15},{9,14},{10,... | collective-permute-start | bytes 786440 | tf_op jit(solution)/shard_map/ppermute | solution.py:316
  56.2 49.2 %collective-permute-start.4 = (bf16[8,64,256]{2,1,0:T(8,128)(2,1)}, bf16[8,64,256]{2,1,0:T(8,128)(2,1)S(1)}, u32[]{:S(2)}, u32[]{:S(2)}) collective-permute-start(bf16[8,64,256]{2,1,0:T(8,128)(2,1)} %bitcast.44), channel_id=1, source_target_pairs={{0,1},{1,0},{2,3},{3,2},{4,5},{5,4},{6,7},{7,6},{8,9},{9,8},{10,11... | collective-permute-start | bytes 786440 | tf_op jit(solution)/shard_map/ppermute | solution.py:316
  56.8 48.7 %collective-permute-start.5 = (bf16[8,64,256]{2,1,0:T(8,128)(2,1)}, bf16[8,64,256]{2,1,0:T(8,128)(2,1)S(1)}, u32[]{:S(2)}, u32[]{:S(2)}) collective-permute-start(bf16[8,64,256]{2,1,0:T(8,128)(2,1)} %bitcast.43), channel_id=1, source_target_pairs={{0,2},{1,3},{2,0},{3,1},{4,6},{5,7},{6,4},{7,5},{8,10},{9,11},{10,... | collective-permute-start | bytes 786440 | tf_op jit(solution)/shard_map/ppermute | solution.py:316
  57.4 58.1 %collective-permute-start.6 = (bf16[8,64,256]{2,1,0:T(8,128)(2,1)}, bf16[8,64,256]{2,1,0:T(8,128)(2,1)S(1)}, u32[]{:S(2)}, u32[]{:S(2)}) collective-permute-start(bf16[8,64,256]{2,1,0:T(8,128)(2,1)} %bitcast.42), channel_id=1, source_target_pairs={{0,3},{1,2},{2,1},{3,0},{4,7},{5,6},{6,5},{7,4},{8,11},{9,10},{10,... | collective-permute-start | bytes 786440 | tf_op jit(solution)/shard_map/ppermute | solution.py:316
  59.7 55.7 %collective-permute-start.7 = (bf16[8,64,256]{2,1,0:T(8,128)(2,1)}, bf16[8,64,256]{2,1,0:T(8,128)(2,1)S(1)}, u32[]{:S(2)}, u32[]{:S(2)}) collective-permute-start(bf16[8,64,256]{2,1,0:T(8,128)(2,1)} %bitcast.41), channel_id=1, source_target_pairs={{0,4},{1,5},{2,6},{3,7},{4,0},{5,1},{6,2},{7,3},{8,12},{9,13},{10,... | collective-permute-start | bytes 786440 | tf_op jit(solution)/shard_map/ppermute | solution.py:316
  95.8 29.3 %copy-start.5 = (bf16[8,64,256]{2,1,0:T(8,128)(2,1)}, bf16[8,64,256]{2,1,0:T(8,128)(2,1)S(1)}, u32[]{:S(2)}) copy-start(bf16[8,64,256]{2,1,0:T(8,128)(2,1)S(1)} %collective-permute-done.10.refs_7_) | copy-start | bytes 786436
  95.8 29.3 %collective-permute-start.8 = (bf16[8,64,256]{2,1,0:T(8,128)(2,1)}, bf16[8,64,256]{2,1,0:T(8,128)(2,1)S(1)}, u32[]{:S(2)}, u32[]{:S(2)}) collective-permute-start(bf16[8,64,256]{2,1,0:T(8,128)(2,1)} %bitcast.40), channel_id=1, source_target_pairs={{0,5},{1,4},{2,7},{3,6},{4,1},{5,0},{6,3},{7,2},{8,13},{9,12},{10,... | collective-permute-start | bytes 786440 | tf_op jit(solution)/shard_map/ppermute | solution.py:316
  105.4 19.6 %copy-start.6 = (bf16[8,64,256]{2,1,0:T(8,128)(2,1)}, bf16[8,64,256]{2,1,0:T(8,128)(2,1)S(1)}, u32[]{:S(2)}) copy-start(bf16[8,64,256]{2,1,0:T(8,128)(2,1)S(1)} %collective-permute-done.4.refs_1_) | copy-start | bytes 786436
  105.4 19.6 %collective-permute-start.9 = (bf16[8,64,256]{2,1,0:T(8,128)(2,1)}, bf16[8,64,256]{2,1,0:T(8,128)(2,1)S(1)}, u32[]{:S(2)}, u32[]{:S(2)}) collective-permute-start(bf16[8,64,256]{2,1,0:T(8,128)(2,1)} %bitcast.39), channel_id=1, source_target_pairs={{0,6},{1,7},{2,4},{3,5},{4,2},{5,3},{6,0},{7,1},{8,14},{9,15},{10,... | collective-permute-start | bytes 786440 | tf_op jit(solution)/shard_map/ppermute | solution.py:316
  105.4 19.6 %copy-start.7 = (bf16[8,64,256]{2,1,0:T(8,128)(2,1)}, bf16[8,64,256]{2,1,0:T(8,128)(2,1)S(1)}, u32[]{:S(2)}) copy-start(bf16[8,64,256]{2,1,0:T(8,128)(2,1)S(1)} %collective-permute-done.5.refs_2_) | copy-start | bytes 786436
  115.5 9.7 %copy-start.8 = (bf16[8,64,256]{2,1,0:T(8,128)(2,1)}, bf16[8,64,256]{2,1,0:T(8,128)(2,1)S(1)}, u32[]{:S(2)}) copy-start(bf16[8,64,256]{2,1,0:T(8,128)(2,1)S(1)} %collective-permute-done.6.refs_3_) | copy-start | bytes 786436
  115.5 9.7 %copy-start.9 = (bf16[8,64,256]{2,1,0:T(8,128)(2,1)}, bf16[8,64,256]{2,1,0:T(8,128)(2,1)S(1)}, u32[]{:S(2)}) copy-start(bf16[8,64,256]{2,1,0:T(8,128)(2,1)S(1)} %collective-permute-done.7.refs_4_) | copy-start | bytes 786436
  125.1 0.8 copy-start.11
  133.4 87.6 %collective-permute-start.11 = (bf16[16,16,1024]{2,1,0:T(8,128)(2,1)}, bf16[16,16,1024]{2,1,0:T(8,128)(2,1)S(1)}, u32[]{:S(2)}, u32[]{:S(2)}) collective-permute-start(bf16[16,16,1024]{2,1,0:T(8,128)(2,1)} %get-tuple-element.32), channel_id=1, source_target_pairs={{0,8},{1,9},{2,10},{3,11},{4,12},{5,13},{6,14},{7,15},{8,0},{9,1},... | collective-permute-start | bytes 1572872 | tf_op jit(solution)/shard_map/ppermute | solution.py:308
  143.1 79.3 %collective-permute-start.12 = (bf16[16,16,1024]{2,1,0:T(8,128)(2,1)}, bf16[16,16,1024]{2,1,0:T(8,128)(2,1)S(1)}, u32[]{:S(2)}, u32[]{:S(2)}) collective-permute-start(bf16[16,16,1024]{2,1,0:T(8,128)(2,1)} %get-tuple-element.33), channel_id=1, source_target_pairs={{0,16},{1,17},{2,18},{3,19},{4,20},{5,21},{6,22},{7,23},{8,24},{9,... | collective-permute-start | bytes 1572872 | tf_op jit(solution)/shard_map/ppermute | solution.py:308
  143.9 86.6 %collective-permute-start.13 = (bf16[16,16,1024]{2,1,0:T(8,128)(2,1)}, bf16[16,16,1024]{2,1,0:T(8,128)(2,1)S(1)}, u32[]{:S(2)}, u32[]{:S(2)}) collective-permute-start(bf16[16,16,1024]{2,1,0:T(8,128)(2,1)} %get-tuple-element.34), channel_id=1, source_target_pairs={{0,24},{1,25},{2,26},{3,27},{4,28},{5,29},{6,30},{7,31},{8,16},{9,... | collective-permute-start | bytes 1572872 | tf_op jit(solution)/shard_map/ppermute | solution.py:308
  205.5 14.0 %copy-start = (bf16[16,16,1024]{2,1,0:T(8,128)(2,1)S(1)}, bf16[16,16,1024]{2,1,0:T(8,128)(2,1)}, u32[]{:S(2)}) copy-start(bf16[16,16,1024]{2,1,0:T(8,128)(2,1)} %get-tuple-element.30) | copy-start | bytes 1572868
  (3 other events, 2.1 us)

commit v3 on v2

--- a/solution.py
+++ b/solution.py
@@ -39,7 +39,7 @@
     return lax.axis_index("wide") * lax.axis_size("narrow") + lax.axis_index("narrow")
 
 
-def planes_kernel(start, planes, total, block, sizes, normals, counts, low_y, high_y, low, high, low_counts,
+def planes_kernel(start, planes, total, block, sizes, normals, counts, lines, low, high, low_counts,
                   high_counts, table, *rest):
     *outs, flux_y, last_x, partial, divergence, ordered = rest
     step = pl.program_id(0)
@@ -50,6 +50,9 @@
     columns = [slice(c, c + LANES) for c in range(0, depth, LANES)]
     now = lax.rem(step, 2)
     before = 1 - now
+    here, narrow = lax.axis_index("narrow"), lines.shape[0]
+    below = jnp.where(here > 0, here - 1, here)
+    above = jnp.where(here < narrow - 1, here + 1, here)
 
     @pl.when(step == 0)
     def _():
@@ -124,8 +127,8 @@
         for plane in range(block - 1):
             transform(plane)
         for plane in range(block):
-            low_line = low_y[pl.ds(start + step * block + plane, 1), :]
-            high_line = high_y[pl.ds(start + step * block + plane, 1), :]
+            low_line = lines[below, pl.ds(start + step * block + plane, 1), :]
+            high_line = lines[above, pl.ds(start + step * block + plane, 1), :]
             for tile, cut in enumerate(columns):
                 flux_y[now, plane, tile, PAD - 1:PAD, :] = low_line[:, cut]
                 flux_y[now, plane, tile, PAD + rows:PAD + rows + 1, :] = high_line[:, cut]
@@ -153,7 +156,7 @@
 
 def along_z_of(normals, counts, halos, table, start, planes, count=1, groups=1, sizes=None):
     _, total, rows, depth = normals.shape
-    low_y, high_y, low_x, high_x = halos
+    lines, low_x, high_x = halos
     block = 4 if planes % 4 == 0 else 1
     steps = planes // block
 
@@ -167,7 +170,6 @@
         return pl.BlockSpec((1, rows, depth), lambda step: (plane, 0, 0))
 
     whole = pl.BlockSpec((rows, depth), lambda step: (0, 0))
-    lines = pl.BlockSpec((total, depth), lambda step: (0, 0))
     at_low, at_high = start == 0, start + planes == total
     below, above = max(start - 1, 0), min(start + planes, total - 1)
     size = planes * rows * depth
@@ -178,8 +180,7 @@
         in_specs=[
             pl.BlockSpec((3, block, rows, depth), lambda step: (0, block_at(step), 0, 0)),
             pl.BlockSpec((block, rows, depth), lambda step: (block_at(step), 0, 0)),
-            lines,
-            lines,
+            pl.BlockSpec(lines.shape, lambda step: (0, 0, 0)),
             whole if at_low else edge(below),
             whole if at_high else edge(above),
             edge_counts(below),
@@ -199,7 +200,7 @@
         ],
         compiler_params=pltpu.CompilerParams(vmem_limit_bytes=VMEM_BYTES),
         cost_estimate=pl.CostEstimate(flops=2 * size * depth, bytes_accessed=12 * size, transcendentals=size),
-    )(normals, counts, low_y, high_y, low_x if at_low else normals, high_x if at_high else normals, counts, counts, table)
+    )(normals, counts, lines, low_x if at_low else normals, high_x if at_high else normals, counts, counts, table)
 
 
 def order_of(planes, slab):
@@ -244,10 +245,11 @@
                 out[:, core * planes:(core + 1) * planes, :] = part
 
 
-def far_kernel(narrow, tiles, table, order, out):
+def far_kernel(narrow, tiles, table, order, *rest):
+    out = rest[-1]
     groups = [[tiles.at[at + place] for place in range(narrow)] for at in range(0, tiles.shape[0], narrow)]
     for at, moved in enumerate(y_of(groups, table, order)):
-        out[:, at, :moved.shape[1]] = moved
+        out[:, at] = moved
 
 
 def y_cost(planes, slab, wide, full_y):
@@ -277,23 +279,32 @@
     )(*tiles, table, order_of(planes, slab))
 
 
-def along_y_far(tiles, table, total, narrow):
+def along_y_far(tiles, table, so_far, start, total, narrow):
     count, planes, slab, rows = tiles.shape
     wide = count // narrow
     full_y = table.shape[1]
+    group = max(1, 512 // (planes * slab))
+    operands = [tiles, table, order_of(planes, slab)]
+    in_specs = [
+        pl.BlockSpec((group * narrow, planes, slab, rows), lambda at: (at, 0, 0, 0)),
+        pl.BlockSpec(table.shape, lambda at: (0, 0)),
+        pl.BlockSpec((planes * slab, planes * slab), lambda at: (0, 0)),
+    ]
+    aliases = {}
+    if so_far is not None:
+        operands.append(so_far.reshape(slab, wide, total, full_y))
+        in_specs.append(pl.BlockSpec(memory_space=pl.ANY))
+        aliases = {3: 0}
     return pl.pallas_call(
         functools.partial(far_kernel, narrow),
-        grid=(wide // 2,),
-        in_specs=[
-            pl.BlockSpec((2 * narrow, planes, slab, rows), lambda at: (at, 0, 0, 0)),
-            pl.BlockSpec(table.shape, lambda at: (0, 0)),
-            pl.BlockSpec((planes * slab, planes * slab), lambda at: (0, 0)),
-        ],
-        out_specs=pl.BlockSpec((slab, 2, total, full_y), lambda at: (0, at, 0, 0)),
+        grid=(wide // group,),
+        in_specs=in_specs,
+        out_specs=pl.BlockSpec((slab, group, planes, full_y), lambda at: (0, at, start // planes, 0)),
         out_shape=jax.ShapeDtypeStruct((slab, wide, total, full_y), jnp.bfloat16),
+        input_output_aliases=aliases,
         compiler_params=pltpu.CompilerParams(vmem_limit_bytes=VMEM_BYTES),
         cost_estimate=y_cost(planes, slab, wide, full_y),
-    )(tiles, table, order_of(planes, slab)).reshape(slab, wide * total, full_y)
+    )(*operands).reshape(slab, wide * total, full_y)
 
 
 def after(array, *others):
@@ -319,15 +330,15 @@
 def halos_of(normals, counts):
     wide = lax.axis_size("wide")
     narrow = lax.axis_size("narrow")
-    up = lambda count: [(i, i + 1) for i in range(count - 1)]
-    down = lambda count: [(i + 1, i) for i in range(count - 1)]
+    here = lax.axis_index("narrow")
     edge_y = lambda at: weight_of(counts[:, at, :]) * normals[1, :, at, :].astype(jnp.float32)
     edge_x = lambda at: (weight_of(counts[at]) * normals[0, at].astype(jnp.float32)).astype(jnp.bfloat16)
-    low_y = lax.ppermute(edge_y(counts.shape[1] - 1), "narrow", up(narrow))
-    high_y = lax.ppermute(edge_y(0), "narrow", down(narrow))
-    low_x = lax.ppermute(edge_x(counts.shape[0] - 1), "wide", up(wide))
-    high_x = lax.ppermute(edge_x(0), "wide", down(wide))
-    return low_y, high_y, low_x, high_x
+    to = lax.broadcasted_iota(jnp.int32, (narrow, 1, 1), 0)
+    lines = jnp.where(to == here + 1, edge_y(counts.shape[1] - 1), jnp.where(to == here - 1, edge_y(0), 0.0))
+    lines = lax.all_to_all(lines, "narrow", split_axis=0, concat_axis=0, tiled=True)
+    low_x = lax.ppermute(edge_x(counts.shape[0] - 1), "wide", [(i, i + 1) for i in range(wide - 1)])
+    high_x = lax.ppermute(edge_x(0), "wide", [(i + 1, i) for i in range(wide - 1)])
+    return lines, low_x, high_x
 
 
 def per_device(normals, counts):
@@ -343,23 +354,28 @@
     far = wide // cores
     near = cores * narrow
     if slab % 16 == 0 and total % 32 == 0 and wide == cores * far and far & (far - 1) == 0 and near & (near - 1) == 0:
-        most = total * 3 // 4
-        rest = total - most
-        pieces = along_z_of(normals, counts, halos, after(table_z, halos[3]), 0, most, 1, wide * narrow)[0]
+        few = total // 4
+        third, first, second = 0, few, 2 * few
+        pieces = along_z_of(normals, counts, halos, table_z, first, few, 1, wide * narrow)[0]
+        pieces = after(pieces, *halos)
+        arrived = lax.all_to_all(pieces, ("wide", "narrow"), split_axis=0, concat_axis=0, tiled=True)
         later = after(table_z, pieces)
-        pieces = lax.all_to_all(pieces, ("wide", "narrow"), split_axis=0, concat_axis=0, tiled=True)
-        tiles = along_z_of(normals, counts, halos, later, most, rest, near, 1, (far, near))
+        tiles = along_z_of(normals, counts, halos, later, third, few, near, 1, (far, near))
+        later = after(table_z, tiles[0])
         tiles = [swap_near(tile[0], step, near) for step, tile in enumerate(tiles)]
+        pieces = along_z_of(normals, counts, halos, later, second, 2 * few, 1, wide * narrow)[0]
+        arrived_later = lax.all_to_all(pieces, ("wide", "narrow"), split_axis=0, concat_axis=0, tiled=True)
         far_pieces = along_y_near(tiles, table_y, far, narrow)
-        pieces = after(pieces, far_pieces[0])
+        arrived = after(arrived, far_pieces[0])
         far_pieces = [swap_far(piece, step, near) for step, piece in enumerate(far_pieces)]
-        spectrum = along_y_far(pieces, table_y, total, narrow)
+        spectrum = along_y_far(arrived, table_y, None, first, total, narrow)
+        spectrum = along_y_far(arrived_later, table_y, spectrum, second, total, narrow)
         mine = device() // near
         for step, piece in enumerate(far_pieces):
             for turn in range(cores):
                 core = partner(device() % near // narrow, turn)
-                at = (partner(mine, step) * cores + core) * total + most
-                spectrum = lax.dynamic_update_slice(spectrum, piece[:, turn * rest:(turn + 1) * rest], (0, at, 0))
+                at = (partner(mine, step) * cores + core) * total + third
+                spectrum = lax.dynamic_update_slice(spectrum, piece[:, turn * few:(turn + 1) * few], (0, at, 0))
         return spectrum
     along = along_z_of(normals, counts, halos, table_z, 0, total)[0]
     along = along.reshape(total, wide * narrow, slab, rows)

time: 234 us -> 224 us (0.957)
  waiting for transfers between devices: 138 us -> 126 us
  Pallas kernels: 50.2 us -> 54.9 us
    ppermute x3, starting transfers between devices: 11.2 us -> 3.55 us  [swap_far(): return lax.ppermute(array, ('wide', 'narrow'), pairs)]
    ppermute x7, waiting for transfers between devices: 65.3 us -> 58.4 us  [swap_near(): return lax.ppermute(array, ('wide', 'narrow'), pairs)]
    all_to_all x1 -> x2, starting transfers between devices: 5.57 us -> 11.2 us  [per_device(): lax.all_to_all(pieces, ('wide', 'narrow'), split_axis=0, concat_axis=0, t...]
    ppermute x4 -> x2, waiting for transfers between devices: 5.33 us -> 0.01 us  [the longest x1 0.01 us: halos_of(): lax.ppermute(edge_x(0), 'wide', [(i + 1, i) for i in range(wide - 1)])]
    all_to_all x1 -> x2, waiting for transfers between devices: 60.9 us -> 55.5 us  [per_device(): lax.all_to_all(pieces, ('wide', 'narrow'), split_axis=0, concat_axis=0, t...]
    ppermute x3, waiting for transfers between devices: 6.65 us -> 11.9 us  [swap_far(): return lax.ppermute(array, ('wide', 'narrow'), pairs)]
    ppermute x4 -> x2, starting transfers between devices: 9.02 us -> 4.33 us  [the longest x1 2.41 us: halos_of(): lax.ppermute(edge_x(counts.shape[0] - 1), 'wide', [(i, i + 1) for i in ra...]
    pallas_call x2 -> x3, Pallas kernels: 28.6 us -> 32.4 us  [along_z_of(): pl.pallas_call(functools.partial(planes_kernel, start, planes, total, blo...]
  transfers between devices with their start and end apart: 15 -> 15, of which waited for: 8 -> 7; matrix products, arithmetic and copies ran while one was open for 3% -> 3% of each run, Pallas kernels for 13% -> 25%
where the time goes in v3:
time: 224 us
  waiting for transfers between devices  126 us (56%)
  Pallas kernels  54.9 us (25%)
  starting transfers between devices  30.6 us (14%)
  local copies, waits for them, and re-layouts  9.73 us (4%)
  other arithmetic  2.44 us (1%)
    ppermute x7, waiting for transfers between devices, swap_near(): return lax.ppermute(array, ('wide', 'narrow'), pairs)  58.4 us
    all_to_all x2, waiting for transfers between devices, per_device(): lax.all_to_all(pieces, ('wide', 'narrow'), split_axis=0, concat_axis=0, t...  55.5 us
    pallas_call x3, Pallas kernels, along_z_of(): pl.pallas_call(functools.partial(planes_kernel, start, planes, total, blo...  32.4 us
    pallas_call x2, Pallas kernels, along_y_far(): pl.pallas_call(functools.partial(far_kernel, narrow), grid=(wide // group...  15.1 us
    ppermute x3, waiting for transfers between devices, swap_far(): return lax.ppermute(array, ('wide', 'narrow'), pairs)  11.9 us
    all_to_all x2, starting transfers between devices, per_device(): lax.all_to_all(pieces, ('wide', 'narrow'), split_axis=0, concat_axis=0, t...  11.2 us
    ppermute x7, starting transfers between devices, swap_near(): return lax.ppermute(array, ('wide', 'narrow'), pairs)  7.73 us
    pallas_call x1, Pallas kernels, along_y_near(): pl.pallas_call(functools.partial(near_kernel, near, narrow), grid=(far,),...  7.46 us
  transfers between devices with their start and end apart: 15, of which 7 were waited for; matrix products, arithmetic and copies ran while one was open for 3% of the time, Pallas kernels for 25%

profile of v3, /device:TPU:8, one launch (start us, length us, event | category | flops | bytes accessed | tf_op | source)
XLA Modules:
  0.0 223.7 jit_solution(4583217779497686683)
XLA Ops:
  3.3 3.7 %all-to-all-start = ((f32[4,32,512]{2,1,0:T(8,128)}), f32[4,32,512]{2,1,0:T(8,128)S(1)}, u32[]{:S(2)}, u32[]{:S(2)}) async-start(f32[4,32,512]{2,1,0:T(8,128)} %select_select_fusion), calls=%async_computation | async-start | bytes 524288 | tf_op jit(solution)/shard_map/all_to_all | solution.py:338
  7.0 1.6 fusion.3
  8.6 1.9 collective-permute-start
  10.6 2.4 %collective-permute-start.1 = (bf16[256,512]{1,0:T(8,128)(2,1)S(1)}, bf16[256,512]{1,0:T(8,128)(2,1)S(1)}, u32[]{:S(2)}, u32[]{:S(2)}) collective-permute-start(bf16[256,512]{1,0:T(8,128)(2,1)S(1)} %get-tuple-element.37), channel_id=1, source_target_pairs={{0,4},{4,8},{8,12},{12,16},{16,20},{20,24},{24,28},{1,5},{5,9},{9,... | collective-permute-start | bytes 786440 | tf_op jit(solution)/shard_map/ppermute | solution.py:339
  13.7 8.8 %shard_map.73 = bf16[32,8,16,256]{3,2,1,0:T(8,128)(2,1)} custom-call(bf16[3,32,256,512]{3,2,1,0:T(8,128)(2,1)} %low.3, s32[32,256,512]{2,1,0:T(8,128)} %high_counts.5, f32[4,32,512]{2,1,0:T(8,128)} %copy-done.1, bf16[3,32,256,512]{3,2,1,0:T(8,128)(2,1)} %low.3, bf16[3,32,256,512]{3,2,1,0:T(8,128)(2,1)} %low.3, s32[32,256,512]{2,1,0:T(8,128)} %high_counts.5, ...), custom_call_target="tpu_custom_call" | custom-call | flops 1073741824 | bytes 12582912 | tf_op jit(solution)/shard_map/pallas_call | solution.py:177
  22.5 6.5 %all-to-all-start.2 = ((bf16[32,8,16,256]{3,2,1,0:T(8,128)(2,1)}), bf16[32,8,16,256]{3,2,1,0:T(8,128)(2,1)S(1)}, u32[]{:S(2)}, u32[]{:S(2)}) async-start(bf16[32,8,16,256]{3,2,1,0:T(8,128)(2,1)} %shard_map.73), calls=%async_computation.2 | async-start | bytes 4194304 | tf_op jit(solution)/shard_map/all_to_all | solution.py:361
  29.1 9.9 %shard_map.74 = (bf16[1,8,64,256]{3,2,1,0:T(8,128)(2,1)}, bf16[1,8,64,256]{3,2,1,0:T(8,128)(2,1)}, bf16[1,8,64,256]{3,2,1,0:T(8,128)(2,1)}, bf16[1,8,64,256]{3,2...) custom-call(bf16[3,32,256,512]{3,2,1,0:T(8,128)(2,1)} %low.3, ...), custom_call_target="tpu_custom_call" | custom-call | flops 1073741824 | bytes 12582912 | tf_op jit(solution)/shard_map/pallas_call | solution.py:177
  39.0 13.7 %shard_map.75 = bf16[32,16,16,256]{3,2,1,0:T(8,128)(2,1)} custom-call(bf16[3,32,256,512]{3,2,1,0:T(8,128)(2,1)} %low.3, s32[32,256,512]{2,1,0:T(8,128)} %high_counts.5, f32[4,32,512]{2,1,0:T(8,128)} %copy-done.1, bf16[3,32,256,512]{3,2,1,0:T(8,128)(2,1)} %low.3, bf16[256,512]{1,0:T(8,128)(2,1)} %copy-done.3, s32[32,256,512]{2,1,0:T(8,128)} %high_counts.5, ...), custom_call_target="tpu_custom_call" | custom-call | flops 2147483648 | bytes 25165824 | tf_op jit(solution)/shard_map/pallas_call | solution.py:177
  52.7 24.8 %all-to-all-done.2.tiles = bf16[32,8,16,256]{3,2,1,0:T(8,128)(2,1)S(1)} async-done(((bf16[32,8,16,256]{3,2,1,0:T(8,128)(2,1)}), bf16[32,8,16,256]{3,2,1,0:T(8,128)(2,1)S(1)}, u32[]{:S(2)}, u32[]{:S(2)}) %all-to-all-start.2) | async-done | bytes 2097184 | tf_op jit(solution)/shard_map/all_to_all | solution.py:361
  77.5 4.7 %all-to-all-start.1 = ((bf16[32,16,16,256]{3,2,1,0:T(8,128)(2,1)}), bf16[32,16,16,256]{3,2,1,0:T(8,128)(2,1)}, u32[]{:S(2)}, u32[]{:S(2)}) async-start(bf16[32,16,16,256]{3,2,1,0:T(8,128)(2,1)} %shard_map.75), calls=%async_computation.1 | async-start | bytes 8388608 | tf_op jit(solution)/shard_map/all_to_all | solution.py:367
  82.2 1.5 collective-permute-start.2
  83.8 1.5 collective-permute-start.3
  85.8 1.6 collective-permute-start.6
  87.4 29.4 %collective-permute-done.2.refs_1_ = bf16[8,64,256]{2,1,0:T(8,128)(2,1)S(1)} collective-permute-done((bf16[8,64,256]{2,1,0:T(8,128)(2,1)}, bf16[8,64,256]{2,1,0:T(8,128)(2,1)S(1)}, u32[]{:S(2)}, u32[]{:S(2)}) %collective-permute-start.2) | collective-permute-done | bytes 262176 | tf_op jit(solution)/shard_map/ppermute | solution.py:327
  117.6 2.6 %collective-permute-start.8 = (bf16[8,64,256]{2,1,0:T(8,128)(2,1)S(1)}, bf16[8,64,256]{2,1,0:T(8,128)(2,1)}, u32[]{:S(2)}, u32[]{:S(2)}) collective-permute-start(bf16[8,64,256]{2,1,0:T(8,128)(2,1)S(1)} %bitcast.39), channel_id=1, source_target_pairs={{0,7},{1,6},{2,5},{3,4},{4,3},{5,2},{6,1},{7,0},{8,15},{9,14},{10,... | collective-permute-start | bytes 786440 | tf_op jit(solution)/shard_map/ppermute | solution.py:327
  120.2 6.6 %collective-permute-done.4.refs_3_ = bf16[8,64,256]{2,1,0:T(8,128)(2,1)} collective-permute-done((bf16[8,64,256]{2,1,0:T(8,128)(2,1)}, bf16[8,64,256]{2,1,0:T(8,128)(2,1)}, u32[]{:S(2)}, u32[]{:S(2)}) %collective-permute-start.4) | collective-permute-done | bytes 262176 | tf_op jit(solution)/shard_map/ppermute | solution.py:327
  126.8 9.3 %collective-permute-done.6.refs_5_ = bf16[8,64,256]{2,1,0:T(8,128)(2,1)} collective-permute-done((bf16[8,64,256]{2,1,0:T(8,128)(2,1)S(1)}, bf16[8,64,256]{2,1,0:T(8,128)(2,1)}, u32[]{:S(2)}, u32[]{:S(2)}) %collective-permute-start.6) | collective-permute-done | bytes 262176 | tf_op jit(solution)/shard_map/ppermute | solution.py:327
  136.1 13.1 %collective-permute-done.7.refs_6_ = bf16[8,64,256]{2,1,0:T(8,128)(2,1)} collective-permute-done((bf16[8,64,256]{2,1,0:T(8,128)(2,1)S(1)}, bf16[8,64,256]{2,1,0:T(8,128)(2,1)}, u32[]{:S(2)}, u32[]{:S(2)}) %collective-permute-start.7) | collective-permute-done | bytes 262176 | tf_op jit(solution)/shard_map/ppermute | solution.py:327
  149.2 7.5 %shard_map.76 = (bf16[16,16,1024]{2,1,0:T(8,128)(2,1)}, bf16[16,16,1024]{2,1,0:T(8,128)(2,1)}, bf16[16,16,1024]{2,1,0:T(8,128)(2,1)}, bf16[16,16,1024]{2,1,0:T(8,128)(2,1)}) custom-call(bf16[8,64,256]{2,1,0:T(8,128)(2,1)} %bitcast.38, bf16[8,64,256]{2,1,0:T(8,128)(2,1)} %copy-done.9, bf16[8,64,256]{2,1,0:T(8,128)(2,1)} %copy-done.10, ...), custom_call_target="tpu_custom_call" | custom-call | flops 2415919104 | bytes 4194304 | tf_op jit(solution)/shard_map/pallas_call | solution.py:267
  156.7 2.7 %collective-permute-start.10 = (bf16[16,16,1024]{2,1,0:T(8,128)(2,1)}, bf16[16,16,1024]{2,1,0:T(8,128)(2,1)S(1)}, u32[]{:S(2)}, u32[]{:S(2)}) collective-permute-start(bf16[16,16,1024]{2,1,0:T(8,128)(2,1)} %get-tuple-element.35), channel_id=1, source_target_pairs={{0,16},{1,17},{2,18},{3,19},{4,20},{5,21},{6,22},{7,23},{8,24},{9,... | collective-permute-start | bytes 1572872 | tf_op jit(solution)/shard_map/ppermute | solution.py:319
  160.2 6.0 %shard_map.77.rest_0_ = bf16[16,8,32,1024]{3,2,1,0:T(8,128)(2,1)} custom-call(bf16[32,8,16,256]{3,2,1,0:T(8,128)(2,1)} %copy-done, bf16[1024,1024]{1,0:T(8,128)(2,1)} %constant.97.clone.refs_8_.table, bf16[128,128]{1,0:T(8,128)(2,1)} %constant.98.clone.refs_9_.order), custom_call_target="tpu_custom_call" | custom-call | flops 2415919104 | bytes 4194304 | tf_op jit(solution)/shard_map/pallas_call | solution.py:298
  166.2 30.7 %all-to-all-done.1.tiles = bf16[32,16,16,256]{3,2,1,0:T(8,128)(2,1)} async-done(((bf16[32,16,16,256]{3,2,1,0:T(8,128)(2,1)}), bf16[32,16,16,256]{3,2,1,0:T(8,128)(2,1)}, u32[]{:S(2)}, u32[]{:S(2)}) %all-to-all-start.1) | async-done | bytes 4194336 | tf_op jit(solution)/shard_map/all_to_all | solution.py:367
  196.9 9.1 %shard_map.78 = bf16[16,8,32,1024]{3,2,1,0:T(8,128)(2,1)} custom-call(bf16[32,16,16,256]{3,2,1,0:T(8,128)(2,1)} %all-to-all-done.1.tiles, bf16[1024,1024]{1,0:T(8,128)(2,1)} %constant.97.clone.refs_8_.table, bf16[256,256]{1,0:T(8,128)(2,1)} %constant.99.clone.order, bf16[16,8,32,1024]{3,2,1,0:T(8,128)(2,1)} %shard_map.77.rest_0_), custom_call_target="tpu_custom_call", output_to_operand_aliasing={{}: (3, {})} | custom-call | flops 5368709120 | bytes 8388608 | tf_op jit(solution)/shard_map/pallas_call | solution.py:298
  210.4 11.9 %collective-permute-done.11 = bf16[16,16,1024]{2,1,0:T(8,128)(2,1)S(1)} collective-permute-done((bf16[16,16,1024]{2,1,0:T(8,128)(2,1)}, bf16[16,16,1024]{2,1,0:T(8,128)(2,1)S(1)}, u32[]{:S(2)}, u32[]{:S(2)}) %collective-permute-start.11) | collective-permute-done | bytes 524320 | tf_op jit(solution)/shard_map/ppermute | solution.py:319
  (48 shorter events, 12.0 us)
Async XLA Ops:
  3.3 9.7 %all-to-all-start = ((f32[4,32,512]{2,1,0:T(8,128)}), f32[4,32,512]{2,1,0:T(8,128)S(1)}, u32[]{:S(2)}, u32[]{:S(2)}) async-start(f32[4,32,512]{2,1,0:T(8,128)} %select_select_fusion), calls=%async_computation | async-start | bytes 524288 | tf_op jit(solution)/shard_map/all_to_all | solution.py:338
  8.6 13.9 %collective-permute-start = (bf16[256,512]{1,0:T(8,128)(2,1)S(1)}, bf16[256,512]{1,0:T(8,128)(2,1)S(1)}, u32[]{:S(2)}, u32[]{:S(2)}) collective-permute-start(bf16[256,512]{1,0:T(8,128)(2,1)S(1)} %get-tuple-element.38), channel_id=1, source_target_pairs={{4,0},{8,4},{12,8},{16,12},{20,16},{24,20},{28,24},{5,1},{9,5},{13... | collective-permute-start | bytes 786440 | tf_op jit(solution)/shard_map/ppermute | solution.py:340
  10.6 12.0 %collective-permute-start.1 = (bf16[256,512]{1,0:T(8,128)(2,1)S(1)}, bf16[256,512]{1,0:T(8,128)(2,1)S(1)}, u32[]{:S(2)}, u32[]{:S(2)}) collective-permute-start(bf16[256,512]{1,0:T(8,128)(2,1)S(1)} %get-tuple-element.37), channel_id=1, source_target_pairs={{0,4},{4,8},{8,12},{12,16},{16,20},{20,24},{24,28},{1,5},{5,9},{9,... | collective-permute-start | bytes 786440 | tf_op jit(solution)/shard_map/ppermute | solution.py:339
  22.5 16.5 %copy-start.3 = (bf16[256,512]{1,0:T(8,128)(2,1)}, bf16[256,512]{1,0:T(8,128)(2,1)S(1)}, u32[]{:S(2)}) copy-start(bf16[256,512]{1,0:T(8,128)(2,1)S(1)} %collective-permute-done.high) | copy-start | bytes 786436
  22.5 6.6 %copy-start.4 = (bf16[256,512]{1,0:T(8,128)(2,1)}, bf16[256,512]{1,0:T(8,128)(2,1)S(1)}, u32[]{:S(2)}) copy-start(bf16[256,512]{1,0:T(8,128)(2,1)S(1)} %collective-permute-done.1.low) | copy-start | bytes 786436
  22.5 55.0 %all-to-all-start.2 = ((bf16[32,8,16,256]{3,2,1,0:T(8,128)(2,1)}), bf16[32,8,16,256]{3,2,1,0:T(8,128)(2,1)S(1)}, u32[]{:S(2)}, u32[]{:S(2)}) async-start(bf16[32,8,16,256]{3,2,1,0:T(8,128)(2,1)} %shard_map.73), calls=%async_computation.2 | async-start | bytes 4194304 | tf_op jit(solution)/shard_map/all_to_all | solution.py:361
  52.7 33.1 %copy-start.8 = (bf16[1,8,64,256]{3,2,1,0:T(8,128)(2,1)S(1)}, bf16[1,8,64,256]{3,2,1,0:T(8,128)(2,1)}, u32[]{:S(2)}) copy-start(bf16[1,8,64,256]{3,2,1,0:T(8,128)(2,1)} %get-tuple-element.28) | copy-start | bytes 786436
  52.7 33.1 %copy-start.7 = (bf16[1,8,64,256]{3,2,1,0:T(8,128)(2,1)S(1)}, bf16[1,8,64,256]{3,2,1,0:T(8,128)(2,1)}, u32[]{:S(2)}) copy-start(bf16[1,8,64,256]{3,2,1,0:T(8,128)(2,1)} %get-tuple-element.29) | copy-start | bytes 786436
  52.7 64.1 %copy-start.6 = (bf16[1,8,64,256]{3,2,1,0:T(8,128)(2,1)S(1)}, bf16[1,8,64,256]{3,2,1,0:T(8,128)(2,1)}, u32[]{:S(2)}) copy-start(bf16[1,8,64,256]{3,2,1,0:T(8,128)(2,1)} %get-tuple-element.30) | copy-start | bytes 786436
  52.7 64.9 %copy-start.5 = (bf16[1,8,64,256]{3,2,1,0:T(8,128)(2,1)S(1)}, bf16[1,8,64,256]{3,2,1,0:T(8,128)(2,1)}, u32[]{:S(2)}) copy-start(bf16[1,8,64,256]{3,2,1,0:T(8,128)(2,1)} %get-tuple-element.31) | copy-start | bytes 786436
  77.5 79.1 %copy-start = (bf16[32,8,16,256]{3,2,1,0:T(8,128)(2,1)}, bf16[32,8,16,256]{3,2,1,0:T(8,128)(2,1)S(1)}, u32[]{:S(2)}) copy-start(bf16[32,8,16,256]{3,2,1,0:T(8,128)(2,1)S(1)} %all-to-all-done.2.tiles) | copy-start | bytes 6291460
  77.5 119.4 %all-to-all-start.1 = ((bf16[32,16,16,256]{3,2,1,0:T(8,128)(2,1)}), bf16[32,16,16,256]{3,2,1,0:T(8,128)(2,1)}, u32[]{:S(2)}, u32[]{:S(2)}) async-start(bf16[32,16,16,256]{3,2,1,0:T(8,128)(2,1)} %shard_map.75), calls=%async_computation.1 | async-start | bytes 8388608 | tf_op jit(solution)/shard_map/all_to_all | solution.py:367
  82.2 34.6 %collective-permute-start.2 = (bf16[8,64,256]{2,1,0:T(8,128)(2,1)}, bf16[8,64,256]{2,1,0:T(8,128)(2,1)S(1)}, u32[]{:S(2)}, u32[]{:S(2)}) collective-permute-start(bf16[8,64,256]{2,1,0:T(8,128)(2,1)} %bitcast.45), channel_id=1, source_target_pairs={{0,1},{1,0},{2,3},{3,2},{4,5},{5,4},{6,7},{7,6},{8,9},{9,8},{10,11... | collective-permute-start | bytes 786440 | tf_op jit(solution)/shard_map/ppermute | solution.py:327
  83.8 33.1 %collective-permute-start.3 = (bf16[8,64,256]{2,1,0:T(8,128)(2,1)}, bf16[8,64,256]{2,1,0:T(8,128)(2,1)S(1)}, u32[]{:S(2)}, u32[]{:S(2)}) collective-permute-start(bf16[8,64,256]{2,1,0:T(8,128)(2,1)} %bitcast.44), channel_id=1, source_target_pairs={{0,2},{1,3},{2,0},{3,1},{4,6},{5,7},{6,4},{7,5},{8,10},{9,11},{10,... | collective-permute-start | bytes 786440 | tf_op jit(solution)/shard_map/ppermute | solution.py:327
  85.2 41.5 %collective-permute-start.4 = (bf16[8,64,256]{2,1,0:T(8,128)(2,1)}, bf16[8,64,256]{2,1,0:T(8,128)(2,1)}, u32[]{:S(2)}, u32[]{:S(2)}) collective-permute-start(bf16[8,64,256]{2,1,0:T(8,128)(2,1)} %bitcast.43), channel_id=1, source_target_pairs={{0,3},{1,2},{2,1},{3,0},{4,7},{5,6},{6,5},{7,4},{8,11},{9,10},{10,... | collective-permute-start | bytes 786440 | tf_op jit(solution)/shard_map/ppermute | solution.py:327
  85.8 41.0 %collective-permute-start.5 = (bf16[8,64,256]{2,1,0:T(8,128)(2,1)S(1)}, bf16[8,64,256]{2,1,0:T(8,128)(2,1)}, u32[]{:S(2)}, u32[]{:S(2)}) collective-permute-start(bf16[8,64,256]{2,1,0:T(8,128)(2,1)S(1)} %bitcast.42), channel_id=1, source_target_pairs={{0,4},{1,5},{2,6},{3,7},{4,0},{5,1},{6,2},{7,3},{8,12},{9,13},{10,... | collective-permute-start | bytes 786440 | tf_op jit(solution)/shard_map/ppermute | solution.py:327
  85.8 50.3 %collective-permute-start.6 = (bf16[8,64,256]{2,1,0:T(8,128)(2,1)S(1)}, bf16[8,64,256]{2,1,0:T(8,128)(2,1)}, u32[]{:S(2)}, u32[]{:S(2)}) collective-permute-start(bf16[8,64,256]{2,1,0:T(8,128)(2,1)S(1)} %bitcast.41), channel_id=1, source_target_pairs={{0,5},{1,4},{2,7},{3,6},{4,1},{5,0},{6,3},{7,2},{8,13},{9,12},{10,... | collective-permute-start | bytes 786440 | tf_op jit(solution)/shard_map/ppermute | solution.py:327
  116.8 32.3 %copy-start.9 = (bf16[8,64,256]{2,1,0:T(8,128)(2,1)}, bf16[8,64,256]{2,1,0:T(8,128)(2,1)S(1)}, u32[]{:S(2)}) copy-start(bf16[8,64,256]{2,1,0:T(8,128)(2,1)S(1)} %collective-permute-done.2.refs_1_) | copy-start | bytes 786436
  116.8 32.3 %collective-permute-start.7 = (bf16[8,64,256]{2,1,0:T(8,128)(2,1)S(1)}, bf16[8,64,256]{2,1,0:T(8,128)(2,1)}, u32[]{:S(2)}, u32[]{:S(2)}) collective-permute-start(bf16[8,64,256]{2,1,0:T(8,128)(2,1)S(1)} %bitcast.40), channel_id=1, source_target_pairs={{0,6},{1,7},{2,4},{3,5},{4,2},{5,3},{6,0},{7,1},{8,14},{9,15},{10,... | collective-permute-start | bytes 786440 | tf_op jit(solution)/shard_map/ppermute | solution.py:327
  117.6 31.6 %collective-permute-start.8 = (bf16[8,64,256]{2,1,0:T(8,128)(2,1)S(1)}, bf16[8,64,256]{2,1,0:T(8,128)(2,1)}, u32[]{:S(2)}, u32[]{:S(2)}) collective-permute-start(bf16[8,64,256]{2,1,0:T(8,128)(2,1)S(1)} %bitcast.39), channel_id=1, source_target_pairs={{0,7},{1,6},{2,5},{3,4},{4,3},{5,2},{6,1},{7,0},{8,15},{9,14},{10,... | collective-permute-start | bytes 786440 | tf_op jit(solution)/shard_map/ppermute | solution.py:327
  156.6 50.8 %collective-permute-start.9 = (bf16[16,16,1024]{2,1,0:T(8,128)(2,1)}, bf16[16,16,1024]{2,1,0:T(8,128)(2,1)S(1)}, u32[]{:S(2)}, u32[]{:S(2)}) collective-permute-start(bf16[16,16,1024]{2,1,0:T(8,128)(2,1)} %get-tuple-element.34), channel_id=1, source_target_pairs={{0,8},{1,9},{2,10},{3,11},{4,12},{5,13},{6,14},{7,15},{8,0},{9,1},... | collective-permute-start | bytes 1572872 | tf_op jit(solution)/shard_map/ppermute | solution.py:319
  156.7 52.2 %collective-permute-start.10 = (bf16[16,16,1024]{2,1,0:T(8,128)(2,1)}, bf16[16,16,1024]{2,1,0:T(8,128)(2,1)S(1)}, u32[]{:S(2)}, u32[]{:S(2)}) collective-permute-start(bf16[16,16,1024]{2,1,0:T(8,128)(2,1)} %get-tuple-element.35), channel_id=1, source_target_pairs={{0,16},{1,17},{2,18},{3,19},{4,20},{5,21},{6,22},{7,23},{8,24},{9,... | collective-permute-start | bytes 1572872 | tf_op jit(solution)/shard_map/ppermute | solution.py:319
  159.4 62.9 %collective-permute-start.11 = (bf16[16,16,1024]{2,1,0:T(8,128)(2,1)}, bf16[16,16,1024]{2,1,0:T(8,128)(2,1)S(1)}, u32[]{:S(2)}, u32[]{:S(2)}) collective-permute-start(bf16[16,16,1024]{2,1,0:T(8,128)(2,1)} %get-tuple-element.36), channel_id=1, source_target_pairs={{0,24},{1,25},{2,26},{3,27},{4,28},{5,29},{6,30},{7,31},{8,16},{9,... | collective-permute-start | bytes 1572872 | tf_op jit(solution)/shard_map/ppermute | solution.py:319
  166.2 39.9 %copy-start.2 = (bf16[16,16,1024]{2,1,0:T(8,128)(2,1)S(1)}, bf16[16,16,1024]{2,1,0:T(8,128)(2,1)}, u32[]{:S(2)}) copy-start(bf16[16,16,1024]{2,1,0:T(8,128)(2,1)} %get-tuple-element.32) | copy-start | bytes 1572868
  (2 other events, 1.5 us)

commit v4 on v3

--- a/solution.py
+++ b/solution.py
@@ -327,17 +327,52 @@
     return lax.ppermute(array, ("wide", "narrow"), pairs)
 
 
+def edges_kernel(low_y, high_y, low_y_counts, high_y_counts, low_x, high_x, low_x_counts, high_x_counts,
+                 lines, low_plane, high_plane):
+    narrow = lines.shape[0]
+    here = lax.axis_index("narrow")
+    last = low_y_counts.shape[1] - 1
+    first_line = weight_of(low_y_counts[:, 0, :]) * low_y[0, :, 0, :].astype(jnp.float32)
+    last_line = weight_of(high_y_counts[:, last, :]) * high_y[0, :, high_y.shape[2] - 1, :].astype(jnp.float32)
+    for to in range(narrow):
+        lines[to] = jnp.where(here + 1 == to, last_line, jnp.where(here - 1 == to, first_line, 0.0))
+    low_plane[...] = (weight_of(low_x_counts[0]) * low_x[0, 0].astype(jnp.float32)).astype(jnp.bfloat16)
+    high_plane[...] = (weight_of(high_x_counts[0]) * high_x[0, 0].astype(jnp.float32)).astype(jnp.bfloat16)
+
+
+def edges_of(normals, counts, narrow):
+    _, total, rows, depth = normals.shape
+    few, fewer = 16, 8
+    whole = pl.BlockSpec((rows, depth), lambda at: (0, 0))
+    return pl.pallas_call(
+        edges_kernel,
+        grid=(1,),
+        in_specs=[
+            pl.BlockSpec((1, total, few, depth), lambda at: (1, 0, 0, 0)),
+            pl.BlockSpec((1, total, few, depth), lambda at: (1, 0, rows // few - 1, 0)),
+            pl.BlockSpec((total, fewer, depth), lambda at: (0, 0, 0)),
+            pl.BlockSpec((total, fewer, depth), lambda at: (0, rows // fewer - 1, 0)),
+            pl.BlockSpec((1, 1, rows, depth), lambda at: (0, 0, 0, 0)),
+            pl.BlockSpec((1, 1, rows, depth), lambda at: (0, total - 1, 0, 0)),
+            pl.BlockSpec((1, rows, depth), lambda at: (0, 0, 0)),
+            pl.BlockSpec((1, rows, depth), lambda at: (total - 1, 0, 0)),
+        ],
+        out_specs=[pl.BlockSpec((narrow, total, depth), lambda at: (0, 0, 0)), whole, whole],
+        out_shape=[
+            jax.ShapeDtypeStruct((narrow, total, depth), jnp.float32),
+            jax.ShapeDtypeStruct((rows, depth), jnp.bfloat16),
+            jax.ShapeDtypeStruct((rows, depth), jnp.bfloat16),
+        ],
+        compiler_params=pltpu.CompilerParams(vmem_limit_bytes=VMEM_BYTES),
+    )(normals, normals, counts, counts, normals, normals, counts, counts)
+
+
 def halos_of(normals, counts):
     wide = lax.axis_size("wide")
-    narrow = lax.axis_size("narrow")
-    here = lax.axis_index("narrow")
-    edge_y = lambda at: weight_of(counts[:, at, :]) * normals[1, :, at, :].astype(jnp.float32)
-    edge_x = lambda at: (weight_of(counts[at]) * normals[0, at].astype(jnp.float32)).astype(jnp.bfloat16)
-    to = lax.broadcasted_iota(jnp.int32, (narrow, 1, 1), 0)
-    lines = jnp.where(to == here + 1, edge_y(counts.shape[1] - 1), jnp.where(to == here - 1, edge_y(0), 0.0))
+    lines, first, last = edges_of(normals, counts, lax.axis_size("narrow"))
     lines = lax.all_to_all(lines, "narrow", split_axis=0, concat_axis=0, tiled=True)
-    low_x = lax.ppermute(edge_x(counts.shape[0] - 1), "wide", [(i, i + 1) for i in range(wide - 1)])
-    high_x = lax.ppermute(edge_x(0), "wide", [(i + 1, i) for i in range(wide - 1)])
+    low_x = lax.ppermute(last, "wide", [(i, i + 1) for i in range(wide - 1)])
+    high_x = lax.ppermute(first, "wide", [(i + 1, i) for i in range(wide - 1)])
     return lines, low_x, high_x
 
 

time: 224 us -> 222 us (level)
  Pallas kernels: 54.9 us -> 58.1 us
  local copies, waits for them, and re-layouts: 9.73 us -> 6.53 us
  other arithmetic: 2.44 us -> 0 us
    pallas_call x0 -> x1, Pallas kernels: none -> 3.14 us  [edges_of(): pl.pallas_call(edges_kernel, grid=(1,), in_specs=[pl.BlockSpec((1, total,...]
    slice x2 -> x0, local copies, waits for them, and re-layouts: 2.45 us -> none  [the longest x1 1.32 us: halos_of(): counts[:, at, :]]
  transfers between devices with their start and end apart: 15 -> 15, of which waited for: 7 -> 8; matrix products, arithmetic and copies ran while one was open for 3% -> 2% of each run, Pallas kernels for 25% -> 25%
where the time goes in v4:
time: 222 us
  waiting for transfers between devices  127 us (57%)
  Pallas kernels  58.1 us (26%)
  starting transfers between devices  29.6 us (13%)
  local copies, waits for them, and re-layouts  6.53 us (3%)
    ppermute x7, waiting for transfers between devices, swap_near(): return lax.ppermute(array, ('wide', 'narrow'), pairs)  59 us
    all_to_all x2, waiting for transfers between devices, per_device(): lax.all_to_all(pieces, ('wide', 'narrow'), split_axis=0, concat_axis=0, t...  55.5 us
    pallas_call x3, Pallas kernels, along_z_of(): pl.pallas_call(functools.partial(planes_kernel, start, planes, total, blo...  32.4 us
    pallas_call x2, Pallas kernels, along_y_far(): pl.pallas_call(functools.partial(far_kernel, narrow), grid=(wide // group...  15.1 us
    ppermute x3, waiting for transfers between devices, swap_far(): return lax.ppermute(array, ('wide', 'narrow'), pairs)  11.9 us
    all_to_all x2, starting transfers between devices, per_device(): lax.all_to_all(pieces, ('wide', 'narrow'), split_axis=0, concat_axis=0, t...  10.2 us
    ppermute x7, starting transfers between devices, swap_near(): return lax.ppermute(array, ('wide', 'narrow'), pairs)  7.84 us
    pallas_call x1, Pallas kernels, along_y_near(): pl.pallas_call(functools.partial(near_kernel, near, narrow), grid=(far,),...  7.48 us
  transfers between devices with their start and end apart: 15, of which 8 were waited for; matrix products, arithmetic and copies ran while one was open for 2% of the time, Pallas kernels for 25%

profile of v4, /device:TPU:8, one launch (start us, length us, event | category | flops | bytes accessed | tf_op | source)
XLA Modules:
  0.0 221.9 jit_solution(588605330596751543)
XLA Ops:
  0.0 3.1 %shard_map.73 = (f32[4,32,512]{2,1,0:T(8,128)}, bf16[256,512]{1,0:T(8,128)(2,1)}, bf16[256,512]{1,0:T(8,128)(2,1)}) custom-call(bf16[3,32,256,512]{3,2,1,0:T(8,128)(2,1)} %low.3, bf16[3,32,256,512]{3,2,1,0:T(8,128)(2,1)} %low.3, s32[32,256,512]{2,1,0:T(8,128)} %high_counts.5, s32[32,256,512]{2,1,0:T(8,128)} %high_counts.5, bf16[3,32,256,512]{3,2,1,0:T(8,128)(2,1)} %low.3, ...), custom_call_target="tpu_custom_call" | custom-call | tf_op jit(solution)/shard_map/pallas_call | solution.py:347
  3.1 3.7 %all-to-all-start = ((f32[4,32,512]{2,1,0:T(8,128)}), f32[4,32,512]{2,1,0:T(8,128)S(1)}, u32[]{:S(2)}, u32[]{:S(2)}) async-start(f32[4,32,512]{2,1,0:T(8,128)} %get-tuple-element.24), calls=%async_computation | async-start | bytes 524288 | tf_op jit(solution)/shard_map/all_to_all | solution.py:373
  6.9 1.9 collective-permute-start
  8.8 2.4 %collective-permute-start.1 = (bf16[256,512]{1,0:T(8,128)(2,1)}, bf16[256,512]{1,0:T(8,128)(2,1)S(1)}, u32[]{:S(2)}, u32[]{:S(2)}) collective-permute-start(bf16[256,512]{1,0:T(8,128)(2,1)} %get-tuple-element.26), channel_id=1, source_target_pairs={{0,4},{4,8},{8,12},{12,16},{16,20},{20,24},{24,28},{1,5},{5,9},{9,... | collective-permute-start | bytes 786440 | tf_op jit(solution)/shard_map/ppermute | solution.py:374
  12.9 8.8 %shard_map.74 = bf16[32,8,16,256]{3,2,1,0:T(8,128)(2,1)} custom-call(bf16[3,32,256,512]{3,2,1,0:T(8,128)(2,1)} %low.3, s32[32,256,512]{2,1,0:T(8,128)} %high_counts.5, f32[4,32,512]{2,1,0:T(8,128)} %copy-done.1, bf16[3,32,256,512]{3,2,1,0:T(8,128)(2,1)} %low.3, bf16[3,32,256,512]{3,2,1,0:T(8,128)(2,1)} %low.3, s32[32,256,512]{2,1,0:T(8,128)} %high_counts.5, ...), custom_call_target="tpu_custom_call" | custom-call | flops 1073741824 | bytes 12582912 | tf_op jit(solution)/shard_map/pallas_call | solution.py:177
  21.8 5.5 %all-to-all-start.2 = ((bf16[32,8,16,256]{3,2,1,0:T(8,128)(2,1)}), bf16[32,8,16,256]{3,2,1,0:T(8,128)(2,1)S(1)}, u32[]{:S(2)}, u32[]{:S(2)}) async-start(bf16[32,8,16,256]{3,2,1,0:T(8,128)(2,1)} %shard_map.74), calls=%async_computation.2 | async-start | bytes 4194304 | tf_op jit(solution)/shard_map/all_to_all | solution.py:396
  27.3 9.9 %shard_map.75 = (bf16[1,8,64,256]{3,2,1,0:T(8,128)(2,1)}, bf16[1,8,64,256]{3,2,1,0:T(8,128)(2,1)}, bf16[1,8,64,256]{3,2,1,0:T(8,128)(2,1)}, bf16[1,8,64,256]{3,2...) custom-call(bf16[3,32,256,512]{3,2,1,0:T(8,128)(2,1)} %low.3, ...), custom_call_target="tpu_custom_call" | custom-call | flops 1073741824 | bytes 12582912 | tf_op jit(solution)/shard_map/pallas_call | solution.py:177
  37.2 13.7 %shard_map.76 = bf16[32,16,16,256]{3,2,1,0:T(8,128)(2,1)} custom-call(bf16[3,32,256,512]{3,2,1,0:T(8,128)(2,1)} %low.3, s32[32,256,512]{2,1,0:T(8,128)} %high_counts.5, f32[4,32,512]{2,1,0:T(8,128)} %copy-done.1, bf16[3,32,256,512]{3,2,1,0:T(8,128)(2,1)} %low.3, bf16[256,512]{1,0:T(8,128)(2,1)} %copy-done.3, s32[32,256,512]{2,1,0:T(8,128)} %high_counts.5, ...), custom_call_target="tpu_custom_call" | custom-call | flops 2147483648 | bytes 25165824 | tf_op jit(solution)/shard_map/pallas_call | solution.py:177
  50.9 24.8 %all-to-all-done.2.tiles = bf16[32,8,16,256]{3,2,1,0:T(8,128)(2,1)S(1)} async-done(((bf16[32,8,16,256]{3,2,1,0:T(8,128)(2,1)}), bf16[32,8,16,256]{3,2,1,0:T(8,128)(2,1)S(1)}, u32[]{:S(2)}, u32[]{:S(2)}) %all-to-all-start.2) | async-done | bytes 2097184 | tf_op jit(solution)/shard_map/all_to_all | solution.py:396
  75.7 4.7 %all-to-all-start.1 = ((bf16[32,16,16,256]{3,2,1,0:T(8,128)(2,1)}), bf16[32,16,16,256]{3,2,1,0:T(8,128)(2,1)}, u32[]{:S(2)}, u32[]{:S(2)}) async-start(bf16[32,16,16,256]{3,2,1,0:T(8,128)(2,1)} %shard_map.76), calls=%async_computation.1 | async-start | bytes 8388608 | tf_op jit(solution)/shard_map/all_to_all | solution.py:402
  80.4 1.5 collective-permute-start.2
  82.0 1.5 collective-permute-start.3
  84.0 1.6 collective-permute-start.6
  85.6 29.4 %collective-permute-done.2.refs_1_ = bf16[8,64,256]{2,1,0:T(8,128)(2,1)S(1)} collective-permute-done((bf16[8,64,256]{2,1,0:T(8,128)(2,1)}, bf16[8,64,256]{2,1,0:T(8,128)(2,1)S(1)}, u32[]{:S(2)}, u32[]{:S(2)}) %collective-permute-start.2) | collective-permute-done | bytes 262176 | tf_op jit(solution)/shard_map/ppermute | solution.py:327
  115.0 2.7 %collective-permute-start.8 = (bf16[8,64,256]{2,1,0:T(8,128)(2,1)S(1)}, bf16[8,64,256]{2,1,0:T(8,128)(2,1)}, u32[]{:S(2)}, u32[]{:S(2)}) collective-permute-start(bf16[8,64,256]{2,1,0:T(8,128)(2,1)S(1)} %bitcast.11), channel_id=1, source_target_pairs={{0,7},{1,6},{2,5},{3,4},{4,3},{5,2},{6,1},{7,0},{8,15},{9,14},{10,... | collective-permute-start | bytes 786440 | tf_op jit(solution)/shard_map/ppermute | solution.py:327
  117.8 7.2 %collective-permute-done.4.refs_3_ = bf16[8,64,256]{2,1,0:T(8,128)(2,1)} collective-permute-done((bf16[8,64,256]{2,1,0:T(8,128)(2,1)}, bf16[8,64,256]{2,1,0:T(8,128)(2,1)}, u32[]{:S(2)}, u32[]{:S(2)}) %collective-permute-start.4) | collective-permute-done | bytes 262176 | tf_op jit(solution)/shard_map/ppermute | solution.py:327
  124.9 9.3 %collective-permute-done.6.refs_5_ = bf16[8,64,256]{2,1,0:T(8,128)(2,1)} collective-permute-done((bf16[8,64,256]{2,1,0:T(8,128)(2,1)S(1)}, bf16[8,64,256]{2,1,0:T(8,128)(2,1)}, u32[]{:S(2)}, u32[]{:S(2)}) %collective-permute-start.6) | collective-permute-done | bytes 262176 | tf_op jit(solution)/shard_map/ppermute | solution.py:327
  134.2 13.1 %collective-permute-done.7.refs_6_ = bf16[8,64,256]{2,1,0:T(8,128)(2,1)} collective-permute-done((bf16[8,64,256]{2,1,0:T(8,128)(2,1)S(1)}, bf16[8,64,256]{2,1,0:T(8,128)(2,1)}, u32[]{:S(2)}, u32[]{:S(2)}) %collective-permute-start.7) | collective-permute-done | bytes 262176 | tf_op jit(solution)/shard_map/ppermute | solution.py:327
  147.4 7.5 %shard_map.77 = (bf16[16,16,1024]{2,1,0:T(8,128)(2,1)}, bf16[16,16,1024]{2,1,0:T(8,128)(2,1)}, bf16[16,16,1024]{2,1,0:T(8,128)(2,1)}, bf16[16,16,1024]{2,1,0:T(8,128)(2,1)}) custom-call(bf16[8,64,256]{2,1,0:T(8,128)(2,1)} %bitcast.10, bf16[8,64,256]{2,1,0:T(8,128)(2,1)} %copy-done.9, bf16[8,64,256]{2,1,0:T(8,128)(2,1)} %copy-done.10, ...), custom_call_target="tpu_custom_call" | custom-call | flops 2415919104 | bytes 4194304 | tf_op jit(solution)/shard_map/pallas_call | solution.py:267
  154.9 2.7 %collective-permute-start.10 = (bf16[16,16,1024]{2,1,0:T(8,128)(2,1)}, bf16[16,16,1024]{2,1,0:T(8,128)(2,1)S(1)}, u32[]{:S(2)}, u32[]{:S(2)}) collective-permute-start(bf16[16,16,1024]{2,1,0:T(8,128)(2,1)} %get-tuple-element.41), channel_id=1, source_target_pairs={{0,16},{1,17},{2,18},{3,19},{4,20},{5,21},{6,22},{7,23},{8,24},{9,... | collective-permute-start | bytes 1572872 | tf_op jit(solution)/shard_map/ppermute | solution.py:319
  158.4 6.0 %shard_map.78.rest_0_ = bf16[16,8,32,1024]{3,2,1,0:T(8,128)(2,1)} custom-call(bf16[32,8,16,256]{3,2,1,0:T(8,128)(2,1)} %copy-done, bf16[1024,1024]{1,0:T(8,128)(2,1)} %constant.91.clone.refs_8_.table, bf16[128,128]{1,0:T(8,128)(2,1)} %constant.92.clone.refs_9_.order), custom_call_target="tpu_custom_call" | custom-call | flops 2415919104 | bytes 4194304 | tf_op jit(solution)/shard_map/pallas_call | solution.py:298
  164.4 30.7 %all-to-all-done.1.tiles = bf16[32,16,16,256]{3,2,1,0:T(8,128)(2,1)} async-done(((bf16[32,16,16,256]{3,2,1,0:T(8,128)(2,1)}), bf16[32,16,16,256]{3,2,1,0:T(8,128)(2,1)}, u32[]{:S(2)}, u32[]{:S(2)}) %all-to-all-start.1) | async-done | bytes 4194336 | tf_op jit(solution)/shard_map/all_to_all | solution.py:402
  195.1 9.1 %shard_map.79 = bf16[16,8,32,1024]{3,2,1,0:T(8,128)(2,1)} custom-call(bf16[32,16,16,256]{3,2,1,0:T(8,128)(2,1)} %all-to-all-done.1.tiles, bf16[1024,1024]{1,0:T(8,128)(2,1)} %constant.91.clone.refs_8_.table, bf16[256,256]{1,0:T(8,128)(2,1)} %constant.93.clone.order, bf16[16,8,32,1024]{3,2,1,0:T(8,128)(2,1)} %shard_map.78.rest_0_), custom_call_target="tpu_custom_call", output_to_operand_aliasing={{}: (3, {})} | custom-call | flops 5368709120 | bytes 8388608 | tf_op jit(solution)/shard_map/pallas_call | solution.py:298
  208.6 11.9 %collective-permute-done.11 = bf16[16,16,1024]{2,1,0:T(8,128)(2,1)S(1)} collective-permute-done((bf16[16,16,1024]{2,1,0:T(8,128)(2,1)}, bf16[16,16,1024]{2,1,0:T(8,128)(2,1)S(1)}, u32[]{:S(2)}, u32[]{:S(2)}) %collective-permute-start.11) | collective-permute-done | bytes 524320 | tf_op jit(solution)/shard_map/ppermute | solution.py:319
  (43 shorter events, 9.0 us)
Async XLA Ops:
  3.1 9.1 %all-to-all-start = ((f32[4,32,512]{2,1,0:T(8,128)}), f32[4,32,512]{2,1,0:T(8,128)S(1)}, u32[]{:S(2)}, u32[]{:S(2)}) async-start(f32[4,32,512]{2,1,0:T(8,128)} %get-tuple-element.24), calls=%async_computation | async-start | bytes 524288 | tf_op jit(solution)/shard_map/all_to_all | solution.py:373
  6.9 14.9 %collective-permute-start = (bf16[256,512]{1,0:T(8,128)(2,1)}, bf16[256,512]{1,0:T(8,128)(2,1)S(1)}, u32[]{:S(2)}, u32[]{:S(2)}) collective-permute-start(bf16[256,512]{1,0:T(8,128)(2,1)} %get-tuple-element.25), channel_id=1, source_target_pairs={{4,0},{8,4},{12,8},{16,12},{20,16},{24,20},{28,24},{5,1},{9,5},{13... | collective-permute-start | bytes 786440 | tf_op jit(solution)/shard_map/ppermute | solution.py:375
  8.8 13.0 %collective-permute-start.1 = (bf16[256,512]{1,0:T(8,128)(2,1)}, bf16[256,512]{1,0:T(8,128)(2,1)S(1)}, u32[]{:S(2)}, u32[]{:S(2)}) collective-permute-start(bf16[256,512]{1,0:T(8,128)(2,1)} %get-tuple-element.26), channel_id=1, source_target_pairs={{0,4},{4,8},{8,12},{12,16},{16,20},{20,24},{24,28},{1,5},{5,9},{9,... | collective-permute-start | bytes 786440 | tf_op jit(solution)/shard_map/ppermute | solution.py:374
  21.7 15.5 %copy-start.3 = (bf16[256,512]{1,0:T(8,128)(2,1)}, bf16[256,512]{1,0:T(8,128)(2,1)S(1)}, u32[]{:S(2)}) copy-start(bf16[256,512]{1,0:T(8,128)(2,1)S(1)} %collective-permute-done.high) | copy-start | bytes 786436
  21.8 5.5 %copy-start.4 = (bf16[256,512]{1,0:T(8,128)(2,1)}, bf16[256,512]{1,0:T(8,128)(2,1)S(1)}, u32[]{:S(2)}) copy-start(bf16[256,512]{1,0:T(8,128)(2,1)S(1)} %collective-permute-done.1.low) | copy-start | bytes 786436
  21.8 53.9 %all-to-all-start.2 = ((bf16[32,8,16,256]{3,2,1,0:T(8,128)(2,1)}), bf16[32,8,16,256]{3,2,1,0:T(8,128)(2,1)S(1)}, u32[]{:S(2)}, u32[]{:S(2)}) async-start(bf16[32,8,16,256]{3,2,1,0:T(8,128)(2,1)} %shard_map.74), calls=%async_computation.2 | async-start | bytes 4194304 | tf_op jit(solution)/shard_map/all_to_all | solution.py:396
  50.9 33.1 %copy-start.8 = (bf16[1,8,64,256]{3,2,1,0:T(8,128)(2,1)S(1)}, bf16[1,8,64,256]{3,2,1,0:T(8,128)(2,1)}, u32[]{:S(2)}) copy-start(bf16[1,8,64,256]{3,2,1,0:T(8,128)(2,1)} %get-tuple-element.34) | copy-start | bytes 786436
  50.9 33.1 %copy-start.7 = (bf16[1,8,64,256]{3,2,1,0:T(8,128)(2,1)S(1)}, bf16[1,8,64,256]{3,2,1,0:T(8,128)(2,1)}, u32[]{:S(2)}) copy-start(bf16[1,8,64,256]{3,2,1,0:T(8,128)(2,1)} %get-tuple-element.35) | copy-start | bytes 786436
  50.9 64.1 %copy-start.6 = (bf16[1,8,64,256]{3,2,1,0:T(8,128)(2,1)S(1)}, bf16[1,8,64,256]{3,2,1,0:T(8,128)(2,1)}, u32[]{:S(2)}) copy-start(bf16[1,8,64,256]{3,2,1,0:T(8,128)(2,1)} %get-tuple-element.36) | copy-start | bytes 786436
  50.9 64.1 %copy-start.5 = (bf16[1,8,64,256]{3,2,1,0:T(8,128)(2,1)S(1)}, bf16[1,8,64,256]{3,2,1,0:T(8,128)(2,1)}, u32[]{:S(2)}) copy-start(bf16[1,8,64,256]{3,2,1,0:T(8,128)(2,1)} %get-tuple-element.37) | copy-start | bytes 786436
  75.7 79.1 %copy-start = (bf16[32,8,16,256]{3,2,1,0:T(8,128)(2,1)}, bf16[32,8,16,256]{3,2,1,0:T(8,128)(2,1)S(1)}, u32[]{:S(2)}) copy-start(bf16[32,8,16,256]{3,2,1,0:T(8,128)(2,1)S(1)} %all-to-all-done.2.tiles) | copy-start | bytes 6291460
  75.7 119.4 %all-to-all-start.1 = ((bf16[32,16,16,256]{3,2,1,0:T(8,128)(2,1)}), bf16[32,16,16,256]{3,2,1,0:T(8,128)(2,1)}, u32[]{:S(2)}, u32[]{:S(2)}) async-start(bf16[32,16,16,256]{3,2,1,0:T(8,128)(2,1)} %shard_map.76), calls=%async_computation.1 | async-start | bytes 8388608 | tf_op jit(solution)/shard_map/all_to_all | solution.py:402
  80.4 34.6 %collective-permute-start.2 = (bf16[8,64,256]{2,1,0:T(8,128)(2,1)}, bf16[8,64,256]{2,1,0:T(8,128)(2,1)S(1)}, u32[]{:S(2)}, u32[]{:S(2)}) collective-permute-start(bf16[8,64,256]{2,1,0:T(8,128)(2,1)} %bitcast.17), channel_id=1, source_target_pairs={{0,1},{1,0},{2,3},{3,2},{4,5},{5,4},{6,7},{7,6},{8,9},{9,8},{10,11... | collective-permute-start | bytes 786440 | tf_op jit(solution)/shard_map/ppermute | solution.py:327
  82.0 33.1 %collective-permute-start.3 = (bf16[8,64,256]{2,1,0:T(8,128)(2,1)}, bf16[8,64,256]{2,1,0:T(8,128)(2,1)S(1)}, u32[]{:S(2)}, u32[]{:S(2)}) collective-permute-start(bf16[8,64,256]{2,1,0:T(8,128)(2,1)} %bitcast.16), channel_id=1, source_target_pairs={{0,2},{1,3},{2,0},{3,1},{4,6},{5,7},{6,4},{7,5},{8,10},{9,11},{10,... | collective-permute-start | bytes 786440 | tf_op jit(solution)/shard_map/ppermute | solution.py:327
  83.4 41.5 %collective-permute-start.4 = (bf16[8,64,256]{2,1,0:T(8,128)(2,1)}, bf16[8,64,256]{2,1,0:T(8,128)(2,1)}, u32[]{:S(2)}, u32[]{:S(2)}) collective-permute-start(bf16[8,64,256]{2,1,0:T(8,128)(2,1)} %bitcast.15), channel_id=1, source_target_pairs={{0,3},{1,2},{2,1},{3,0},{4,7},{5,6},{6,5},{7,4},{8,11},{9,10},{10,... | collective-permute-start | bytes 786440 | tf_op jit(solution)/shard_map/ppermute | solution.py:327
  84.0 41.0 %collective-permute-start.5 = (bf16[8,64,256]{2,1,0:T(8,128)(2,1)S(1)}, bf16[8,64,256]{2,1,0:T(8,128)(2,1)}, u32[]{:S(2)}, u32[]{:S(2)}) collective-permute-start(bf16[8,64,256]{2,1,0:T(8,128)(2,1)S(1)} %bitcast.14), channel_id=1, source_target_pairs={{0,4},{1,5},{2,6},{3,7},{4,0},{5,1},{6,2},{7,3},{8,12},{9,13},{10,... | collective-permute-start | bytes 786440 | tf_op jit(solution)/shard_map/ppermute | solution.py:327
  84.0 50.3 %collective-permute-start.6 = (bf16[8,64,256]{2,1,0:T(8,128)(2,1)S(1)}, bf16[8,64,256]{2,1,0:T(8,128)(2,1)}, u32[]{:S(2)}, u32[]{:S(2)}) collective-permute-start(bf16[8,64,256]{2,1,0:T(8,128)(2,1)S(1)} %bitcast.13), channel_id=1, source_target_pairs={{0,5},{1,4},{2,7},{3,6},{4,1},{5,0},{6,3},{7,2},{8,13},{9,12},{10,... | collective-permute-start | bytes 786440 | tf_op jit(solution)/shard_map/ppermute | solution.py:327
  115.0 32.3 %copy-start.9 = (bf16[8,64,256]{2,1,0:T(8,128)(2,1)}, bf16[8,64,256]{2,1,0:T(8,128)(2,1)S(1)}, u32[]{:S(2)}) copy-start(bf16[8,64,256]{2,1,0:T(8,128)(2,1)S(1)} %collective-permute-done.2.refs_1_) | copy-start | bytes 786436
  115.0 32.3 %collective-permute-start.7 = (bf16[8,64,256]{2,1,0:T(8,128)(2,1)S(1)}, bf16[8,64,256]{2,1,0:T(8,128)(2,1)}, u32[]{:S(2)}, u32[]{:S(2)}) collective-permute-start(bf16[8,64,256]{2,1,0:T(8,128)(2,1)S(1)} %bitcast.12), channel_id=1, source_target_pairs={{0,6},{1,7},{2,4},{3,5},{4,2},{5,3},{6,0},{7,1},{8,14},{9,15},{10,... | collective-permute-start | bytes 786440 | tf_op jit(solution)/shard_map/ppermute | solution.py:327
  115.0 32.3 %collective-permute-start.8 = (bf16[8,64,256]{2,1,0:T(8,128)(2,1)S(1)}, bf16[8,64,256]{2,1,0:T(8,128)(2,1)}, u32[]{:S(2)}, u32[]{:S(2)}) collective-permute-start(bf16[8,64,256]{2,1,0:T(8,128)(2,1)S(1)} %bitcast.11), channel_id=1, source_target_pairs={{0,7},{1,6},{2,5},{3,4},{4,3},{5,2},{6,1},{7,0},{8,15},{9,14},{10,... | collective-permute-start | bytes 786440 | tf_op jit(solution)/shard_map/ppermute | solution.py:327
  154.8 50.8 %collective-permute-start.9 = (bf16[16,16,1024]{2,1,0:T(8,128)(2,1)}, bf16[16,16,1024]{2,1,0:T(8,128)(2,1)S(1)}, u32[]{:S(2)}, u32[]{:S(2)}) collective-permute-start(bf16[16,16,1024]{2,1,0:T(8,128)(2,1)} %get-tuple-element.40), channel_id=1, source_target_pairs={{0,8},{1,9},{2,10},{3,11},{4,12},{5,13},{6,14},{7,15},{8,0},{9,1},... | collective-permute-start | bytes 1572872 | tf_op jit(solution)/shard_map/ppermute | solution.py:319
  154.9 52.2 %collective-permute-start.10 = (bf16[16,16,1024]{2,1,0:T(8,128)(2,1)}, bf16[16,16,1024]{2,1,0:T(8,128)(2,1)S(1)}, u32[]{:S(2)}, u32[]{:S(2)}) collective-permute-start(bf16[16,16,1024]{2,1,0:T(8,128)(2,1)} %get-tuple-element.41), channel_id=1, source_target_pairs={{0,16},{1,17},{2,18},{3,19},{4,20},{5,21},{6,22},{7,23},{8,24},{9,... | collective-permute-start | bytes 1572872 | tf_op jit(solution)/shard_map/ppermute | solution.py:319
  157.6 62.9 %collective-permute-start.11 = (bf16[16,16,1024]{2,1,0:T(8,128)(2,1)}, bf16[16,16,1024]{2,1,0:T(8,128)(2,1)S(1)}, u32[]{:S(2)}, u32[]{:S(2)}) collective-permute-start(bf16[16,16,1024]{2,1,0:T(8,128)(2,1)} %get-tuple-element.42), channel_id=1, source_target_pairs={{0,24},{1,25},{2,26},{3,27},{4,28},{5,29},{6,30},{7,31},{8,16},{9,... | collective-permute-start | bytes 1572872 | tf_op jit(solution)/shard_map/ppermute | solution.py:319
  164.4 39.8 %copy-start.2 = (bf16[16,16,1024]{2,1,0:T(8,128)(2,1)S(1)}, bf16[16,16,1024]{2,1,0:T(8,128)(2,1)}, u32[]{:S(2)}) copy-start(bf16[16,16,1024]{2,1,0:T(8,128)(2,1)} %get-tuple-element.38) | copy-start | bytes 1572868
  (2 other events, 3.4 us)

commit v5 on v4

--- a/solution.py
+++ b/solution.py
@@ -226,6 +226,13 @@
     return moved
 
 
+def pick(parts, chosen):
+    picked = parts[0]
+    for part, here in zip(parts[1:], chosen[1:]):
+        picked = jnp.where(here, part, picked)
+    return picked
+
+
 def near_kernel(near, narrow, *refs):
     tiles, (table, order), (*outs, ordered) = refs[:near], refs[near:near + 2], refs[near + 2:]
     planes, _, rows = tiles[0].shape
@@ -237,12 +244,14 @@
             ordered[place * rows:(place + 1) * rows, :] = table[pl.ds(pl.multiple_of(owner * rows, rows), rows), :]
 
     moved = y_of([tiles[at:at + narrow] for at in range(0, near, narrow)], ordered, order)
+    own = device() % near // narrow
+    moved = [pick(moved, [own == partner(turn, core) for turn in range(len(moved))]) for core in range(len(moved))]
     for step, out in enumerate(outs):
 
         @pl.when(pl.program_id(0) == step)
         def _():
             for core, part in enumerate(moved):
-                out[:, core * planes:(core + 1) * planes, :] = part
+                out[:, core] = part
 
 
 def far_kernel(narrow, tiles, table, order, *rest):
@@ -271,8 +280,8 @@
             pl.BlockSpec(table.shape, lambda step: (0, 0)),
             pl.BlockSpec((count, count), lambda step: (0, 0)),
         ],
-        out_specs=[pl.BlockSpec((slab, cores * planes, full_y), lambda step: (0, 0, 0))] * far,
-        out_shape=[jax.ShapeDtypeStruct((slab, cores * planes, full_y), jnp.bfloat16)] * far,
+        out_specs=[pl.BlockSpec((slab, cores, planes, full_y), lambda step: (0, 0, 0, 0))] * far,
+        out_shape=[jax.ShapeDtypeStruct((slab, cores, planes, full_y), jnp.bfloat16)] * far,
         scratch_shapes=[pltpu.VMEM(table.shape, jnp.bfloat16)],
         compiler_params=pltpu.CompilerParams(vmem_limit_bytes=VMEM_BYTES),
         cost_estimate=y_cost(planes, slab, far * cores, full_y),
@@ -405,13 +414,11 @@
         far_pieces = [swap_far(piece, step, near) for step, piece in enumerate(far_pieces)]
         spectrum = along_y_far(arrived, table_y, None, first, total, narrow)
         spectrum = along_y_far(arrived_later, table_y, spectrum, second, total, narrow)
-        mine = device() // near
+        spectrum = spectrum.reshape(slab, wide, total, full_y)
         for step, piece in enumerate(far_pieces):
-            for turn in range(cores):
-                core = partner(device() % near // narrow, turn)
-                at = (partner(mine, step) * cores + core) * total + third
-                spectrum = lax.dynamic_update_slice(spectrum, piece[:, turn * few:(turn + 1) * few], (0, at, 0))
-        return spectrum
+            at = partner(device() // near, step) * cores
+            spectrum = lax.dynamic_update_slice(spectrum, piece, (0, at, third, 0))
+        return spectrum.reshape(slab, wide * total, full_y)
     along = along_z_of(normals, counts, halos, table_z, 0, total)[0]
     along = along.reshape(total, wide * narrow, slab, rows)
     arrived = lax.all_to_all(along, ("wide", "narrow"), split_axis=1, concat_axis=1, tiled=True)

time: 222 us -> 222 us (level)
  local copies, waits for them, and re-layouts: 6.53 us -> 4.1 us
    dynamic_update_slice x8 -> x4, local copies, waits for them, and re-layouts: 5.78 us -> 3.36 us  [per_device(): spectrum = lax.dynamic_update_slice(spectrum, piece, (0, at, third, 0))]
  transfers between devices with their start and end apart: 15 -> 15, of which waited for: 8 -> 9; matrix products, arithmetic and copies ran while one was open for 2% -> 1% of each run, Pallas kernels for 25% -> 25%
where the time goes in v5:
time: 222 us; the launch traced here: 221 us
  waiting for transfers between devices  129 us (58%)
  Pallas kernels  58.2 us (26%)
  starting transfers between devices  29.6 us (13%)
  local copies, waits for them, and re-layouts  4.1 us (2%)
    ppermute x7, waiting for transfers between devices, swap_near(): return lax.ppermute(array, ('wide', 'narrow'), pairs)  59 us
    all_to_all x2, waiting for transfers between devices, per_device(): lax.all_to_all(pieces, ('wide', 'narrow'), split_axis=0, concat_axis=0, t...  55.5 us
    pallas_call x3, Pallas kernels, along_z_of(): pl.pallas_call(functools.partial(planes_kernel, start, planes, total, blo...  32.4 us
    pallas_call x2, Pallas kernels, along_y_far(): pl.pallas_call(functools.partial(far_kernel, narrow), grid=(wide // group...  15.1 us
    ppermute x3, waiting for transfers between devices, swap_far(): return lax.ppermute(array, ('wide', 'narrow'), pairs)  13.7 us
    all_to_all x2, starting transfers between devices, per_device(): lax.all_to_all(pieces, ('wide', 'narrow'), split_axis=0, concat_axis=0, t...  10.2 us
    ppermute x7, starting transfers between devices, swap_near(): return lax.ppermute(array, ('wide', 'narrow'), pairs)  7.84 us
    pallas_call x1, Pallas kernels, along_y_near(): pl.pallas_call(functools.partial(near_kernel, near, narrow), grid=(far,),...  7.49 us
  transfers between devices with their start and end apart: 15, of which 9 were waited for; matrix products, arithmetic and copies ran while one was open for 1% of the time, Pallas kernels for 25%

profile of v5, /device:TPU:8, one launch (start us, length us, event | category | flops | bytes accessed | tf_op | source)
XLA Modules:
  0.0 221.3 jit_solution(11381187672960965609)
XLA Ops:
  0.0 3.1 %shard_map.73 = (f32[4,32,512]{2,1,0:T(8,128)}, bf16[256,512]{1,0:T(8,128)(2,1)}, bf16[256,512]{1,0:T(8,128)(2,1)}) custom-call(bf16[3,32,256,512]{3,2,1,0:T(8,128)(2,1)} %low.3, bf16[3,32,256,512]{3,2,1,0:T(8,128)(2,1)} %low.3, s32[32,256,512]{2,1,0:T(8,128)} %high_counts.5, s32[32,256,512]{2,1,0:T(8,128)} %high_counts.5, bf16[3,32,256,512]{3,2,1,0:T(8,128)(2,1)} %low.3, ...), custom_call_target="tpu_custom_call" | custom-call | tf_op jit(solution)/shard_map/pallas_call | solution.py:356
  3.1 3.7 %all-to-all-start = ((f32[4,32,512]{2,1,0:T(8,128)}), f32[4,32,512]{2,1,0:T(8,128)S(1)}, u32[]{:S(2)}, u32[]{:S(2)}) async-start(f32[4,32,512]{2,1,0:T(8,128)} %get-tuple-element.24), calls=%async_computation | async-start | bytes 524288 | tf_op jit(solution)/shard_map/all_to_all | solution.py:382
  6.9 1.9 collective-permute-start
  8.8 2.4 %collective-permute-start.1 = (bf16[256,512]{1,0:T(8,128)(2,1)}, bf16[256,512]{1,0:T(8,128)(2,1)S(1)}, u32[]{:S(2)}, u32[]{:S(2)}) collective-permute-start(bf16[256,512]{1,0:T(8,128)(2,1)} %get-tuple-element.26), channel_id=1, source_target_pairs={{0,4},{4,8},{8,12},{12,16},{16,20},{20,24},{24,28},{1,5},{5,9},{9,... | collective-permute-start | bytes 786440 | tf_op jit(solution)/shard_map/ppermute | solution.py:383
  12.9 8.8 %shard_map.74 = bf16[32,8,16,256]{3,2,1,0:T(8,128)(2,1)} custom-call(bf16[3,32,256,512]{3,2,1,0:T(8,128)(2,1)} %low.3, s32[32,256,512]{2,1,0:T(8,128)} %high_counts.5, f32[4,32,512]{2,1,0:T(8,128)} %copy-done.1, bf16[3,32,256,512]{3,2,1,0:T(8,128)(2,1)} %low.3, bf16[3,32,256,512]{3,2,1,0:T(8,128)(2,1)} %low.3, s32[32,256,512]{2,1,0:T(8,128)} %high_counts.5, ...), custom_call_target="tpu_custom_call" | custom-call | flops 1073741824 | bytes 12582912 | tf_op jit(solution)/shard_map/pallas_call | solution.py:177
  21.8 5.5 %all-to-all-start.2 = ((bf16[32,8,16,256]{3,2,1,0:T(8,128)(2,1)}), bf16[32,8,16,256]{3,2,1,0:T(8,128)(2,1)S(1)}, u32[]{:S(2)}, u32[]{:S(2)}) async-start(bf16[32,8,16,256]{3,2,1,0:T(8,128)(2,1)} %shard_map.74), calls=%async_computation.2 | async-start | bytes 4194304 | tf_op jit(solution)/shard_map/all_to_all | solution.py:405
  27.3 9.9 %shard_map.75 = (bf16[1,8,64,256]{3,2,1,0:T(8,128)(2,1)}, bf16[1,8,64,256]{3,2,1,0:T(8,128)(2,1)}, bf16[1,8,64,256]{3,2,1,0:T(8,128)(2,1)}, bf16[1,8,64,256]{3,2...) custom-call(bf16[3,32,256,512]{3,2,1,0:T(8,128)(2,1)} %low.3, ...), custom_call_target="tpu_custom_call" | custom-call | flops 1073741824 | bytes 12582912 | tf_op jit(solution)/shard_map/pallas_call | solution.py:177
  37.2 13.7 %shard_map.76 = bf16[32,16,16,256]{3,2,1,0:T(8,128)(2,1)} custom-call(bf16[3,32,256,512]{3,2,1,0:T(8,128)(2,1)} %low.3, s32[32,256,512]{2,1,0:T(8,128)} %high_counts.5, f32[4,32,512]{2,1,0:T(8,128)} %copy-done.1, bf16[3,32,256,512]{3,2,1,0:T(8,128)(2,1)} %low.3, bf16[256,512]{1,0:T(8,128)(2,1)} %copy-done.3, s32[32,256,512]{2,1,0:T(8,128)} %high_counts.5, ...), custom_call_target="tpu_custom_call" | custom-call | flops 2147483648 | bytes 25165824 | tf_op jit(solution)/shard_map/pallas_call | solution.py:177
  50.9 24.8 %all-to-all-done.2.tiles = bf16[32,8,16,256]{3,2,1,0:T(8,128)(2,1)S(1)} async-done(((bf16[32,8,16,256]{3,2,1,0:T(8,128)(2,1)}), bf16[32,8,16,256]{3,2,1,0:T(8,128)(2,1)S(1)}, u32[]{:S(2)}, u32[]{:S(2)}) %all-to-all-start.2) | async-done | bytes 2097184 | tf_op jit(solution)/shard_map/all_to_all | solution.py:405
  75.7 4.7 %all-to-all-start.1 = ((bf16[32,16,16,256]{3,2,1,0:T(8,128)(2,1)}), bf16[32,16,16,256]{3,2,1,0:T(8,128)(2,1)}, u32[]{:S(2)}, u32[]{:S(2)}) async-start(bf16[32,16,16,256]{3,2,1,0:T(8,128)(2,1)} %shard_map.76), calls=%async_computation.1 | async-start | bytes 8388608 | tf_op jit(solution)/shard_map/all_to_all | solution.py:411
  80.4 1.5 collective-permute-start.2
  82.0 1.5 collective-permute-start.3
  84.0 1.6 collective-permute-start.6
  85.6 29.4 %collective-permute-done.2.refs_1_ = bf16[8,64,256]{2,1,0:T(8,128)(2,1)S(1)} collective-permute-done((bf16[8,64,256]{2,1,0:T(8,128)(2,1)}, bf16[8,64,256]{2,1,0:T(8,128)(2,1)S(1)}, u32[]{:S(2)}, u32[]{:S(2)}) %collective-permute-start.2) | collective-permute-done | bytes 262176 | tf_op jit(solution)/shard_map/ppermute | solution.py:336
  115.0 2.7 %collective-permute-start.8 = (bf16[8,64,256]{2,1,0:T(8,128)(2,1)S(1)}, bf16[8,64,256]{2,1,0:T(8,128)(2,1)}, u32[]{:S(2)}, u32[]{:S(2)}) collective-permute-start(bf16[8,64,256]{2,1,0:T(8,128)(2,1)S(1)} %bitcast.10), channel_id=1, source_target_pairs={{0,7},{1,6},{2,5},{3,4},{4,3},{5,2},{6,1},{7,0},{8,15},{9,14},{10,... | collective-permute-start | bytes 786440 | tf_op jit(solution)/shard_map/ppermute | solution.py:336
  117.8 7.2 %collective-permute-done.4.refs_3_ = bf16[8,64,256]{2,1,0:T(8,128)(2,1)} collective-permute-done((bf16[8,64,256]{2,1,0:T(8,128)(2,1)}, bf16[8,64,256]{2,1,0:T(8,128)(2,1)}, u32[]{:S(2)}, u32[]{:S(2)}) %collective-permute-start.4) | collective-permute-done | bytes 262176 | tf_op jit(solution)/shard_map/ppermute | solution.py:336
  124.9 9.3 %collective-permute-done.6.refs_5_ = bf16[8,64,256]{2,1,0:T(8,128)(2,1)} collective-permute-done((bf16[8,64,256]{2,1,0:T(8,128)(2,1)S(1)}, bf16[8,64,256]{2,1,0:T(8,128)(2,1)}, u32[]{:S(2)}, u32[]{:S(2)}) %collective-permute-start.6) | collective-permute-done | bytes 262176 | tf_op jit(solution)/shard_map/ppermute | solution.py:336
  134.2 13.1 %collective-permute-done.7.refs_6_ = bf16[8,64,256]{2,1,0:T(8,128)(2,1)} collective-permute-done((bf16[8,64,256]{2,1,0:T(8,128)(2,1)S(1)}, bf16[8,64,256]{2,1,0:T(8,128)(2,1)}, u32[]{:S(2)}, u32[]{:S(2)}) %collective-permute-start.7) | collective-permute-done | bytes 262176 | tf_op jit(solution)/shard_map/ppermute | solution.py:336
  147.4 7.5 %shard_map.77 = (bf16[16,2,8,1024]{3,2,1,0:T(8,128)(2,1)}, bf16[16,2,8,1024]{3,2,1,0:T(8,128)(2,1)}, bf16[16,2,8,1024]{3,2,1,0:T(8,128)(2,1)}, bf16[16,2,8,1024]{3,2,1,0:T(8,128)(2,1)}) custom-call(bf16[8,64,256]{2,1,0:T(8,128)(2,1)} %bitcast.9, bf16[8,64,256]{2,1,0:T(8,128)(2,1)} %copy-done.9, bf16[8,64,256]{2,1,0:T(8,128)(2,1)} %copy-done.10, ...), custom_call_target="tpu_custom_call" | custom-call | flops 2415919104 | bytes 4194304 | tf_op jit(solution)/shard_map/pallas_call | solution.py:276
  154.9 2.7 %collective-permute-start.10 = (bf16[16,2,8,1024]{3,2,1,0:T(8,128)(2,1)}, bf16[16,2,8,1024]{3,2,1,0:T(8,128)(2,1)S(1)}, u32[]{:S(2)}, u32[]{:S(2)}) collective-permute-start(bf16[16,2,8,1024]{3,2,1,0:T(8,128)(2,1)} %get-tuple-element.41), channel_id=1, source_target_pairs={{0,16},{1,17},{2,18},{3,19},{4,20},{5,21},{6,22},{7,23},{8,24},{9,... | collective-permute-start | bytes 1572872 | tf_op jit(solution)/shard_map/ppermute | solution.py:328
  158.4 6.0 %shard_map.78.rest_0_ = bf16[16,8,32,1024]{3,2,1,0:T(8,128)(2,1)} custom-call(bf16[32,8,16,256]{3,2,1,0:T(8,128)(2,1)} %copy-done, bf16[1024,1024]{1,0:T(8,128)(2,1)} %constant.48.clone.refs_8_.table, bf16[128,128]{1,0:T(8,128)(2,1)} %constant.49.clone.refs_9_.order), custom_call_target="tpu_custom_call" | custom-call | flops 2415919104 | bytes 4194304 | tf_op jit(solution)/shard_map/pallas_call | solution.py:307
  164.4 30.7 %all-to-all-done.1.tiles = bf16[32,16,16,256]{3,2,1,0:T(8,128)(2,1)} async-done(((bf16[32,16,16,256]{3,2,1,0:T(8,128)(2,1)}), bf16[32,16,16,256]{3,2,1,0:T(8,128)(2,1)}, u32[]{:S(2)}, u32[]{:S(2)}) %all-to-all-start.1) | async-done | bytes 4194336 | tf_op jit(solution)/shard_map/all_to_all | solution.py:411
  195.1 9.1 %shard_map.79 = bf16[16,8,32,1024]{3,2,1,0:T(8,128)(2,1)} custom-call(bf16[32,16,16,256]{3,2,1,0:T(8,128)(2,1)} %all-to-all-done.1.tiles, bf16[1024,1024]{1,0:T(8,128)(2,1)} %constant.48.clone.refs_8_.table, bf16[256,256]{1,0:T(8,128)(2,1)} %constant.50.clone.order, bf16[16,8,32,1024]{3,2,1,0:T(8,128)(2,1)} %shard_map.78.rest_0_), custom_call_target="tpu_custom_call", output_to_operand_aliasing={{}: (3, {})} | custom-call | flops 5368709120 | bytes 8388608 | tf_op jit(solution)/shard_map/pallas_call | solution.py:307
  207.2 13.3 %collective-permute-done.11 = bf16[16,2,8,1024]{3,2,1,0:T(8,128)(2,1)S(1)} collective-permute-done((bf16[16,2,8,1024]{3,2,1,0:T(8,128)(2,1)}, bf16[16,2,8,1024]{3,2,1,0:T(8,128)(2,1)S(1)}, u32[]{:S(2)}, u32[]{:S(2)}) %collective-permute-start.11) | collective-permute-done | bytes 524320 | tf_op jit(solution)/shard_map/ppermute | solution.py:328
  (39 shorter events, 7.0 us)
Async XLA Ops:
  3.1 9.1 %all-to-all-start = ((f32[4,32,512]{2,1,0:T(8,128)}), f32[4,32,512]{2,1,0:T(8,128)S(1)}, u32[]{:S(2)}, u32[]{:S(2)}) async-start(f32[4,32,512]{2,1,0:T(8,128)} %get-tuple-element.24), calls=%async_computation | async-start | bytes 524288 | tf_op jit(solution)/shard_map/all_to_all | solution.py:382
  6.9 14.9 %collective-permute-start = (bf16[256,512]{1,0:T(8,128)(2,1)}, bf16[256,512]{1,0:T(8,128)(2,1)S(1)}, u32[]{:S(2)}, u32[]{:S(2)}) collective-permute-start(bf16[256,512]{1,0:T(8,128)(2,1)} %get-tuple-element.25), channel_id=1, source_target_pairs={{4,0},{8,4},{12,8},{16,12},{20,16},{24,20},{28,24},{5,1},{9,5},{13... | collective-permute-start | bytes 786440 | tf_op jit(solution)/shard_map/ppermute | solution.py:384
  8.8 13.0 %collective-permute-start.1 = (bf16[256,512]{1,0:T(8,128)(2,1)}, bf16[256,512]{1,0:T(8,128)(2,1)S(1)}, u32[]{:S(2)}, u32[]{:S(2)}) collective-permute-start(bf16[256,512]{1,0:T(8,128)(2,1)} %get-tuple-element.26), channel_id=1, source_target_pairs={{0,4},{4,8},{8,12},{12,16},{16,20},{20,24},{24,28},{1,5},{5,9},{9,... | collective-permute-start | bytes 786440 | tf_op jit(solution)/shard_map/ppermute | solution.py:383
  21.7 15.5 %copy-start.3 = (bf16[256,512]{1,0:T(8,128)(2,1)}, bf16[256,512]{1,0:T(8,128)(2,1)S(1)}, u32[]{:S(2)}) copy-start(bf16[256,512]{1,0:T(8,128)(2,1)S(1)} %collective-permute-done.high) | copy-start | bytes 786436
  21.8 5.5 %copy-start.4 = (bf16[256,512]{1,0:T(8,128)(2,1)}, bf16[256,512]{1,0:T(8,128)(2,1)S(1)}, u32[]{:S(2)}) copy-start(bf16[256,512]{1,0:T(8,128)(2,1)S(1)} %collective-permute-done.1.low) | copy-start | bytes 786436
  21.8 53.9 %all-to-all-start.2 = ((bf16[32,8,16,256]{3,2,1,0:T(8,128)(2,1)}), bf16[32,8,16,256]{3,2,1,0:T(8,128)(2,1)S(1)}, u32[]{:S(2)}, u32[]{:S(2)}) async-start(bf16[32,8,16,256]{3,2,1,0:T(8,128)(2,1)} %shard_map.74), calls=%async_computation.2 | async-start | bytes 4194304 | tf_op jit(solution)/shard_map/all_to_all | solution.py:405
  50.9 33.1 %copy-start.8 = (bf16[1,8,64,256]{3,2,1,0:T(8,128)(2,1)S(1)}, bf16[1,8,64,256]{3,2,1,0:T(8,128)(2,1)}, u32[]{:S(2)}) copy-start(bf16[1,8,64,256]{3,2,1,0:T(8,128)(2,1)} %get-tuple-element.34) | copy-start | bytes 786436
  50.9 33.1 %copy-start.7 = (bf16[1,8,64,256]{3,2,1,0:T(8,128)(2,1)S(1)}, bf16[1,8,64,256]{3,2,1,0:T(8,128)(2,1)}, u32[]{:S(2)}) copy-start(bf16[1,8,64,256]{3,2,1,0:T(8,128)(2,1)} %get-tuple-element.35) | copy-start | bytes 786436
  50.9 64.1 %copy-start.6 = (bf16[1,8,64,256]{3,2,1,0:T(8,128)(2,1)S(1)}, bf16[1,8,64,256]{3,2,1,0:T(8,128)(2,1)}, u32[]{:S(2)}) copy-start(bf16[1,8,64,256]{3,2,1,0:T(8,128)(2,1)} %get-tuple-element.36) | copy-start | bytes 786436
  50.9 64.1 %copy-start.5 = (bf16[1,8,64,256]{3,2,1,0:T(8,128)(2,1)S(1)}, bf16[1,8,64,256]{3,2,1,0:T(8,128)(2,1)}, u32[]{:S(2)}) copy-start(bf16[1,8,64,256]{3,2,1,0:T(8,128)(2,1)} %get-tuple-element.37) | copy-start | bytes 786436
  75.7 79.1 %copy-start = (bf16[32,8,16,256]{3,2,1,0:T(8,128)(2,1)}, bf16[32,8,16,256]{3,2,1,0:T(8,128)(2,1)S(1)}, u32[]{:S(2)}) copy-start(bf16[32,8,16,256]{3,2,1,0:T(8,128)(2,1)S(1)} %all-to-all-done.2.tiles) | copy-start | bytes 6291460
  75.7 119.4 %all-to-all-start.1 = ((bf16[32,16,16,256]{3,2,1,0:T(8,128)(2,1)}), bf16[32,16,16,256]{3,2,1,0:T(8,128)(2,1)}, u32[]{:S(2)}, u32[]{:S(2)}) async-start(bf16[32,16,16,256]{3,2,1,0:T(8,128)(2,1)} %shard_map.76), calls=%async_computation.1 | async-start | bytes 8388608 | tf_op jit(solution)/shard_map/all_to_all | solution.py:411
  80.4 34.6 %collective-permute-start.2 = (bf16[8,64,256]{2,1,0:T(8,128)(2,1)}, bf16[8,64,256]{2,1,0:T(8,128)(2,1)S(1)}, u32[]{:S(2)}, u32[]{:S(2)}) collective-permute-start(bf16[8,64,256]{2,1,0:T(8,128)(2,1)} %bitcast.16), channel_id=1, source_target_pairs={{0,1},{1,0},{2,3},{3,2},{4,5},{5,4},{6,7},{7,6},{8,9},{9,8},{10,11... | collective-permute-start | bytes 786440 | tf_op jit(solution)/shard_map/ppermute | solution.py:336
  82.0 33.1 %collective-permute-start.3 = (bf16[8,64,256]{2,1,0:T(8,128)(2,1)}, bf16[8,64,256]{2,1,0:T(8,128)(2,1)S(1)}, u32[]{:S(2)}, u32[]{:S(2)}) collective-permute-start(bf16[8,64,256]{2,1,0:T(8,128)(2,1)} %bitcast.15), channel_id=1, source_target_pairs={{0,2},{1,3},{2,0},{3,1},{4,6},{5,7},{6,4},{7,5},{8,10},{9,11},{10,... | collective-permute-start | bytes 786440 | tf_op jit(solution)/shard_map/ppermute | solution.py:336
  83.4 41.5 %collective-permute-start.4 = (bf16[8,64,256]{2,1,0:T(8,128)(2,1)}, bf16[8,64,256]{2,1,0:T(8,128)(2,1)}, u32[]{:S(2)}, u32[]{:S(2)}) collective-permute-start(bf16[8,64,256]{2,1,0:T(8,128)(2,1)} %bitcast.14), channel_id=1, source_target_pairs={{0,3},{1,2},{2,1},{3,0},{4,7},{5,6},{6,5},{7,4},{8,11},{9,10},{10,... | collective-permute-start | bytes 786440 | tf_op jit(solution)/shard_map/ppermute | solution.py:336
  84.0 41.0 %collective-permute-start.5 = (bf16[8,64,256]{2,1,0:T(8,128)(2,1)S(1)}, bf16[8,64,256]{2,1,0:T(8,128)(2,1)}, u32[]{:S(2)}, u32[]{:S(2)}) collective-permute-start(bf16[8,64,256]{2,1,0:T(8,128)(2,1)S(1)} %bitcast.13), channel_id=1, source_target_pairs={{0,4},{1,5},{2,6},{3,7},{4,0},{5,1},{6,2},{7,3},{8,12},{9,13},{10,... | collective-permute-start | bytes 786440 | tf_op jit(solution)/shard_map/ppermute | solution.py:336
  84.0 50.3 %collective-permute-start.6 = (bf16[8,64,256]{2,1,0:T(8,128)(2,1)S(1)}, bf16[8,64,256]{2,1,0:T(8,128)(2,1)}, u32[]{:S(2)}, u32[]{:S(2)}) collective-permute-start(bf16[8,64,256]{2,1,0:T(8,128)(2,1)S(1)} %bitcast.12), channel_id=1, source_target_pairs={{0,5},{1,4},{2,7},{3,6},{4,1},{5,0},{6,3},{7,2},{8,13},{9,12},{10,... | collective-permute-start | bytes 786440 | tf_op jit(solution)/shard_map/ppermute | solution.py:336
  115.0 32.3 %copy-start.9 = (bf16[8,64,256]{2,1,0:T(8,128)(2,1)}, bf16[8,64,256]{2,1,0:T(8,128)(2,1)S(1)}, u32[]{:S(2)}) copy-start(bf16[8,64,256]{2,1,0:T(8,128)(2,1)S(1)} %collective-permute-done.2.refs_1_) | copy-start | bytes 786436
  115.0 32.3 %collective-permute-start.7 = (bf16[8,64,256]{2,1,0:T(8,128)(2,1)S(1)}, bf16[8,64,256]{2,1,0:T(8,128)(2,1)}, u32[]{:S(2)}, u32[]{:S(2)}) collective-permute-start(bf16[8,64,256]{2,1,0:T(8,128)(2,1)S(1)} %bitcast.11), channel_id=1, source_target_pairs={{0,6},{1,7},{2,4},{3,5},{4,2},{5,3},{6,0},{7,1},{8,14},{9,15},{10,... | collective-permute-start | bytes 786440 | tf_op jit(solution)/shard_map/ppermute | solution.py:336
  115.0 32.3 %collective-permute-start.8 = (bf16[8,64,256]{2,1,0:T(8,128)(2,1)S(1)}, bf16[8,64,256]{2,1,0:T(8,128)(2,1)}, u32[]{:S(2)}, u32[]{:S(2)}) collective-permute-start(bf16[8,64,256]{2,1,0:T(8,128)(2,1)S(1)} %bitcast.10), channel_id=1, source_target_pairs={{0,7},{1,6},{2,5},{3,4},{4,3},{5,2},{6,1},{7,0},{8,15},{9,14},{10,... | collective-permute-start | bytes 786440 | tf_op jit(solution)/shard_map/ppermute | solution.py:336
  154.9 50.2 %collective-permute-start.9 = (bf16[16,2,8,1024]{3,2,1,0:T(8,128)(2,1)}, bf16[16,2,8,1024]{3,2,1,0:T(8,128)(2,1)S(1)}, u32[]{:S(2)}, u32[]{:S(2)}) collective-permute-start(bf16[16,2,8,1024]{3,2,1,0:T(8,128)(2,1)} %get-tuple-element.40), channel_id=1, source_target_pairs={{0,8},{1,9},{2,10},{3,11},{4,12},{5,13},{6,14},{7,15},{8,0},{9,1},... | collective-permute-start | bytes 1572872 | tf_op jit(solution)/shard_map/ppermute | solution.py:328
  154.9 51.4 %collective-permute-start.10 = (bf16[16,2,8,1024]{3,2,1,0:T(8,128)(2,1)}, bf16[16,2,8,1024]{3,2,1,0:T(8,128)(2,1)S(1)}, u32[]{:S(2)}, u32[]{:S(2)}) collective-permute-start(bf16[16,2,8,1024]{3,2,1,0:T(8,128)(2,1)} %get-tuple-element.41), channel_id=1, source_target_pairs={{0,16},{1,17},{2,18},{3,19},{4,20},{5,21},{6,22},{7,23},{8,24},{9,... | collective-permute-start | bytes 1572872 | tf_op jit(solution)/shard_map/ppermute | solution.py:328
  157.6 62.8 %collective-permute-start.11 = (bf16[16,2,8,1024]{3,2,1,0:T(8,128)(2,1)}, bf16[16,2,8,1024]{3,2,1,0:T(8,128)(2,1)S(1)}, u32[]{:S(2)}, u32[]{:S(2)}) collective-permute-start(bf16[16,2,8,1024]{3,2,1,0:T(8,128)(2,1)} %get-tuple-element.42), channel_id=1, source_target_pairs={{0,24},{1,25},{2,26},{3,27},{4,28},{5,29},{6,30},{7,31},{8,16},{9,... | collective-permute-start | bytes 1572872 | tf_op jit(solution)/shard_map/ppermute | solution.py:328
  164.4 39.8 %copy-start.2 = (bf16[16,2,8,1024]{3,2,1,0:T(8,128)(2,1)S(1)}, bf16[16,2,8,1024]{3,2,1,0:T(8,128)(2,1)}, u32[]{:S(2)}) copy-start(bf16[16,2,8,1024]{3,2,1,0:T(8,128)(2,1)} %get-tuple-element.38) | copy-start | bytes 1572868
  (2 other events, 3.4 us)

commit v6 on v5

--- a/solution.py
+++ b/solution.py
@@ -158,6 +158,8 @@
     _, total, rows, depth = normals.shape
     lines, low_x, high_x = halos
     block = 4 if planes % 4 == 0 else 1
+    if planes == 4:
+        block = 2
     steps = planes // block
 
     def block_at(step):
@@ -172,7 +174,7 @@
     whole = pl.BlockSpec((rows, depth), lambda step: (0, 0))
     at_low, at_high = start == 0, start + planes == total
     below, above = max(start - 1, 0), min(start + planes, total - 1)
-    size = planes * rows * depth
+    size = (planes + 6) * rows * depth
     share = depth // (groups * count)
     return pl.pallas_call(
         functools.partial(planes_kernel, start, planes, total, block, sizes),
@@ -212,17 +214,20 @@
 
 
 def y_of(groups, table, order):
-    planes, slab, rows = groups[0][0].shape
-    count = planes * slab
-    lines = [
-        jnp.concatenate([tile[...].reshape(count, rows) for tile in tiles], axis=1) for tiles in groups
-    ]
+    slab, rows = groups[0][0][0].shape[1:]
+    count = order.shape[0]
+    lines = []
+    for tiles in groups:
+        columns = [
+            jnp.concatenate([part[...].reshape(part.shape[0] * slab, rows) for part in tile], axis=0) for tile in tiles
+        ]
+        lines.append(jnp.concatenate(columns, axis=1))
     along = jnp.dot(jnp.concatenate(lines, axis=0), table[...], preferred_element_type=jnp.float32)
     along = along.astype(jnp.bfloat16)
     moved = []
     for at in range(len(groups)):
         part = jnp.dot(order[...], along[at * count:(at + 1) * count], preferred_element_type=jnp.float32)
-        moved.append(part.astype(jnp.bfloat16).reshape(slab, planes, table.shape[1]))
+        moved.append(part.astype(jnp.bfloat16).reshape(slab, count // slab, table.shape[1]))
     return moved
 
 
@@ -243,7 +248,7 @@
             owner = partner(device() % narrow, place)
             ordered[place * rows:(place + 1) * rows, :] = table[pl.ds(pl.multiple_of(owner * rows, rows), rows), :]
 
-    moved = y_of([tiles[at:at + narrow] for at in range(0, near, narrow)], ordered, order)
+    moved = y_of([[[tile] for tile in tiles[at:at + narrow]] for at in range(0, near, narrow)], ordered, order)
     own = device() % near // narrow
     moved = [pick(moved, [own == partner(turn, core) for turn in range(len(moved))]) for core in range(len(moved))]
     for step, out in enumerate(outs):
@@ -254,9 +259,12 @@
                 out[:, core] = part
 
 
-def far_kernel(narrow, tiles, table, order, *rest):
-    out = rest[-1]
-    groups = [[tiles.at[at + place] for place in range(narrow)] for at in range(0, tiles.shape[0], narrow)]
+def far_kernel(narrow, parts, *refs):
+    tiles, (table, order, out) = refs[:parts], refs[parts:]
+    groups = [
+        [[part.at[at + place] for part in tiles] for place in range(narrow)]
+        for at in range(0, tiles[0].shape[0], narrow)
+    ]
     for at, moved in enumerate(y_of(groups, table, order)):
         out[:, at] = moved
 
@@ -288,32 +296,26 @@
     )(*tiles, table, order_of(planes, slab))
 
 
-def along_y_far(tiles, table, so_far, start, total, narrow):
-    count, planes, slab, rows = tiles.shape
+def along_y_far(parts, table, total, narrow):
+    count, _, slab, rows = parts[0].shape
+    planes = sum(part.shape[1] for part in parts)
     wide = count // narrow
     full_y = table.shape[1]
-    group = max(1, 512 // (planes * slab))
-    operands = [tiles, table, order_of(planes, slab)]
-    in_specs = [
-        pl.BlockSpec((group * narrow, planes, slab, rows), lambda at: (at, 0, 0, 0)),
-        pl.BlockSpec(table.shape, lambda at: (0, 0)),
-        pl.BlockSpec((planes * slab, planes * slab), lambda at: (0, 0)),
-    ]
-    aliases = {}
-    if so_far is not None:
-        operands.append(so_far.reshape(slab, wide, total, full_y))
-        in_specs.append(pl.BlockSpec(memory_space=pl.ANY))
-        aliases = {3: 0}
+    group = 2 if wide % 2 == 0 else 1
     return pl.pallas_call(
-        functools.partial(far_kernel, narrow),
+        functools.partial(far_kernel, narrow, len(parts)),
         grid=(wide // group,),
-        in_specs=in_specs,
-        out_specs=pl.BlockSpec((slab, group, planes, full_y), lambda at: (0, at, start // planes, 0)),
+        in_specs=[
+            pl.BlockSpec((group * narrow, part.shape[1], slab, rows), lambda at: (at, 0, 0, 0)) for part in parts
+        ] + [
+            pl.BlockSpec(table.shape, lambda at: (0, 0)),
+            pl.BlockSpec((planes * slab, planes * slab), lambda at: (0, 0)),
+        ],
+        out_specs=pl.BlockSpec((slab, group, planes, full_y), lambda at: (0, at, 0, 0)),
         out_shape=jax.ShapeDtypeStruct((slab, wide, total, full_y), jnp.bfloat16),
-        input_output_aliases=aliases,
         compiler_params=pltpu.CompilerParams(vmem_limit_bytes=VMEM_BYTES),
         cost_estimate=y_cost(planes, slab, wide, full_y),
-    )(*operands).reshape(slab, wide * total, full_y)
+    )(*parts, table, order_of(planes, slab))
 
 
 def after(array, *others):
@@ -399,22 +401,23 @@
     near = cores * narrow
     if slab % 16 == 0 and total % 32 == 0 and wide == cores * far and far & (far - 1) == 0 and near & (near - 1) == 0:
         few = total // 4
-        third, first, second = 0, few, 2 * few
-        pieces = along_z_of(normals, counts, halos, table_z, first, few, 1, wide * narrow)[0]
+        fewer = few // 2
+        third = 3 * few
+        first, second = third - fewer, 0
+        pieces = along_z_of(normals, counts, halos, table_z, first, fewer, 1, wide * narrow)[0]
         pieces = after(pieces, *halos)
+        first_pieces = pieces
         arrived = lax.all_to_all(pieces, ("wide", "narrow"), split_axis=0, concat_axis=0, tiled=True)
         later = after(table_z, pieces)
+        pieces = along_z_of(normals, counts, halos, later, second, first, 1, wide * narrow)[0]
+        pieces = after(pieces, arrived)
+        arrived_later = lax.all_to_all(pieces, ("wide", "narrow"), split_axis=0, concat_axis=0, tiled=True)
+        later = after(table_z, first_pieces)
         tiles = along_z_of(normals, counts, halos, later, third, few, near, 1, (far, near))
-        later = after(table_z, tiles[0])
         tiles = [swap_near(tile[0], step, near) for step, tile in enumerate(tiles)]
-        pieces = along_z_of(normals, counts, halos, later, second, 2 * few, 1, wide * narrow)[0]
-        arrived_later = lax.all_to_all(pieces, ("wide", "narrow"), split_axis=0, concat_axis=0, tiled=True)
         far_pieces = along_y_near(tiles, table_y, far, narrow)
-        arrived = after(arrived, far_pieces[0])
         far_pieces = [swap_far(piece, step, near) for step, piece in enumerate(far_pieces)]
-        spectrum = along_y_far(arrived, table_y, None, first, total, narrow)
-        spectrum = along_y_far(arrived_later, table_y, spectrum, second, total, narrow)
-        spectrum = spectrum.reshape(slab, wide, total, full_y)
+        spectrum = along_y_far([after(arrived_later, far_pieces[0]), arrived], table_y, total, narrow)
         for step, piece in enumerate(far_pieces):
             at = partner(device() // near, step) * cores
             spectrum = lax.dynamic_update_slice(spectrum, piece, (0, at, third, 0))

time: 222 us -> 220 us (level)
  waiting for transfers between devices: 129 us -> 125 us
    ppermute x3, waiting for transfers between devices: 13.7 us -> 7.42 us  [swap_far(): return lax.ppermute(array, ('wide', 'narrow'), pairs)]
    pallas_call x2 -> x1, Pallas kernels: 15.1 us -> 13.8 us  [along_y_far(): pl.pallas_call(functools.partial(far_kernel, narrow, len(parts)), grid=(w...]
  transfers between devices with their start and end apart: 15 -> 15, of which waited for: 9 -> 7; matrix products, arithmetic and copies ran while one was open for 1% -> 1% of each run, Pallas kernels for 25% -> 25%
where the time goes in v6:
time: 220 us; the launch traced here: 218 us
  waiting for transfers between devices  125 us (57%)
  Pallas kernels  56.7 us (26%)
  starting transfers between devices  31.2 us (14%)
  local copies, waits for them, and re-layouts  4.8 us (2%)
    ppermute x7, waiting for transfers between devices, swap_near(): return lax.ppermute(array, ('wide', 'narrow'), pairs)  60.7 us
    all_to_all x2, waiting for transfers between devices, per_device(): lax.all_to_all(pieces, ('wide', 'narrow'), split_axis=0, concat_axis=0, t...  57.2 us
    pallas_call x3, Pallas kernels, along_z_of(): pl.pallas_call(functools.partial(planes_kernel, start, planes, total, blo...  32.2 us
    pallas_call x1, Pallas kernels, along_y_far(): pl.pallas_call(functools.partial(far_kernel, narrow, len(parts)), grid=(w...  13.8 us
    all_to_all x2, starting transfers between devices, per_device(): lax.all_to_all(pieces, ('wide', 'narrow'), split_axis=0, concat_axis=0, t...  9.92 us
    ppermute x7, starting transfers between devices, swap_near(): return lax.ppermute(array, ('wide', 'narrow'), pairs)  8.47 us
    pallas_call x1, Pallas kernels, along_y_near(): pl.pallas_call(functools.partial(near_kernel, near, narrow), grid=(far,),...  7.52 us
    ppermute x3, waiting for transfers between devices, swap_far(): return lax.ppermute(array, ('wide', 'narrow'), pairs)  7.42 us
  transfers between devices with their start and end apart: 15, of which 7 were waited for; matrix products, arithmetic and copies ran while one was open for 1% of the time, Pallas kernels for 25%

profile of v6, /device:TPU:8, one launch (start us, length us, event | category | flops | bytes accessed | tf_op | source)
XLA Modules:
  0.0 218.2 jit_solution(9635464215836985124)
XLA Ops:
  0.0 3.1 %shard_map.64 = (f32[4,32,512]{2,1,0:T(8,128)}, bf16[256,512]{1,0:T(8,128)(2,1)}, bf16[256,512]{1,0:T(8,128)(2,1)}) custom-call(bf16[3,32,256,512]{3,2,1,0:T(8,128)(2,1)} %low.3, bf16[3,32,256,512]{3,2,1,0:T(8,128)(2,1)} %low.3, s32[32,256,512]{2,1,0:T(8,128)} %high_counts.5, s32[32,256,512]{2,1,0:T(8,128)} %high_counts.5, bf16[3,32,256,512]{3,2,1,0:T(8,128)(2,1)} %low.3, ...), custom_call_target="tpu_custom_call" | custom-call | tf_op jit(solution)/shard_map/pallas_call | solution.py:358
  3.1 3.7 %all-to-all-start = ((f32[4,32,512]{2,1,0:T(8,128)}), f32[4,32,512]{2,1,0:T(8,128)S(1)}, u32[]{:S(2)}, u32[]{:S(2)}) async-start(f32[4,32,512]{2,1,0:T(8,128)} %get-tuple-element.24), calls=%async_computation | async-start | bytes 524288 | tf_op jit(solution)/shard_map/all_to_all | solution.py:384
  6.9 1.9 collective-permute-start
  8.8 3.6 %collective-permute-start.1 = (bf16[256,512]{1,0:T(8,128)(2,1)}, bf16[256,512]{1,0:T(8,128)(2,1)S(1)}, u32[]{:S(2)}, u32[]{:S(2)}) collective-permute-start(bf16[256,512]{1,0:T(8,128)(2,1)} %get-tuple-element.26), channel_id=1, source_target_pairs={{4,0},{8,4},{12,8},{16,12},{20,16},{24,20},{28,24},{5,1},{9,5},{13... | collective-permute-start | bytes 786440 | tf_op jit(solution)/shard_map/ppermute | solution.py:386
  13.2 6.2 %shard_map.65 = bf16[32,4,16,256]{3,2,1,0:T(8,128)(2,1)} custom-call(bf16[3,32,256,512]{3,2,1,0:T(8,128)(2,1)} %low.3, s32[32,256,512]{2,1,0:T(8,128)} %high_counts.5, f32[4,32,512]{2,1,0:T(8,128)} %copy-done, bf16[3,32,256,512]{3,2,1,0:T(8,128)(2,1)} %low.3, bf16[3,32,256,512]{3,2,1,0:T(8,128)(2,1)} %low.3, s32[32,256,512]{2,1,0:T(8,128)} %high_counts.5, ...), custom_call_target="tpu_custom_call" | custom-call | flops 1342177280 | bytes 15728640 | tf_op jit(solution)/shard_map/pallas_call | solution.py:179
  19.4 6.5 %all-to-all-start.1 = ((bf16[32,4,16,256]{3,2,1,0:T(8,128)(2,1)}), bf16[32,4,16,256]{3,2,1,0:T(8,128)(2,1)S(1)}, u32[]{:S(2)}, u32[]{:S(2)}) async-start(bf16[32,4,16,256]{3,2,1,0:T(8,128)(2,1)} %shard_map.65), calls=%async_computation.1 | async-start | bytes 2097152 | tf_op jit(solution)/shard_map/all_to_all | solution.py:410
  25.9 17.2 %shard_map.66 = bf16[32,20,16,256]{3,2,1,0:T(8,128)(2,1)} custom-call(bf16[3,32,256,512]{3,2,1,0:T(8,128)(2,1)} %low.3, s32[32,256,512]{2,1,0:T(8,128)} %high_counts.5, f32[4,32,512]{2,1,0:T(8,128)} %copy-done, bf16[256,512]{1,0:T(8,128)(2,1)} %copy-done.4, bf16[3,32,256,512]{3,2,1,0:T(8,128)(2,1)} %low.3, s32[32,256,512]{2,1,0:T(8,128)} %high_counts.5, ...), custom_call_target="tpu_custom_call" | custom-call | flops 3489660928 | bytes 40894464 | tf_op jit(solution)/shard_map/pallas_call | solution.py:179
  43.1 9.3 %all-to-all-done.1.refs_1_ = bf16[32,4,16,256]{3,2,1,0:T(8,128)(2,1)S(1)} async-done(((bf16[32,4,16,256]{3,2,1,0:T(8,128)(2,1)}), bf16[32,4,16,256]{3,2,1,0:T(8,128)(2,1)S(1)}, u32[]{:S(2)}, u32[]{:S(2)}) %all-to-all-start.1) | async-done | bytes 1048608 | tf_op jit(solution)/shard_map/all_to_all | solution.py:410
  52.4 3.4 %all-to-all-start.2 = ((bf16[32,20,16,256]{3,2,1,0:T(8,128)(2,1)}), bf16[32,20,16,256]{3,2,1,0:T(8,128)(2,1)}, u32[]{:S(2)}, u32[]{:S(2)}) async-start(bf16[32,20,16,256]{3,2,1,0:T(8,128)(2,1)} %shard_map.66), calls=%async_computation.2 | async-start | bytes 10485760 | tf_op jit(solution)/shard_map/all_to_all | solution.py:414
  55.8 8.9 %shard_map.67 = (bf16[1,8,64,256]{3,2,1,0:T(8,128)(2,1)}, bf16[1,8,64,256]{3,2,1,0:T(8,128)(2,1)}, bf16[1,8,64,256]{3,2,1,0:T(8,128)(2,1)}, bf16[1,8,64,256]{3,2...) custom-call(bf16[3,32,256,512]{3,2,1,0:T(8,128)(2,1)} %low.3, ...), custom_call_target="tpu_custom_call" | custom-call | flops 1879048192 | bytes 22020096 | tf_op jit(solution)/shard_map/pallas_call | solution.py:179
  64.7 1.5 collective-permute-start.2
  66.2 1.5 collective-permute-start.3
  68.3 1.6 collective-permute-start.6
  69.9 27.0 %collective-permute-done.2.refs_1_ = bf16[8,64,256]{2,1,0:T(8,128)(2,1)S(1)} collective-permute-done((bf16[8,64,256]{2,1,0:T(8,128)(2,1)}, bf16[8,64,256]{2,1,0:T(8,128)(2,1)S(1)}, u32[]{:S(2)}, u32[]{:S(2)}) %collective-permute-start.2) | collective-permute-done | bytes 262176 | tf_op jit(solution)/shard_map/ppermute | solution.py:338
  96.9 3.3 %collective-permute-start.8 = (bf16[8,64,256]{2,1,0:T(8,128)(2,1)}, bf16[8,64,256]{2,1,0:T(8,128)(2,1)S(1)}, u32[]{:S(2)}, u32[]{:S(2)}) collective-permute-start(bf16[8,64,256]{2,1,0:T(8,128)(2,1)} %bitcast.10), channel_id=1, source_target_pairs={{0,7},{1,6},{2,5},{3,4},{4,3},{5,2},{6,1},{7,0},{8,15},{9,14},{10,... | collective-permute-start | bytes 786440 | tf_op jit(solution)/shard_map/ppermute | solution.py:338
  100.2 6.6 %collective-permute-done.4.refs_3_ = bf16[8,64,256]{2,1,0:T(8,128)(2,1)S(1)} collective-permute-done((bf16[8,64,256]{2,1,0:T(8,128)(2,1)}, bf16[8,64,256]{2,1,0:T(8,128)(2,1)S(1)}, u32[]{:S(2)}, u32[]{:S(2)}) %collective-permute-start.4) | collective-permute-done | bytes 262176 | tf_op jit(solution)/shard_map/ppermute | solution.py:338
  106.9 7.4 %collective-permute-done.6.refs_5_ = bf16[8,64,256]{2,1,0:T(8,128)(2,1)S(1)} collective-permute-done((bf16[8,64,256]{2,1,0:T(8,128)(2,1)}, bf16[8,64,256]{2,1,0:T(8,128)(2,1)S(1)}, u32[]{:S(2)}, u32[]{:S(2)}) %collective-permute-start.6) | collective-permute-done | bytes 262176 | tf_op jit(solution)/shard_map/ppermute | solution.py:338
  114.2 19.7 %collective-permute-done.8.refs_7_ = bf16[8,64,256]{2,1,0:T(8,128)(2,1)S(1)} collective-permute-done((bf16[8,64,256]{2,1,0:T(8,128)(2,1)}, bf16[8,64,256]{2,1,0:T(8,128)(2,1)S(1)}, u32[]{:S(2)}, u32[]{:S(2)}) %collective-permute-start.8) | collective-permute-done | bytes 262176 | tf_op jit(solution)/shard_map/ppermute | solution.py:338
  134.7 7.5 %shard_map.68 = (bf16[16,2,8,1024]{3,2,1,0:T(8,128)(2,1)}, bf16[16,2,8,1024]{3,2,1,0:T(8,128)(2,1)}, bf16[16,2,8,1024]{3,2,1,0:T(8,128)(2,1)}, bf16[16,2,8,1024]{3,2,1,0:T(8,128)(2,1)}) custom-call(bf16[8,64,256]{2,1,0:T(8,128)(2,1)} %bitcast.9, bf16[8,64,256]{2,1,0:T(8,128)(2,1)} %copy-done.5, bf16[8,64,256]{2,1,0:T(8,128)(2,1)} %copy-done.6, ...), custom_call_target="tpu_custom_call" | custom-call | flops 2415919104 | bytes 4194304 | tf_op jit(solution)/shard_map/pallas_call | solution.py:284
  142.2 1.4 collective-permute-start.10
  143.6 2.2 collective-permute-start.11
  145.7 47.9 %all-to-all-done.2.refs_0_ = bf16[32,20,16,256]{3,2,1,0:T(8,128)(2,1)} async-done(((bf16[32,20,16,256]{3,2,1,0:T(8,128)(2,1)}), bf16[32,20,16,256]{3,2,1,0:T(8,128)(2,1)}, u32[]{:S(2)}, u32[]{:S(2)}) %all-to-all-start.2) | async-done | bytes 5242912 | tf_op jit(solution)/shard_map/all_to_all | solution.py:414
  193.6 13.8 %shard_map.69 = bf16[16,8,32,1024]{3,2,1,0:T(8,128)(2,1)} custom-call(bf16[32,20,16,256]{3,2,1,0:T(8,128)(2,1)} %all-to-all-done.2.refs_0_, bf16[32,4,16,256]{3,2,1,0:T(8,128)(2,1)} %copy-done.1, bf16[1024,1024]{1,0:T(8,128)(2,1)} %constant.50.clone.refs_8_.refs_2_, bf16[384,384]{1,0:T(8,128)(2,1)} %constant.52.clone.refs_3_), custom_call_target="tpu_custom_call" | custom-call | flops 8858370048 | bytes 12582912 | tf_op jit(solution)/shard_map/pallas_call | solution.py:305
  209.9 7.4 %collective-permute-done.11 = bf16[16,2,8,1024]{3,2,1,0:T(8,128)(2,1)S(1)} collective-permute-done((bf16[16,2,8,1024]{3,2,1,0:T(8,128)(2,1)}, bf16[16,2,8,1024]{3,2,1,0:T(8,128)(2,1)S(1)}, u32[]{:S(2)}, u32[]{:S(2)}) %collective-permute-start.11) | collective-permute-done | bytes 524320 | tf_op jit(solution)/shard_map/ppermute | solution.py:330
  (40 shorter events, 5.4 us)
Async XLA Ops:
  3.1 9.3 %all-to-all-start = ((f32[4,32,512]{2,1,0:T(8,128)}), f32[4,32,512]{2,1,0:T(8,128)S(1)}, u32[]{:S(2)}, u32[]{:S(2)}) async-start(f32[4,32,512]{2,1,0:T(8,128)} %get-tuple-element.24), calls=%async_computation | async-start | bytes 524288 | tf_op jit(solution)/shard_map/all_to_all | solution.py:384
  6.9 12.5 %collective-permute-start = (bf16[256,512]{1,0:T(8,128)(2,1)}, bf16[256,512]{1,0:T(8,128)(2,1)S(1)}, u32[]{:S(2)}, u32[]{:S(2)}) collective-permute-start(bf16[256,512]{1,0:T(8,128)(2,1)} %get-tuple-element.25), channel_id=1, source_target_pairs={{0,4},{4,8},{8,12},{12,16},{16,20},{20,24},{24,28},{1,5},{5,9},{9,... | collective-permute-start | bytes 786440 | tf_op jit(solution)/shard_map/ppermute | solution.py:385
  8.8 10.6 %collective-permute-start.1 = (bf16[256,512]{1,0:T(8,128)(2,1)}, bf16[256,512]{1,0:T(8,128)(2,1)S(1)}, u32[]{:S(2)}, u32[]{:S(2)}) collective-permute-start(bf16[256,512]{1,0:T(8,128)(2,1)} %get-tuple-element.26), channel_id=1, source_target_pairs={{4,0},{8,4},{12,8},{16,12},{20,16},{24,20},{28,24},{5,1},{9,5},{13... | collective-permute-start | bytes 786440 | tf_op jit(solution)/shard_map/ppermute | solution.py:386
  19.3 23.7 %copy-start.3 = (bf16[256,512]{1,0:T(8,128)(2,1)}, bf16[256,512]{1,0:T(8,128)(2,1)S(1)}, u32[]{:S(2)}) copy-start(bf16[256,512]{1,0:T(8,128)(2,1)S(1)} %collective-permute-done.1.high) | copy-start | bytes 786436
  19.4 33.0 %all-to-all-start.1 = ((bf16[32,4,16,256]{3,2,1,0:T(8,128)(2,1)}), bf16[32,4,16,256]{3,2,1,0:T(8,128)(2,1)S(1)}, u32[]{:S(2)}, u32[]{:S(2)}) async-start(bf16[32,4,16,256]{3,2,1,0:T(8,128)(2,1)} %shard_map.65), calls=%async_computation.1 | async-start | bytes 2097152 | tf_op jit(solution)/shard_map/all_to_all | solution.py:410
  52.4 12.3 %copy-start.1 = (bf16[32,4,16,256]{3,2,1,0:T(8,128)(2,1)}, bf16[32,4,16,256]{3,2,1,0:T(8,128)(2,1)S(1)}, u32[]{:S(2)}) copy-start(bf16[32,4,16,256]{3,2,1,0:T(8,128)(2,1)S(1)} %all-to-all-done.1.refs_1_) | copy-start | bytes 3145732
  52.4 141.2 %all-to-all-start.2 = ((bf16[32,20,16,256]{3,2,1,0:T(8,128)(2,1)}), bf16[32,20,16,256]{3,2,1,0:T(8,128)(2,1)}, u32[]{:S(2)}, u32[]{:S(2)}) async-start(bf16[32,20,16,256]{3,2,1,0:T(8,128)(2,1)} %shard_map.66), calls=%async_computation.2 | async-start | bytes 10485760 | tf_op jit(solution)/shard_map/all_to_all | solution.py:414
  64.7 32.1 %collective-permute-start.2 = (bf16[8,64,256]{2,1,0:T(8,128)(2,1)}, bf16[8,64,256]{2,1,0:T(8,128)(2,1)S(1)}, u32[]{:S(2)}, u32[]{:S(2)}) collective-permute-start(bf16[8,64,256]{2,1,0:T(8,128)(2,1)} %bitcast.16), channel_id=1, source_target_pairs={{0,1},{1,0},{2,3},{3,2},{4,5},{5,4},{6,7},{7,6},{8,9},{9,8},{10,11... | collective-permute-start | bytes 786440 | tf_op jit(solution)/shard_map/ppermute | solution.py:338
  66.2 30.6 %collective-permute-start.3 = (bf16[8,64,256]{2,1,0:T(8,128)(2,1)}, bf16[8,64,256]{2,1,0:T(8,128)(2,1)S(1)}, u32[]{:S(2)}, u32[]{:S(2)}) collective-permute-start(bf16[8,64,256]{2,1,0:T(8,128)(2,1)} %bitcast.15), channel_id=1, source_target_pairs={{0,2},{1,3},{2,0},{3,1},{4,6},{5,7},{6,4},{7,5},{8,10},{9,11},{10,... | collective-permute-start | bytes 786440 | tf_op jit(solution)/shard_map/ppermute | solution.py:338
  67.7 39.1 %collective-permute-start.4 = (bf16[8,64,256]{2,1,0:T(8,128)(2,1)}, bf16[8,64,256]{2,1,0:T(8,128)(2,1)S(1)}, u32[]{:S(2)}, u32[]{:S(2)}) collective-permute-start(bf16[8,64,256]{2,1,0:T(8,128)(2,1)} %bitcast.14), channel_id=1, source_target_pairs={{0,3},{1,2},{2,1},{3,0},{4,7},{5,6},{6,5},{7,4},{8,11},{9,10},{10,... | collective-permute-start | bytes 786440 | tf_op jit(solution)/shard_map/ppermute | solution.py:338
  68.3 38.6 %collective-permute-start.5 = (bf16[8,64,256]{2,1,0:T(8,128)(2,1)}, bf16[8,64,256]{2,1,0:T(8,128)(2,1)S(1)}, u32[]{:S(2)}, u32[]{:S(2)}) collective-permute-start(bf16[8,64,256]{2,1,0:T(8,128)(2,1)} %bitcast.13), channel_id=1, source_target_pairs={{0,4},{1,5},{2,6},{3,7},{4,0},{5,1},{6,2},{7,3},{8,12},{9,13},{10,... | collective-permute-start | bytes 786440 | tf_op jit(solution)/shard_map/ppermute | solution.py:338
  68.3 45.9 %collective-permute-start.6 = (bf16[8,64,256]{2,1,0:T(8,128)(2,1)}, bf16[8,64,256]{2,1,0:T(8,128)(2,1)S(1)}, u32[]{:S(2)}, u32[]{:S(2)}) collective-permute-start(bf16[8,64,256]{2,1,0:T(8,128)(2,1)} %bitcast.12), channel_id=1, source_target_pairs={{0,5},{1,4},{2,7},{3,6},{4,1},{5,0},{6,3},{7,2},{8,13},{9,12},{10,... | collective-permute-start | bytes 786440 | tf_op jit(solution)/shard_map/ppermute | solution.py:338
  96.9 37.1 %copy-start.5 = (bf16[8,64,256]{2,1,0:T(8,128)(2,1)}, bf16[8,64,256]{2,1,0:T(8,128)(2,1)S(1)}, u32[]{:S(2)}) copy-start(bf16[8,64,256]{2,1,0:T(8,128)(2,1)S(1)} %collective-permute-done.2.refs_1_) | copy-start | bytes 786436
  96.9 17.4 %collective-permute-start.7 = (bf16[8,64,256]{2,1,0:T(8,128)(2,1)}, bf16[8,64,256]{2,1,0:T(8,128)(2,1)S(1)}, u32[]{:S(2)}, u32[]{:S(2)}) collective-permute-start(bf16[8,64,256]{2,1,0:T(8,128)(2,1)} %bitcast.11), channel_id=1, source_target_pairs={{0,6},{1,7},{2,4},{3,5},{4,2},{5,3},{6,0},{7,1},{8,14},{9,15},{10,... | collective-permute-start | bytes 786440 | tf_op jit(solution)/shard_map/ppermute | solution.py:338
  96.9 37.1 %copy-start.6 = (bf16[8,64,256]{2,1,0:T(8,128)(2,1)}, bf16[8,64,256]{2,1,0:T(8,128)(2,1)S(1)}, u32[]{:S(2)}) copy-start(bf16[8,64,256]{2,1,0:T(8,128)(2,1)S(1)} %collective-permute-done.3.refs_2_) | copy-start | bytes 786436
  96.9 37.1 %collective-permute-start.8 = (bf16[8,64,256]{2,1,0:T(8,128)(2,1)}, bf16[8,64,256]{2,1,0:T(8,128)(2,1)S(1)}, u32[]{:S(2)}, u32[]{:S(2)}) collective-permute-start(bf16[8,64,256]{2,1,0:T(8,128)(2,1)} %bitcast.10), channel_id=1, source_target_pairs={{0,7},{1,6},{2,5},{3,4},{4,3},{5,2},{6,1},{7,0},{8,15},{9,14},{10,... | collective-permute-start | bytes 786440 | tf_op jit(solution)/shard_map/ppermute | solution.py:338
  106.8 27.1 %copy-start.7 = (bf16[8,64,256]{2,1,0:T(8,128)(2,1)}, bf16[8,64,256]{2,1,0:T(8,128)(2,1)S(1)}, u32[]{:S(2)}) copy-start(bf16[8,64,256]{2,1,0:T(8,128)(2,1)S(1)} %collective-permute-done.4.refs_3_) | copy-start | bytes 786436
  106.9 27.1 %copy-start.8 = (bf16[8,64,256]{2,1,0:T(8,128)(2,1)}, bf16[8,64,256]{2,1,0:T(8,128)(2,1)S(1)}, u32[]{:S(2)}) copy-start(bf16[8,64,256]{2,1,0:T(8,128)(2,1)S(1)} %collective-permute-done.5.refs_4_) | copy-start | bytes 786436
  114.2 19.8 %copy-start.9 = (bf16[8,64,256]{2,1,0:T(8,128)(2,1)}, bf16[8,64,256]{2,1,0:T(8,128)(2,1)S(1)}, u32[]{:S(2)}) copy-start(bf16[8,64,256]{2,1,0:T(8,128)(2,1)S(1)} %collective-permute-done.6.refs_5_) | copy-start | bytes 786436
  114.2 19.8 %copy-start.10 = (bf16[8,64,256]{2,1,0:T(8,128)(2,1)}, bf16[8,64,256]{2,1,0:T(8,128)(2,1)S(1)}, u32[]{:S(2)}) copy-start(bf16[8,64,256]{2,1,0:T(8,128)(2,1)S(1)} %collective-permute-done.7.refs_6_) | copy-start | bytes 786436
  142.2 66.0 %collective-permute-start.9 = (bf16[16,2,8,1024]{3,2,1,0:T(8,128)(2,1)}, bf16[16,2,8,1024]{3,2,1,0:T(8,128)(2,1)S(1)}, u32[]{:S(2)}, u32[]{:S(2)}) collective-permute-start(bf16[16,2,8,1024]{3,2,1,0:T(8,128)(2,1)} %get-tuple-element.40), channel_id=1, source_target_pairs={{0,8},{1,9},{2,10},{3,11},{4,12},{5,13},{6,14},{7,15},{8,0},{9,1},... | collective-permute-start | bytes 1572872 | tf_op jit(solution)/shard_map/ppermute | solution.py:330
  142.2 66.9 %collective-permute-start.10 = (bf16[16,2,8,1024]{3,2,1,0:T(8,128)(2,1)}, bf16[16,2,8,1024]{3,2,1,0:T(8,128)(2,1)S(1)}, u32[]{:S(2)}, u32[]{:S(2)}) collective-permute-start(bf16[16,2,8,1024]{3,2,1,0:T(8,128)(2,1)} %get-tuple-element.41), channel_id=1, source_target_pairs={{0,16},{1,17},{2,18},{3,19},{4,20},{5,21},{6,22},{7,23},{8,24},{9,... | collective-permute-start | bytes 1572872 | tf_op jit(solution)/shard_map/ppermute | solution.py:330
  143.6 73.8 %collective-permute-start.11 = (bf16[16,2,8,1024]{3,2,1,0:T(8,128)(2,1)}, bf16[16,2,8,1024]{3,2,1,0:T(8,128)(2,1)S(1)}, u32[]{:S(2)}, u32[]{:S(2)}) collective-permute-start(bf16[16,2,8,1024]{3,2,1,0:T(8,128)(2,1)} %get-tuple-element.42), channel_id=1, source_target_pairs={{0,24},{1,25},{2,26},{3,27},{4,28},{5,29},{6,30},{7,31},{8,16},{9,... | collective-permute-start | bytes 1572872 | tf_op jit(solution)/shard_map/ppermute | solution.py:330
  193.6 13.8 %copy-start.2 = (bf16[16,2,8,1024]{3,2,1,0:T(8,128)(2,1)S(1)}, bf16[16,2,8,1024]{3,2,1,0:T(8,128)(2,1)}, u32[]{:S(2)}) copy-start(bf16[16,2,8,1024]{3,2,1,0:T(8,128)(2,1)} %get-tuple-element.38) | copy-start | bytes 1572868
  (3 other events, 8.0 us)

commit v7 on v6

--- a/solution.py
+++ b/solution.py
@@ -122,10 +122,10 @@
                 done = partial[plane, at, cut] + diff_y(now, plane, tile, at)
                 divergence[plane, at, cut] = done.astype(jnp.bfloat16)
 
-    @pl.when(step < steps)
-    def _():
-        for plane in range(block - 1):
-            transform(plane)
+    def go_on(begun):
+        if begun:
+            for plane in range(block - 1):
+                transform(plane)
         for plane in range(block):
             low_line = lines[below, pl.ds(start + step * block + plane, 1), :]
             high_line = lines[above, pl.ds(start + step * block + plane, 1), :]
@@ -137,7 +137,11 @@
             if number:
                 put_out(strips[number - 1])
         put_out(strips[-1])
-        transform(block - 1)
+        if begun:
+            transform(block - 1)
+
+    pl.when(step == 0)(lambda: go_on(False))
+    pl.when(jnp.logical_and(step > 0, step < steps))(lambda: go_on(True))
 
     @pl.when(step == steps)
     def _():

time: 220 us -> 220 us (level)
  transfers between devices with their start and end apart: 15 -> 15, of which waited for: 7 -> 7; matrix products, arithmetic and copies ran while one was open for 1% -> 1% of each run, Pallas kernels for 25% -> 24%
where the time goes in v7:
time: 220 us; the launch traced here: 218 us
  waiting for transfers between devices  126 us (57%)
  Pallas kernels  56.3 us (26%)
  starting transfers between devices  31.1 us (14%)
  local copies, waits for them, and re-layouts  4.8 us (2%)
    ppermute x7, waiting for transfers between devices, swap_near(): return lax.ppermute(array, ('wide', 'narrow'), pairs)  60.9 us
    all_to_all x2, waiting for transfers between devices, per_device(): lax.all_to_all(pieces, ('wide', 'narrow'), split_axis=0, concat_axis=0, t...  57.2 us
    pallas_call x3, Pallas kernels, along_z_of(): pl.pallas_call(functools.partial(planes_kernel, start, planes, total, blo...  31.8 us
    pallas_call x1, Pallas kernels, along_y_far(): pl.pallas_call(functools.partial(far_kernel, narrow, len(parts)), grid=(w...  13.8 us
    all_to_all x2, starting transfers between devices, per_device(): lax.all_to_all(pieces, ('wide', 'narrow'), split_axis=0, concat_axis=0, t...  10 us
    ppermute x7, starting transfers between devices, swap_near(): return lax.ppermute(array, ('wide', 'narrow'), pairs)  8.32 us
    pallas_call x1, Pallas kernels, along_y_near(): pl.pallas_call(functools.partial(near_kernel, near, narrow), grid=(far,),...  7.52 us
    ppermute x3, waiting for transfers between devices, swap_far(): return lax.ppermute(array, ('wide', 'narrow'), pairs)  7.49 us
  transfers between devices with their start and end apart: 15, of which 7 were waited for; matrix products, arithmetic and copies ran while one was open for 1% of the time, Pallas kernels for 24%

profile of v7, /device:TPU:8, one launch (start us, length us, event | category | flops | bytes accessed | tf_op | source)
XLA Modules:
  0.0 217.9 jit_solution(208080247629060976)
XLA Ops:
  0.0 3.1 %shard_map.64 = (f32[4,32,512]{2,1,0:T(8,128)}, bf16[256,512]{1,0:T(8,128)(2,1)}, bf16[256,512]{1,0:T(8,128)(2,1)}) custom-call(bf16[3,32,256,512]{3,2,1,0:T(8,128)(2,1)} %low.3, bf16[3,32,256,512]{3,2,1,0:T(8,128)(2,1)} %low.3, s32[32,256,512]{2,1,0:T(8,128)} %high_counts.5, s32[32,256,512]{2,1,0:T(8,128)} %high_counts.5, bf16[3,32,256,512]{3,2,1,0:T(8,128)(2,1)} %low.3, ...), custom_call_target="tpu_custom_call" | custom-call | tf_op jit(solution)/shard_map/pallas_call | solution.py:362
  3.1 3.7 %all-to-all-start = ((f32[4,32,512]{2,1,0:T(8,128)}), f32[4,32,512]{2,1,0:T(8,128)S(1)}, u32[]{:S(2)}, u32[]{:S(2)}) async-start(f32[4,32,512]{2,1,0:T(8,128)} %get-tuple-element.24), calls=%async_computation | async-start | bytes 524288 | tf_op jit(solution)/shard_map/all_to_all | solution.py:388
  6.9 1.9 collective-permute-start
  8.8 3.6 %collective-permute-start.1 = (bf16[256,512]{1,0:T(8,128)(2,1)}, bf16[256,512]{1,0:T(8,128)(2,1)S(1)}, u32[]{:S(2)}, u32[]{:S(2)}) collective-permute-start(bf16[256,512]{1,0:T(8,128)(2,1)} %get-tuple-element.26), channel_id=1, source_target_pairs={{4,0},{8,4},{12,8},{16,12},{20,16},{24,20},{28,24},{5,1},{9,5},{13... | collective-permute-start | bytes 786440 | tf_op jit(solution)/shard_map/ppermute | solution.py:390
  13.2 6.0 %shard_map.65 = bf16[32,4,16,256]{3,2,1,0:T(8,128)(2,1)} custom-call(bf16[3,32,256,512]{3,2,1,0:T(8,128)(2,1)} %low.3, s32[32,256,512]{2,1,0:T(8,128)} %high_counts.5, f32[4,32,512]{2,1,0:T(8,128)} %copy-done, bf16[3,32,256,512]{3,2,1,0:T(8,128)(2,1)} %low.3, bf16[3,32,256,512]{3,2,1,0:T(8,128)(2,1)} %low.3, s32[32,256,512]{2,1,0:T(8,128)} %high_counts.5, ...), custom_call_target="tpu_custom_call" | custom-call | flops 1342177280 | bytes 15728640 | tf_op jit(solution)/shard_map/pallas_call | solution.py:183
  19.2 6.5 %all-to-all-start.1 = ((bf16[32,4,16,256]{3,2,1,0:T(8,128)(2,1)}), bf16[32,4,16,256]{3,2,1,0:T(8,128)(2,1)S(1)}, u32[]{:S(2)}, u32[]{:S(2)}) async-start(bf16[32,4,16,256]{3,2,1,0:T(8,128)(2,1)} %shard_map.65), calls=%async_computation.1 | async-start | bytes 2097152 | tf_op jit(solution)/shard_map/all_to_all | solution.py:414
  25.8 17.0 %shard_map.66 = bf16[32,20,16,256]{3,2,1,0:T(8,128)(2,1)} custom-call(bf16[3,32,256,512]{3,2,1,0:T(8,128)(2,1)} %low.3, s32[32,256,512]{2,1,0:T(8,128)} %high_counts.5, f32[4,32,512]{2,1,0:T(8,128)} %copy-done, bf16[256,512]{1,0:T(8,128)(2,1)} %copy-done.4, bf16[3,32,256,512]{3,2,1,0:T(8,128)(2,1)} %low.3, s32[32,256,512]{2,1,0:T(8,128)} %high_counts.5, ...), custom_call_target="tpu_custom_call" | custom-call | flops 3489660928 | bytes 40894464 | tf_op jit(solution)/shard_map/pallas_call | solution.py:183
  42.8 9.5 %all-to-all-done.1.refs_1_ = bf16[32,4,16,256]{3,2,1,0:T(8,128)(2,1)S(1)} async-done(((bf16[32,4,16,256]{3,2,1,0:T(8,128)(2,1)}), bf16[32,4,16,256]{3,2,1,0:T(8,128)(2,1)S(1)}, u32[]{:S(2)}, u32[]{:S(2)}) %all-to-all-start.1) | async-done | bytes 1048608 | tf_op jit(solution)/shard_map/all_to_all | solution.py:414
  52.3 3.5 %all-to-all-start.2 = ((bf16[32,20,16,256]{3,2,1,0:T(8,128)(2,1)}), bf16[32,20,16,256]{3,2,1,0:T(8,128)(2,1)}, u32[]{:S(2)}, u32[]{:S(2)}) async-start(bf16[32,20,16,256]{3,2,1,0:T(8,128)(2,1)} %shard_map.66), calls=%async_computation.2 | async-start | bytes 10485760 | tf_op jit(solution)/shard_map/all_to_all | solution.py:418
  55.8 8.8 %shard_map.67 = (bf16[1,8,64,256]{3,2,1,0:T(8,128)(2,1)}, bf16[1,8,64,256]{3,2,1,0:T(8,128)(2,1)}, bf16[1,8,64,256]{3,2,1,0:T(8,128)(2,1)}, bf16[1,8,64,256]{3,2...) custom-call(bf16[3,32,256,512]{3,2,1,0:T(8,128)(2,1)} %low.3, ...), custom_call_target="tpu_custom_call" | custom-call | flops 1879048192 | bytes 22020096 | tf_op jit(solution)/shard_map/pallas_call | solution.py:183
  64.6 1.4 collective-permute-start.2
  66.0 1.5 collective-permute-start.3
  68.1 1.5 collective-permute-start.6
  69.6 27.0 %collective-permute-done.2.refs_1_ = bf16[8,64,256]{2,1,0:T(8,128)(2,1)S(1)} collective-permute-done((bf16[8,64,256]{2,1,0:T(8,128)(2,1)}, bf16[8,64,256]{2,1,0:T(8,128)(2,1)S(1)}, u32[]{:S(2)}, u32[]{:S(2)}) %collective-permute-start.2) | collective-permute-done | bytes 262176 | tf_op jit(solution)/shard_map/ppermute | solution.py:342
  96.6 3.3 %collective-permute-start.8 = (bf16[8,64,256]{2,1,0:T(8,128)(2,1)}, bf16[8,64,256]{2,1,0:T(8,128)(2,1)S(1)}, u32[]{:S(2)}, u32[]{:S(2)}) collective-permute-start(bf16[8,64,256]{2,1,0:T(8,128)(2,1)} %bitcast.10), channel_id=1, source_target_pairs={{0,7},{1,6},{2,5},{3,4},{4,3},{5,2},{6,1},{7,0},{8,15},{9,14},{10,... | collective-permute-start | bytes 786440 | tf_op jit(solution)/shard_map/ppermute | solution.py:342
  99.9 6.6 %collective-permute-done.4.refs_3_ = bf16[8,64,256]{2,1,0:T(8,128)(2,1)S(1)} collective-permute-done((bf16[8,64,256]{2,1,0:T(8,128)(2,1)}, bf16[8,64,256]{2,1,0:T(8,128)(2,1)S(1)}, u32[]{:S(2)}, u32[]{:S(2)}) %collective-permute-start.4) | collective-permute-done | bytes 262176 | tf_op jit(solution)/shard_map/ppermute | solution.py:342
  106.5 7.5 %collective-permute-done.6.refs_5_ = bf16[8,64,256]{2,1,0:T(8,128)(2,1)S(1)} collective-permute-done((bf16[8,64,256]{2,1,0:T(8,128)(2,1)}, bf16[8,64,256]{2,1,0:T(8,128)(2,1)S(1)}, u32[]{:S(2)}, u32[]{:S(2)}) %collective-permute-start.6) | collective-permute-done | bytes 262176 | tf_op jit(solution)/shard_map/ppermute | solution.py:342
  114.0 19.9 %collective-permute-done.8.refs_7_ = bf16[8,64,256]{2,1,0:T(8,128)(2,1)S(1)} collective-permute-done((bf16[8,64,256]{2,1,0:T(8,128)(2,1)}, bf16[8,64,256]{2,1,0:T(8,128)(2,1)S(1)}, u32[]{:S(2)}, u32[]{:S(2)}) %collective-permute-start.8) | collective-permute-done | bytes 262176 | tf_op jit(solution)/shard_map/ppermute | solution.py:342
  134.6 7.5 %shard_map.68 = (bf16[16,2,8,1024]{3,2,1,0:T(8,128)(2,1)}, bf16[16,2,8,1024]{3,2,1,0:T(8,128)(2,1)}, bf16[16,2,8,1024]{3,2,1,0:T(8,128)(2,1)}, bf16[16,2,8,1024]{3,2,1,0:T(8,128)(2,1)}) custom-call(bf16[8,64,256]{2,1,0:T(8,128)(2,1)} %bitcast.9, bf16[8,64,256]{2,1,0:T(8,128)(2,1)} %copy-done.5, bf16[8,64,256]{2,1,0:T(8,128)(2,1)} %copy-done.6, ...), custom_call_target="tpu_custom_call" | custom-call | flops 2415919104 | bytes 4194304 | tf_op jit(solution)/shard_map/pallas_call | solution.py:288
  142.1 1.9 collective-permute-start.10
  144.0 1.6 collective-permute-start.11
  145.6 47.7 %all-to-all-done.2.refs_0_ = bf16[32,20,16,256]{3,2,1,0:T(8,128)(2,1)} async-done(((bf16[32,20,16,256]{3,2,1,0:T(8,128)(2,1)}), bf16[32,20,16,256]{3,2,1,0:T(8,128)(2,1)}, u32[]{:S(2)}, u32[]{:S(2)}) %all-to-all-start.2) | async-done | bytes 5242912 | tf_op jit(solution)/shard_map/all_to_all | solution.py:418
  193.3 13.8 %shard_map.69 = bf16[16,8,32,1024]{3,2,1,0:T(8,128)(2,1)} custom-call(bf16[32,20,16,256]{3,2,1,0:T(8,128)(2,1)} %all-to-all-done.2.refs_0_, bf16[32,4,16,256]{3,2,1,0:T(8,128)(2,1)} %copy-done.1, bf16[1024,1024]{1,0:T(8,128)(2,1)} %constant.50.clone.refs_8_.refs_2_, bf16[384,384]{1,0:T(8,128)(2,1)} %constant.52.clone.refs_3_), custom_call_target="tpu_custom_call" | custom-call | flops 8858370048 | bytes 12582912 | tf_op jit(solution)/shard_map/pallas_call | solution.py:309
  209.6 7.5 %collective-permute-done.11 = bf16[16,2,8,1024]{3,2,1,0:T(8,128)(2,1)S(1)} collective-permute-done((bf16[16,2,8,1024]{3,2,1,0:T(8,128)(2,1)}, bf16[16,2,8,1024]{3,2,1,0:T(8,128)(2,1)S(1)}, u32[]{:S(2)}, u32[]{:S(2)}) %collective-permute-start.11) | collective-permute-done | bytes 524320 | tf_op jit(solution)/shard_map/ppermute | solution.py:334
  (40 shorter events, 5.5 us)
Async XLA Ops:
  3.1 9.3 %all-to-all-start = ((f32[4,32,512]{2,1,0:T(8,128)}), f32[4,32,512]{2,1,0:T(8,128)S(1)}, u32[]{:S(2)}, u32[]{:S(2)}) async-start(f32[4,32,512]{2,1,0:T(8,128)} %get-tuple-element.24), calls=%async_computation | async-start | bytes 524288 | tf_op jit(solution)/shard_map/all_to_all | solution.py:388
  6.9 12.3 %collective-permute-start = (bf16[256,512]{1,0:T(8,128)(2,1)}, bf16[256,512]{1,0:T(8,128)(2,1)S(1)}, u32[]{:S(2)}, u32[]{:S(2)}) collective-permute-start(bf16[256,512]{1,0:T(8,128)(2,1)} %get-tuple-element.25), channel_id=1, source_target_pairs={{0,4},{4,8},{8,12},{12,16},{16,20},{20,24},{24,28},{1,5},{5,9},{9,... | collective-permute-start | bytes 786440 | tf_op jit(solution)/shard_map/ppermute | solution.py:389
  8.8 10.4 %collective-permute-start.1 = (bf16[256,512]{1,0:T(8,128)(2,1)}, bf16[256,512]{1,0:T(8,128)(2,1)S(1)}, u32[]{:S(2)}, u32[]{:S(2)}) collective-permute-start(bf16[256,512]{1,0:T(8,128)(2,1)} %get-tuple-element.26), channel_id=1, source_target_pairs={{4,0},{8,4},{12,8},{16,12},{20,16},{24,20},{28,24},{5,1},{9,5},{13... | collective-permute-start | bytes 786440 | tf_op jit(solution)/shard_map/ppermute | solution.py:390
  19.2 23.6 %copy-start.3 = (bf16[256,512]{1,0:T(8,128)(2,1)}, bf16[256,512]{1,0:T(8,128)(2,1)S(1)}, u32[]{:S(2)}) copy-start(bf16[256,512]{1,0:T(8,128)(2,1)S(1)} %collective-permute-done.1.high) | copy-start | bytes 786436
  19.2 33.0 %all-to-all-start.1 = ((bf16[32,4,16,256]{3,2,1,0:T(8,128)(2,1)}), bf16[32,4,16,256]{3,2,1,0:T(8,128)(2,1)S(1)}, u32[]{:S(2)}, u32[]{:S(2)}) async-start(bf16[32,4,16,256]{3,2,1,0:T(8,128)(2,1)} %shard_map.65), calls=%async_computation.1 | async-start | bytes 2097152 | tf_op jit(solution)/shard_map/all_to_all | solution.py:414
  52.3 12.3 %copy-start.1 = (bf16[32,4,16,256]{3,2,1,0:T(8,128)(2,1)}, bf16[32,4,16,256]{3,2,1,0:T(8,128)(2,1)S(1)}, u32[]{:S(2)}) copy-start(bf16[32,4,16,256]{3,2,1,0:T(8,128)(2,1)S(1)} %all-to-all-done.1.refs_1_) | copy-start | bytes 3145732
  52.3 141.0 %all-to-all-start.2 = ((bf16[32,20,16,256]{3,2,1,0:T(8,128)(2,1)}), bf16[32,20,16,256]{3,2,1,0:T(8,128)(2,1)}, u32[]{:S(2)}, u32[]{:S(2)}) async-start(bf16[32,20,16,256]{3,2,1,0:T(8,128)(2,1)} %shard_map.66), calls=%async_computation.2 | async-start | bytes 10485760 | tf_op jit(solution)/shard_map/all_to_all | solution.py:418
  64.6 32.0 %collective-permute-start.2 = (bf16[8,64,256]{2,1,0:T(8,128)(2,1)}, bf16[8,64,256]{2,1,0:T(8,128)(2,1)S(1)}, u32[]{:S(2)}, u32[]{:S(2)}) collective-permute-start(bf16[8,64,256]{2,1,0:T(8,128)(2,1)} %bitcast.16), channel_id=1, source_target_pairs={{0,1},{1,0},{2,3},{3,2},{4,5},{5,4},{6,7},{7,6},{8,9},{9,8},{10,11... | collective-permute-start | bytes 786440 | tf_op jit(solution)/shard_map/ppermute | solution.py:342
  66.0 30.6 %collective-permute-start.3 = (bf16[8,64,256]{2,1,0:T(8,128)(2,1)}, bf16[8,64,256]{2,1,0:T(8,128)(2,1)S(1)}, u32[]{:S(2)}, u32[]{:S(2)}) collective-permute-start(bf16[8,64,256]{2,1,0:T(8,128)(2,1)} %bitcast.15), channel_id=1, source_target_pairs={{0,2},{1,3},{2,0},{3,1},{4,6},{5,7},{6,4},{7,5},{8,10},{9,11},{10,... | collective-permute-start | bytes 786440 | tf_op jit(solution)/shard_map/ppermute | solution.py:342
  67.5 39.0 %collective-permute-start.4 = (bf16[8,64,256]{2,1,0:T(8,128)(2,1)}, bf16[8,64,256]{2,1,0:T(8,128)(2,1)S(1)}, u32[]{:S(2)}, u32[]{:S(2)}) collective-permute-start(bf16[8,64,256]{2,1,0:T(8,128)(2,1)} %bitcast.14), channel_id=1, source_target_pairs={{0,3},{1,2},{2,1},{3,0},{4,7},{5,6},{6,5},{7,4},{8,11},{9,10},{10,... | collective-permute-start | bytes 786440 | tf_op jit(solution)/shard_map/ppermute | solution.py:342
  68.1 38.4 %collective-permute-start.5 = (bf16[8,64,256]{2,1,0:T(8,128)(2,1)}, bf16[8,64,256]{2,1,0:T(8,128)(2,1)S(1)}, u32[]{:S(2)}, u32[]{:S(2)}) collective-permute-start(bf16[8,64,256]{2,1,0:T(8,128)(2,1)} %bitcast.13), channel_id=1, source_target_pairs={{0,4},{1,5},{2,6},{3,7},{4,0},{5,1},{6,2},{7,3},{8,12},{9,13},{10,... | collective-permute-start | bytes 786440 | tf_op jit(solution)/shard_map/ppermute | solution.py:342
  68.1 45.9 %collective-permute-start.6 = (bf16[8,64,256]{2,1,0:T(8,128)(2,1)}, bf16[8,64,256]{2,1,0:T(8,128)(2,1)S(1)}, u32[]{:S(2)}, u32[]{:S(2)}) collective-permute-start(bf16[8,64,256]{2,1,0:T(8,128)(2,1)} %bitcast.12), channel_id=1, source_target_pairs={{0,5},{1,4},{2,7},{3,6},{4,1},{5,0},{6,3},{7,2},{8,13},{9,12},{10,... | collective-permute-start | bytes 786440 | tf_op jit(solution)/shard_map/ppermute | solution.py:342
  96.6 37.2 %copy-start.5 = (bf16[8,64,256]{2,1,0:T(8,128)(2,1)}, bf16[8,64,256]{2,1,0:T(8,128)(2,1)S(1)}, u32[]{:S(2)}) copy-start(bf16[8,64,256]{2,1,0:T(8,128)(2,1)S(1)} %collective-permute-done.2.refs_1_) | copy-start | bytes 786436
  96.6 17.4 %collective-permute-start.7 = (bf16[8,64,256]{2,1,0:T(8,128)(2,1)}, bf16[8,64,256]{2,1,0:T(8,128)(2,1)S(1)}, u32[]{:S(2)}, u32[]{:S(2)}) collective-permute-start(bf16[8,64,256]{2,1,0:T(8,128)(2,1)} %bitcast.11), channel_id=1, source_target_pairs={{0,6},{1,7},{2,4},{3,5},{4,2},{5,3},{6,0},{7,1},{8,14},{9,15},{10,... | collective-permute-start | bytes 786440 | tf_op jit(solution)/shard_map/ppermute | solution.py:342
  96.6 37.2 %copy-start.6 = (bf16[8,64,256]{2,1,0:T(8,128)(2,1)}, bf16[8,64,256]{2,1,0:T(8,128)(2,1)S(1)}, u32[]{:S(2)}) copy-start(bf16[8,64,256]{2,1,0:T(8,128)(2,1)S(1)} %collective-permute-done.3.refs_2_) | copy-start | bytes 786436
  96.6 37.2 %collective-permute-start.8 = (bf16[8,64,256]{2,1,0:T(8,128)(2,1)}, bf16[8,64,256]{2,1,0:T(8,128)(2,1)S(1)}, u32[]{:S(2)}, u32[]{:S(2)}) collective-permute-start(bf16[8,64,256]{2,1,0:T(8,128)(2,1)} %bitcast.10), channel_id=1, source_target_pairs={{0,7},{1,6},{2,5},{3,4},{4,3},{5,2},{6,1},{7,0},{8,15},{9,14},{10,... | collective-permute-start | bytes 786440 | tf_op jit(solution)/shard_map/ppermute | solution.py:342
  106.5 27.3 %copy-start.7 = (bf16[8,64,256]{2,1,0:T(8,128)(2,1)}, bf16[8,64,256]{2,1,0:T(8,128)(2,1)S(1)}, u32[]{:S(2)}) copy-start(bf16[8,64,256]{2,1,0:T(8,128)(2,1)S(1)} %collective-permute-done.4.refs_3_) | copy-start | bytes 786436
  106.5 27.3 %copy-start.8 = (bf16[8,64,256]{2,1,0:T(8,128)(2,1)}, bf16[8,64,256]{2,1,0:T(8,128)(2,1)S(1)}, u32[]{:S(2)}) copy-start(bf16[8,64,256]{2,1,0:T(8,128)(2,1)S(1)} %collective-permute-done.5.refs_4_) | copy-start | bytes 786436
  114.0 19.9 %copy-start.9 = (bf16[8,64,256]{2,1,0:T(8,128)(2,1)}, bf16[8,64,256]{2,1,0:T(8,128)(2,1)S(1)}, u32[]{:S(2)}) copy-start(bf16[8,64,256]{2,1,0:T(8,128)(2,1)S(1)} %collective-permute-done.6.refs_5_) | copy-start | bytes 786436
  114.0 19.9 %copy-start.10 = (bf16[8,64,256]{2,1,0:T(8,128)(2,1)}, bf16[8,64,256]{2,1,0:T(8,128)(2,1)S(1)}, u32[]{:S(2)}) copy-start(bf16[8,64,256]{2,1,0:T(8,128)(2,1)S(1)} %collective-permute-done.7.refs_6_) | copy-start | bytes 786436
  142.1 65.9 %collective-permute-start.9 = (bf16[16,2,8,1024]{3,2,1,0:T(8,128)(2,1)}, bf16[16,2,8,1024]{3,2,1,0:T(8,128)(2,1)S(1)}, u32[]{:S(2)}, u32[]{:S(2)}) collective-permute-start(bf16[16,2,8,1024]{3,2,1,0:T(8,128)(2,1)} %get-tuple-element.40), channel_id=1, source_target_pairs={{0,8},{1,9},{2,10},{3,11},{4,12},{5,13},{6,14},{7,15},{8,0},{9,1},... | collective-permute-start | bytes 1572872 | tf_op jit(solution)/shard_map/ppermute | solution.py:334
  142.1 66.7 %collective-permute-start.10 = (bf16[16,2,8,1024]{3,2,1,0:T(8,128)(2,1)}, bf16[16,2,8,1024]{3,2,1,0:T(8,128)(2,1)S(1)}, u32[]{:S(2)}, u32[]{:S(2)}) collective-permute-start(bf16[16,2,8,1024]{3,2,1,0:T(8,128)(2,1)} %get-tuple-element.41), channel_id=1, source_target_pairs={{0,16},{1,17},{2,18},{3,19},{4,20},{5,21},{6,22},{7,23},{8,24},{9,... | collective-permute-start | bytes 1572872 | tf_op jit(solution)/shard_map/ppermute | solution.py:334
  144.0 73.1 %collective-permute-start.11 = (bf16[16,2,8,1024]{3,2,1,0:T(8,128)(2,1)}, bf16[16,2,8,1024]{3,2,1,0:T(8,128)(2,1)S(1)}, u32[]{:S(2)}, u32[]{:S(2)}) collective-permute-start(bf16[16,2,8,1024]{3,2,1,0:T(8,128)(2,1)} %get-tuple-element.42), channel_id=1, source_target_pairs={{0,24},{1,25},{2,26},{3,27},{4,28},{5,29},{6,30},{7,31},{8,16},{9,... | collective-permute-start | bytes 1572872 | tf_op jit(solution)/shard_map/ppermute | solution.py:334
  193.3 13.8 %copy-start.2 = (bf16[16,2,8,1024]{3,2,1,0:T(8,128)(2,1)S(1)}, bf16[16,2,8,1024]{3,2,1,0:T(8,128)(2,1)}, u32[]{:S(2)}) copy-start(bf16[16,2,8,1024]{3,2,1,0:T(8,128)(2,1)} %get-tuple-element.38) | copy-start | bytes 1572868
  (3 other events, 8.0 us)
